TPU v7x, 256 devices: a whole 4x4x8 slice. The times are simulated.
256 devices in a mesh: inst: 32 (over x, z_lo, core), tp: 8 (over y, z_hi).
Axes of the slice: x: 4, y: 4, z: 8 (z_hi: 2, z_lo: 4; z = z_hi * 4 + z_lo), core: 2. Of those that a mesh axis runs over, the one named last changes fastest.
Arguments:
- queries: bfloat16 [4, 2048, 64, 128], P(None, 'inst', 'tp'), may hold values from -80 to 80
- new_keys: bfloat16 [4, 2048, 8, 128], P(None, 'inst', 'tp'), may hold values from -5 to 5
- new_values: bfloat16 [4, 2048, 8, 128], P(None, 'inst', 'tp'), may hold values from -6 to 6
- pool_keys: bfloat16 [6144, 8, 16, 128], P('inst', 'tp'), may hold values from -6 to 6
- pool_values: bfloat16 [6144, 8, 16, 128], P('inst', 'tp'), may hold values from -6 to 6
- prompt_keys: bfloat16 [6144, 8, 16, 128], P('inst', 'tp'), may hold values from -6 to 6
- prompt_values: bfloat16 [6144, 8, 16, 128], P('inst', 'tp'), may hold values from -6 to 6
- moved_keys: bfloat16 [3072, 8, 16, 128], P('inst', 'tp'), may hold values from -6 to 6
- moved_values: bfloat16 [3072, 8, 16, 128], P('inst', 'tp'), may hold values from -6 to 6
- prompt_dest: int32 [6144], P('inst'), may hold values from 0 to 31, as said below
- moved_dest: int32 [3072], P('inst'), may hold values from 0 to 31, as said below
- block_table: int32 [2048, 48], P('inst'), may hold values from 0 to 767, as said below
- context_len: int32 [2048], P('inst'), may hold values from 1 to 768, as said below
- out_weight: bfloat16 [8192, 4096], P('tp'), may hold values from -0.25 to 0.25
Outputs:
- mixed: bfloat16 [4, 2048, 4096], P(None, 'inst', 'tp')
Inputs may be any that keep to these rules, and one draw needn't show every extreme that they name: `prompt_dest`: entry s * 192 + j names the instance that receives prompt page j of instance s. No instance receives more than 12 pages from one source; in every draw every source sends exactly 12 pages to some instance. `moved_dest`: entry s * 96 + j names the new owner of migrating page j of instance s. No instance receives more than 6 pages from one source; in every draw every source sends exactly 6 pages to some instance. `block_table`: local page ids of the instance that holds the row. Only filled arrival slots are named; over the rows of an instance each page is named at most once in the first ceil(context_len / 16) entries of a row; later entries hold 0 and are not read. `context_len`: some sequence of every instance has exactly 768 cached tokens.
All inputs are finite; a program needn't handle non-finite values.
Results may differ from a plain program's by a relative error of at most 0.0057.
Values may be sent and summed in bfloat16 or wider, within the bound.
No kernel may reach another device: no remote copies, remote signals or barrier semaphores. Data moves between devices by JAX's collectives and lax.ppermute only.
A program may use at most 256 MiB of HBM per device.

v0:
```python
import jax
import jax.numpy as jnp
from jax import lax
from jax.sharding import PartitionSpec as P


def arrival_rank(destination, count):
    onehot = (destination[:, None] == jnp.arange(count, dtype=jnp.int32)[None, :]).astype(jnp.int32)
    before = jnp.cumsum(onehot, axis=0) - onehot
    return jnp.sum(before * onehot, axis=1)


def pack_pages(pages, destination, count, capacity):
    target = destination * capacity + arrival_rank(destination, count)
    empty = jnp.zeros((count * capacity,) + pages.shape[1:], pages.dtype)
    return empty.at[target].set(pages)


def attention_weights(query_block, keys_block, fresh_keys, lengths):
    steps_count = query_block.shape[0]
    scale = query_block.shape[-1] ** (-0.5)
    cached = (
        jnp.einsum(
            "srkgd,rpkod->srkgpo", query_block, keys_block, preferred_element_type=jnp.float32
        )
        * scale
    )
    cached = cached.reshape(cached.shape[:4] + (-1,))
    position = jnp.arange(cached.shape[-1], dtype=jnp.int32)
    visible = position[None, :] < lengths[:, None]
    cached = jnp.where(visible[None, :, None, None, :], cached, -jnp.inf)
    recent = (
        jnp.einsum("srkgd,urkd->srkgu", query_block, fresh_keys, preferred_element_type=jnp.float32)
        * scale
    )
    causal = (
        jnp.arange(steps_count, dtype=jnp.int32)[None, :]
        <= jnp.arange(steps_count, dtype=jnp.int32)[:, None]
    )
    recent = jnp.where(causal[:, None, None, None, :], recent, -jnp.inf)
    largest = jnp.maximum(jnp.max(cached, axis=-1), jnp.max(recent, axis=-1))
    cached_exp = jnp.exp(cached - largest[..., None])
    recent_exp = jnp.exp(recent - largest[..., None])
    total = jnp.sum(cached_exp, axis=-1) + jnp.sum(recent_exp, axis=-1)
    cached_w = (cached_exp / total[..., None]).astype(jnp.bfloat16)
    recent_w = (recent_exp / total[..., None]).astype(jnp.bfloat16)
    return (cached_w, recent_w)


def per_device(
    queries,
    new_keys,
    new_values,
    pool_keys,
    pool_values,
    prompt_keys,
    prompt_values,
    moved_keys,
    moved_values,
    prompt_dest,
    moved_dest,
    block_table,
    context_len,
    out_weight,
):
    instances = lax.axis_size("inst")
    prompt_cap = 2 * prompt_keys.shape[0] // instances
    moved_cap = 2 * moved_keys.shape[0] // instances
    prompt_send_k = pack_pages(prompt_keys, prompt_dest, instances, prompt_cap)
    prompt_send_v = pack_pages(prompt_values, prompt_dest, instances, prompt_cap)
    moved_send_k = pack_pages(moved_keys, moved_dest, instances, moved_cap)
    moved_send_v = pack_pages(moved_values, moved_dest, instances, moved_cap)
    got_prompt = (
        lax.all_to_all(prompt_send_k, "inst", split_axis=0, concat_axis=0, tiled=True),
        lax.all_to_all(prompt_send_v, "inst", split_axis=0, concat_axis=0, tiled=True),
    )
    got_moved = (
        lax.all_to_all(moved_send_k, "inst", split_axis=0, concat_axis=0, tiled=True),
        lax.all_to_all(moved_send_v, "inst", split_axis=0, concat_axis=0, tiled=True),
    )
    arrived_keys = jnp.concatenate([got_prompt[0], got_moved[0]], axis=0)
    arrived_values = jnp.concatenate([got_prompt[1], got_moved[1]], axis=0)
    store_keys = jnp.concatenate([pool_keys, arrived_keys], axis=0)
    store_values = jnp.concatenate([pool_values, arrived_values], axis=0)
    keys_block = jnp.take(store_keys, block_table, axis=0)
    values_block = jnp.take(store_values, block_table, axis=0)
    steps_count, row_count, local_heads, head_size = queries.shape
    local_kv = new_keys.shape[2]
    groups = local_heads // local_kv
    query_block = queries.reshape(steps_count, row_count, local_kv, groups, head_size)
    cached_w, recent_w = attention_weights(query_block, keys_block, new_keys, context_len)
    cached_w = cached_w.reshape(cached_w.shape[:4] + keys_block.shape[1:2] + keys_block.shape[3:4])
    heads = jnp.einsum(
        "srkgpo,rpkod->srkgd", cached_w, values_block, preferred_element_type=jnp.float32
    )
    heads = heads + jnp.einsum(
        "srkgu,urkd->srkgd", recent_w, new_values, preferred_element_type=jnp.float32
    )
    heads_out = heads.astype(jnp.bfloat16).reshape(steps_count * row_count, local_heads * head_size)
    partial_terms = jnp.dot(heads_out, out_weight, preferred_element_type=jnp.float32)
    reduced = lax.psum_scatter(partial_terms, "tp", scatter_dimension=1, tiled=True)
    return reduced.astype(jnp.bfloat16).reshape(steps_count, row_count, -1)


def solution(mesh):
    in_specs = (
        P(None, "inst", "tp", None),
        P(None, "inst", "tp", None),
        P(None, "inst", "tp", None),
        P("inst", "tp", None, None),
        P("inst", "tp", None, None),
        P("inst", "tp", None, None),
        P("inst", "tp", None, None),
        P("inst", "tp", None, None),
        P("inst", "tp", None, None),
        P("inst"),
        P("inst"),
        P("inst", None),
        P("inst"),
        P("tp", None),
    )
    out_specs = P(None, "inst", "tp")
    return jax.shard_map(
        per_device, mesh=mesh, in_specs=in_specs, out_specs=out_specs, check_vma=False
    )
```

profile of v0, /device:TPU:8, one launch (start us, length us, event | category | flops | bytes accessed | tf_op | source)
XLA Modules:
  0.0 429.6 jit_solution(3961201721038842166)
XLA Ops:
  10.0 10.4 %scatter_fusion.3 = bf16[192,16,128]{2,1,0:T(8,128)(2,1)} fusion(bf16[192,16,128]{2,1,0:T(8,128)(2,1)} %broadcast.128.clone, s32[96]{0:T(128)S(1)} %compare_select_fusion.2, bf16[96,16,128]{2,1,0:T(8,128)(2,1)} %bitcast.131), kind=kCustom, calls=%fused_computation.5 | custom fusion | bytes 1180032 | tf_op jit(solution)/shard_map/scatter | solution.py:16
  20.4 8.7 %all-to-all-start.3 = ((bf16[192,1,16,128]{3,2,1,0:T(8,128)(2,1)}), bf16[192,1,16,128]{3,2,1,0:T(8,128)(2,1)S(1)}, u32[]{:S(2)}, u32[]{:S(2)}) async-start(bf16[192,1,16,128]{3,2,1,0:T(8,128)(2,1)} %bitcast.15), calls=%async_computation.3 | async-start | bytes 1572864 | tf_op jit(solution)/shard_map/all_to_all | solution.py:78
  32.1 1.4 broadcast.126.clone
  33.5 20.2 %scatter_fusion.2 = bf16[384,16,128]{2,1,0:T(8,128)(2,1)} fusion(bf16[384,16,128]{2,1,0:T(8,128)(2,1)} %broadcast.126.clone, s32[192]{0:T(256)S(1)} %compare_select_fusion.1, bf16[192,16,128]{2,1,0:T(8,128)(2,1)} %bitcast.129), kind=kCustom, calls=%fused_computation.4 | custom fusion | bytes 2360064 | tf_op jit(solution)/shard_map/scatter | solution.py:16
  53.7 7.7 %all-to-all-start.2 = ((bf16[384,1,16,128]{3,2,1,0:T(8,128)(2,1)}), bf16[384,1,16,128]{3,2,1,0:T(8,128)(2,1)S(1)}, u32[]{:S(2)}, u32[]{:S(2)}) async-start(bf16[384,1,16,128]{3,2,1,0:T(8,128)(2,1)} %bitcast.12), calls=%async_computation.2 | async-start | bytes 3145728 | tf_op jit(solution)/shard_map/all_to_all | solution.py:74
  63.7 1.4 broadcast.126.clone.1
  65.1 20.2 %scatter_fusion = bf16[384,16,128]{2,1,0:T(8,128)(2,1)} fusion(bf16[384,16,128]{2,1,0:T(8,128)(2,1)} %broadcast.126.clone.1, s32[192]{0:T(256)S(1)} %compare_select_fusion.1, bf16[192,16,128]{2,1,0:T(8,128)(2,1)} %bitcast.130), kind=kCustom, calls=%fused_computation.2 | custom fusion | bytes 2360064 | tf_op jit(solution)/shard_map/scatter | solution.py:16
  85.3 1.0 broadcast.128.clone.1
  86.3 9.4 %scatter_fusion.1 = bf16[192,16,128]{2,1,0:T(8,128)(2,1)} fusion(bf16[192,16,128]{2,1,0:T(8,128)(2,1)} %broadcast.128.clone.1, s32[96]{0:T(128)S(1)} %compare_select_fusion.2, bf16[96,16,128]{2,1,0:T(8,128)(2,1)S(1)} %bitcast.132), kind=kCustom, calls=%fused_computation.3 | custom fusion | bytes 1180032 | tf_op jit(solution)/shard_map/scatter | solution.py:16
  96.0 4.1 fusion.41
  100.6 7.4 %all-to-all-start.1 = ((bf16[192,1,16,128]{3,2,1,0:T(8,128)(2,1)}), bf16[192,1,16,128]{3,2,1,0:T(8,128)(2,1)}, u32[]{:S(2)}, u32[]{:S(2)}) async-start(bf16[192,1,16,128]{3,2,1,0:T(8,128)(2,1)} %bitcast.4), calls=%async_computation.1 | async-start | bytes 1572864 | tf_op jit(solution)/shard_map/all_to_all | solution.py:79
  108.0 2.9 maximum_bitcast_fusion.1
  110.9 25.8 %gather_fusion.1 = bf16[3072,16,128]{2,1,0:T(8,128)(2,1)} fusion(bf16[768,16,128]{2,1,0:T(8,128)(2,1)} %maximum_bitcast_fusion.1, s32[3072]{0:T(1024)S(1)} %broadcast_clamp_fusion), kind=kCustom, calls=%fused_computation.1.clone | custom fusion | bytes 25178112 | tf_op jit(solution)/shard_map/jit(_take)/gather | solution.py:85
  136.7 40.7 %bitcast_reduce_fusion = (f32[4,64,8]{2,0,1:T(4,128)S(1)}, f32[64,48,16,4,8]{2,4,3,1,0:T(8,128)}) fusion(pred[64,48,16]{2,1,0:T(8,128)(4,1)S(1)} %broadcast_compare_fusion, bf16[64,48,1,16,128]{4,3,1,0,2:T(8,128)(2,1)} %bitcast.127, pred[64,48]{1,0:T(8,128)(4,1)S(1)} %copy-done.7, bf16[4,64,8,128]{3,2,1,0:T(8,128)(2,1)S(1)} %copy-done), kind=kOutput, calls=%fused_computation.7 | convolution fusion | flops 413661184 | bytes 19459072 | tf_op jit(solution)/shard_map/srkgd,rpkod->srkgpo/dot_general | solution.py:23
  177.5 1.1 fusion.29
  178.6 7.7 %all-to-all-start = ((bf16[384,1,16,128]{3,2,1,0:T(8,128)(2,1)}), bf16[384,1,16,128]{3,2,1,0:T(8,128)(2,1)}, u32[]{:S(2)}, u32[]{:S(2)}) async-start(bf16[384,1,16,128]{3,2,1,0:T(8,128)(2,1)} %bitcast.2), calls=%async_computation | async-start | bytes 3145728 | tf_op jit(solution)/shard_map/all_to_all | solution.py:75
  186.6 23.8 %fusion.1 = f32[4,64,8]{2,0,1:T(4,128)} fusion(f32[64,48,16,4,8]{2,4,3,1,0:T(8,128)} %get-tuple-element.7, f32[4,64,8]{2,0,1:T(4,128)S(1)} %max.9, pred[64,48,16]{2,1,0:T(8,128)(4,1)S(1)} %broadcast_compare_fusion), kind=kLoop, calls=%fused_computation.11 | loop fusion | flops 6289408 | bytes 6356992 | tf_op jit(solution)/shard_map/reduce_sum | solution.py:44
  210.4 15.2 %all-to-all-done = bf16[384,1,16,128]{3,2,1,0:T(8,128)(2,1)} async-done(((bf16[384,1,16,128]{3,2,1,0:T(8,128)(2,1)}), bf16[384,1,16,128]{3,2,1,0:T(8,128)(2,1)}, u32[]{:S(2)}, u32[]{:S(2)}) %all-to-all-start) | async-done | bytes 1572896 | tf_op jit(solution)/shard_map/all_to_all | solution.py:75
  225.6 2.1 maximum_bitcast_fusion
  227.7 23.9 %gather_fusion = bf16[3072,16,128]{2,1,0:T(8,128)(2,1)} fusion(bf16[768,16,128]{2,1,0:T(8,128)(2,1)S(1)} %maximum_bitcast_fusion, s32[3072]{0:T(1024)S(1)} %broadcast_clamp_fusion), kind=kCustom, calls=%fused_computation.clone | custom fusion | bytes 25178112 | tf_op jit(solution)/shard_map/jit(_take)/gather | solution.py:86
  252.7 34.6 %fusion.15 = f32[64,128,4,8]{1,3,2,0:T(8,128)S(1)} fusion(f32[4,64,8]{2,0,1:T(4,128)S(1)} %add.43, f32[4,64,8]{2,0,1:T(4,128)} %copy-done.2, f32[64,48,16,4,8]{2,4,3,1,0:T(8,128)} %get-tuple-element.7, pred[64,48,16]{2,1,0:T(8,128)(4,1)S(1)} %broadcast_compare_fusion, bf16[64,48,1,16,128]{4,3,1,0,2:T(8,128)(2,1)} %bitcast.126, pred[64,48]{1,0:T(8,128)(4,1)} %copy.39), kind=kOutput, calls=%fused_computation.28 | convolution fusion | flops 416808960 | bytes 19991552 | tf_op jit(solution)/shard_map/srkgpo,rpkod->srkgd/dot_general | solution.py:93
  287.8 7.6 %fusion.24 = f32[256,4096]{1,0:T(8,128)} fusion(bf16[1024,4096]{1,0:T(8,128)(2,1)} %param.29, bf16[32,8,8,128]{3,2,1,0:T(8,128)(2,1)S(1)} %bitcast.128), kind=kOutput, calls=%fused_computation.35 | convolution fusion | flops 2147483648 | bytes 13107200 | tf_op jit(solution)/shard_map/dot_general | solution.py:100
  295.5 125.5 %reduce-scatter.2.cloned.1.call-done = f32[256,512]{1,0:T(8,128)} async-done(((f32[256,4096]{1,0:T(8,128)}), f32[256,512]{1,0:T(8,128)}) %reduce-scatter.2.cloned.1.call-update) | async-done | bytes 524304 | tf_op jit(solution)/shard_map/reduce_scatter | solution.py:101
  421.0 1.8 convert_element_type.37
  (52 shorter events, 11.4 us)
Async XLA Ops:
  6.5 89.5 %copy-start = (bf16[4,64,8,128]{3,2,1,0:T(8,128)(2,1)S(1)}, bf16[4,64,8,128]{3,2,1,0:T(8,128)(2,1)}, u32[]{:S(2)}) copy-start(bf16[4,64,8,128]{3,2,1,0:T(8,128)(2,1)} %param.16) | copy-start | bytes 1572868
  6.5 79.8 %copy-start.6 = (bf16[96,1,16,128]{3,2,1,0:T(8,128)(2,1)S(1)}, bf16[96,1,16,128]{3,2,1,0:T(8,128)(2,1)}, u32[]{:S(2)}) copy-start(bf16[96,1,16,128]{3,2,1,0:T(8,128)(2,1)} %param.24) | copy-start | bytes 1179652
  6.5 89.2 %copy-start.8 = (s32[64]{0:T(128)S(1)}, s32[64]{0:T(128)}, u32[]{:S(2)}) copy-start(s32[64]{0:T(128)} %param.28) | copy-start | bytes 772
  20.4 33.3 %all-to-all-start.3 = ((bf16[192,1,16,128]{3,2,1,0:T(8,128)(2,1)}), bf16[192,1,16,128]{3,2,1,0:T(8,128)(2,1)S(1)}, u32[]{:S(2)}, u32[]{:S(2)}) async-start(bf16[192,1,16,128]{3,2,1,0:T(8,128)(2,1)} %bitcast.15), calls=%async_computation.3 | async-start | bytes 1572864 | tf_op jit(solution)/shard_map/all_to_all | solution.py:78
  53.7 46.9 %all-to-all-start.2 = ((bf16[384,1,16,128]{3,2,1,0:T(8,128)(2,1)}), bf16[384,1,16,128]{3,2,1,0:T(8,128)(2,1)S(1)}, u32[]{:S(2)}, u32[]{:S(2)}) async-start(bf16[384,1,16,128]{3,2,1,0:T(8,128)(2,1)} %bitcast.12), calls=%async_computation.2 | async-start | bytes 3145728 | tf_op jit(solution)/shard_map/all_to_all | solution.py:74
  100.6 78.1 %all-to-all-start.1 = ((bf16[192,1,16,128]{3,2,1,0:T(8,128)(2,1)}), bf16[192,1,16,128]{3,2,1,0:T(8,128)(2,1)}, u32[]{:S(2)}, u32[]{:S(2)}) async-start(bf16[192,1,16,128]{3,2,1,0:T(8,128)(2,1)} %bitcast.4), calls=%async_computation.1 | async-start | bytes 1572864 | tf_op jit(solution)/shard_map/all_to_all | solution.py:79
  110.9 25.8 %copy-start.7 = (pred[64,48]{1,0:T(8,128)(4,1)S(1)}, pred[64,48]{1,0:T(8,128)(4,1)}, u32[]{:S(2)}) copy-start(pred[64,48]{1,0:T(8,128)(4,1)} %copy.39) | copy-start | bytes 9220
  136.7 40.8 %copy-start.4 = (f32[4,64,1,8,4]{3,4,0,1,2:T(4,128)S(1)}, f32[4,64,1,8,4]{3,4,0,1,2:T(4,128)}, u32[]{:S(2)}) copy-start(f32[4,64,1,8,4]{3,4,0,1,2:T(4,128)} %get-tuple-element.9) | copy-start | bytes 98308
  177.5 32.9 %copy-start.2 = (f32[4,64,8]{2,0,1:T(4,128)}, f32[4,64,8]{2,0,1:T(4,128)S(1)}, u32[]{:S(2)}) copy-start(f32[4,64,8]{2,0,1:T(4,128)S(1)} %max.9) | copy-start | bytes 24580
  178.6 46.9 %all-to-all-start = ((bf16[384,1,16,128]{3,2,1,0:T(8,128)(2,1)}), bf16[384,1,16,128]{3,2,1,0:T(8,128)(2,1)}, u32[]{:S(2)}, u32[]{:S(2)}) async-start(bf16[384,1,16,128]{3,2,1,0:T(8,128)(2,1)} %bitcast.2), calls=%async_computation | async-start | bytes 3145728 | tf_op jit(solution)/shard_map/all_to_all | solution.py:75
  186.4 234.6 %reduce-scatter.2.cloned.1.call-start = ((), (), s32[]{:S(2)}) async-start(), calls=%async_computation.5 | async-start | bytes 4718592 | tf_op jit(solution)/shard_map/reduce_scatter | solution.py:101
  252.6 34.6 %copy-start.3 = (f32[4,64,8]{2,0,1:T(4,128)S(1)}, f32[4,64,8]{2,0,1:T(4,128)}, u32[]{:S(2)}) copy-start(f32[4,64,8]{2,0,1:T(4,128)} %copy-done.2) | copy-start | bytes 24580
  252.6 34.6 %copy-start.5 = (f32[4,64,1,8,4]{3,4,0,1,2:T(4,128)S(1)}, f32[4,64,1,8,4]{3,4,0,1,2:T(4,128)}, u32[]{:S(2)}) copy-start(f32[4,64,1,8,4]{3,4,0,1,2:T(4,128)} %get-tuple-element.9) | copy-start | bytes 98308
  252.6 34.6 %copy-start.9 = (bf16[4,64,1,128]{3,1,2,0:T(8,128)(2,1)S(1)}, bf16[4,64,1,128]{3,1,2,0:T(8,128)(2,1)}, u32[]{:S(2)}) copy-start(bf16[4,64,1,128]{3,1,2,0:T(8,128)(2,1)} %param.18) | copy-start | bytes 196612
  252.7 170.1 %copy-start.1 = (bf16[4,64,8,128]{3,2,1,0:T(8,128)(2,1)S(1)}, bf16[4,64,8,128]{3,2,1,0:T(8,128)(2,1)}, u32[]{:S(2)}) copy-start(bf16[4,64,8,128]{3,2,1,0:T(8,128)(2,1)} %param.16) | copy-start | bytes 1572868
Sparse Core Ops, SparseCore 0:
  295.6 125.2 reduce-scatter.1
where the time goes:
time: 433 us; the launch traced here: 430 us
  waiting for transfers between devices  141 us (33%)
  local copies, waits for them, and re-layouts  116 us (27%)
  matrix products  87.5 us (20%)
  other arithmetic  39.8 us (9%)
  starting transfers between devices  31.8 us (7%)
  between operations  13.6 us (3%)
    reduce_scatter x1, waiting for transfers between devices, per_device(): lax.psum_scatter(partial_terms, 'tp', scatter_dimension=1, tiled=True)  125 us
    scatter x4, local copies, waits for them, and re-layouts, pack_pages(): return empty.at[target].set(pages)  60.2 us
    dot_general x1, matrix products, attention_weights(): jnp.einsum('srkgd,rpkod->srkgpo', query_block, keys_block, preferred_elem...  40.7 us
    dot_general x1, matrix products, per_device(): jnp.einsum('srkgpo,rpkod->srkgd', cached_w, values_block, preferred_eleme...  34.6 us
    gather x1, local copies, waits for them, and re-layouts, per_device(): keys_block = jnp.take(store_keys, block_table, axis=0)  25.8 us
    reduce_sum x2, other arithmetic, attention_weights(): total = jnp.sum(cached_exp, axis=-1) + jnp.sum(recent_exp, axis=-1)  24.9 us
    gather x1, local copies, waits for them, and re-layouts, per_device(): values_block = jnp.take(store_values, block_table, axis=0)  23.9 us
    all_to_all x1, waiting for transfers between devices, per_device(): lax.all_to_all(prompt_send_v, 'inst', split_axis=0, concat_axis=0, tiled=...  15.2 us
  transfers between devices with their start and end apart: 5, of which 3 were waited for; matrix products, arithmetic and copies ran while one was open for 37% of the time, Pallas kernels for 0%

commit v1 on v0

v1 whole, which is shorter than its diff:
```python
import functools

import jax
import jax.numpy as jnp
from jax import lax
from jax.experimental import pallas as pl
from jax.experimental.pallas import tpu as pltpu
from jax.sharding import Mesh, PartitionSpec as P

NAMES = ("ix", "izh", "izl", "ic", "ty", "tz")
SIZES = (4, 2, 2, 2, 4, 2)
INST = ("ix", "izh", "izl", "ic")
HALF = ("ix", "izl", "ic")
TP = ("ty", "tz")

N_INST = 32
N_HALF = 16
STEPS, ROWS, GROUPS, DH = 4, 64, 8, 128
QROWS = STEPS * GROUPS
PAGE, MAXP = 16, 48
POOL, OUT, MIG = 192, 192, 96
PCAP, MCAP = 12, 6
SLOTS = PCAP + MCAP
RECV = N_HALF * SLOTS
CHUNK_PAGES = 16
CHUNK = CHUNK_PAGES * PAGE
WIDE_CHUNKS = 4
POSITIONS = CHUNK_PAGES * WIDE_CHUNKS
UNROLL = 8
SCALE = DH ** -0.5
VMEM_LIMIT = 40 * 1024 * 1024


def pack_kernel(pdest, mdest, pk, pv, mk, mv, send, count):
    def clear(i, carry):
        count[i] = 0
        return carry

    def place(dest, keys, values, first, j):
        d = dest[j]
        k = count[d]
        count[d] = k + 1
        block = (d >> 3) * 8 + (d & 3) * 2 + ((d >> 2) & 1)
        slot = block * SLOTS + first + k
        send[slot, 0] = keys[j]
        send[slot, 1] = values[j]

    def prompt(j, carry):
        place(pdest, pk, pv, 0, j)
        return carry

    def moved(j, carry):
        place(mdest, mk, mv, PCAP, j)
        return carry

    lax.fori_loop(0, N_INST, clear, 0)
    lax.fori_loop(0, OUT, prompt, 0, unroll=4)
    lax.fori_loop(0, N_INST, clear, 0)
    lax.fori_loop(0, MIG, moved, 0, unroll=4)


def pack(pdest, mdest, pk, pv, mk, mv):
    smem = pl.BlockSpec(memory_space=pltpu.SMEM)
    vmem = pl.BlockSpec(memory_space=pltpu.VMEM)
    return pl.pallas_call(
        pack_kernel,
        out_shape=jax.ShapeDtypeStruct((N_INST * SLOTS, 2, PAGE, DH), jnp.bfloat16),
        in_specs=[smem, smem, vmem, vmem, vmem, vmem],
        out_specs=vmem,
        scratch_shapes=[pltpu.SMEM((N_INST,), jnp.int32)],
        compiler_params=pltpu.CompilerParams(vmem_limit_bytes=VMEM_LIMIT),
        name="pack_pages",
    )(pdest, mdest, pk, pv, mk, mv)


def attend_kernel(own, half, ctx, idx, bias, q, recv, *refs):
    if own:
        pool_k, pool_v, fresh, out, lse, kv, acc, sem = refs
    else:
        out, lse, kv, acc, sem = refs
    first = 1 + POOL + ROWS if own else 1
    copies = [
        pltpu.make_async_copy(recv.at[g, half[0]], kv.at[pl.ds(first + g * SLOTS, SLOTS)], sem)
        for g in range(N_HALF)
    ]
    if own:
        copies.append(pltpu.make_async_copy(pool_k, kv.at[pl.ds(1, POOL), 0], sem))
        copies.append(pltpu.make_async_copy(pool_v, kv.at[pl.ds(1, POOL), 1], sem))
        copies.append(pltpu.make_async_copy(fresh, kv.at[pl.ds(1 + POOL, ROWS)], sem))
    for copy in copies:
        copy.start()
    kv[0] = jnp.zeros((2, PAGE, DH), jnp.bfloat16)
    for copy in copies:
        copy.wait()

    lane = lax.broadcasted_iota(jnp.int32, (QROWS, CHUNK), 1)
    step = lax.broadcasted_iota(jnp.int32, (QROWS, CHUNK), 0) // GROUPS
    causal = jnp.where((lane > step) & (lane < PAGE), -jnp.inf, 0.0).astype(jnp.float32)
    column = lax.broadcasted_iota(jnp.int32, (QROWS, 128), 1)

    def chunk_pages(r, c):
        return [idx[r * POSITIONS + c * CHUNK_PAGES + p] for p in range(CHUNK_PAGES)]

    def chunk_scores(r, c, pages):
        keys = jnp.concatenate([kv[i, 0] for i in pages], axis=0)
        s = lax.dot_general(q[r], keys, (((1,), (1,)), ((), ())), preferred_element_type=jnp.float32)
        s = s * SCALE + bias[pl.ds(r, 1), pl.ds(c * CHUNK, CHUNK)]
        return s + causal if own and c == 0 else s

    def chunk_out(weights, pages):
        values = jnp.concatenate([kv[i, 1] for i in pages], axis=0)
        return jnp.dot(weights.astype(jnp.bfloat16), values, preferred_element_type=jnp.float32)

    def finish(r, m, total, product):
        safe = jnp.maximum(total, 1e-30)
        acc[pl.ds(r, QROWS, stride=ROWS), :] = product / safe
        return jnp.where(total > 0.0, m + jnp.log(safe), -1e30)

    def narrow(i, stats):
        for u in range(UNROLL):
            r = i * UNROLL + u
            pages = chunk_pages(r, 0)
            s = chunk_scores(r, 0, pages)
            m = jnp.maximum(jnp.max(s, axis=1, keepdims=True), -1e30)
            e = jnp.exp(s - m)
            total = jnp.sum(e, axis=1, keepdims=True)
            stats = jnp.where(column == r, finish(r, m, total, chunk_out(e, pages)), stats)
        return stats

    lse[...] = lax.fori_loop(0, ROWS // UNROLL, narrow, jnp.zeros((QROWS, 128), jnp.float32))

    def wide(r, carry):
        @pl.when(ctx[r] > (CHUNK_PAGES - 1) * PAGE)
        def _():
            scores = [chunk_scores(r, c, chunk_pages(r, c)) for c in range(WIDE_CHUNKS)]
            m = jnp.full((QROWS, 1), -1e30, jnp.float32)
            for s in scores:
                m = jnp.maximum(m, jnp.max(s, axis=1, keepdims=True))
            total = jnp.zeros((QROWS, 1), jnp.float32)
            product = jnp.zeros((QROWS, DH), jnp.float32)
            for c, s in enumerate(scores):
                e = jnp.exp(s - m)
                total = total + jnp.sum(e, axis=1, keepdims=True)
                product = product + chunk_out(e, chunk_pages(r, c))
            lse[...] = jnp.where(column == r, finish(r, m, total, product), lse[...])

        return carry

    lax.fori_loop(0, ROWS, wide, 0)
    out[...] = acc[...].astype(out.dtype)


def attend(own, half, ctx, idx, bias, q, recv, *local):
    smem = pl.BlockSpec(memory_space=pltpu.SMEM)
    vmem = pl.BlockSpec(memory_space=pltpu.VMEM)
    hbm = pl.BlockSpec(memory_space=pl.ANY)
    pages = 1 + RECV + (POOL + ROWS if own else 0)
    dtype = jnp.float32 if own else jnp.bfloat16
    return pl.pallas_call(
        functools.partial(attend_kernel, own),
        out_shape=(
            jax.ShapeDtypeStruct((QROWS * ROWS, DH), dtype),
            jax.ShapeDtypeStruct((QROWS, 128), jnp.float32),
        ),
        in_specs=[smem, smem, smem, vmem, vmem, hbm] + [hbm] * len(local),
        out_specs=(vmem, vmem),
        scratch_shapes=[
            pltpu.VMEM((pages, 2, PAGE, DH), jnp.bfloat16),
            pltpu.VMEM((QROWS * ROWS, DH), jnp.float32),
            pltpu.SemaphoreType.DMA,
        ],
        compiler_params=pltpu.CompilerParams(vmem_limit_bytes=VMEM_LIMIT),
        cost_estimate=pl.CostEstimate(flops=10**9, bytes_accessed=8 * 10**6, transcendentals=10**6),
        name="attend_own" if own else "attend_mirror",
    )(half, ctx, idx, bias, q, recv, *local)


def mix_kernel(o1, lse1, o2, lse2, weight, out, heads):
    @pl.when(pl.program_id(0) == 0)
    def _():
        top = jnp.maximum(lse1[...], lse2[...])
        e1 = jnp.exp(lse1[...] - top)
        e2 = jnp.exp(lse2[...] - top)
        inverse = 1.0 / (e1 + e2)
        f1 = (e1 * inverse).T
        f2 = (e2 * inverse).T
        for j in range(QROWS):
            t, h = j // GROUPS, j % GROUPS
            rows = pl.ds(j * ROWS, ROWS)
            merged = f1[:ROWS, j : j + 1] * o1[rows, :] + f2[:ROWS, j : j + 1] * o2[rows, :].astype(jnp.float32)
            heads[pl.ds(t * ROWS, ROWS), pl.ds(h * DH, DH)] = merged.astype(jnp.bfloat16)

    out[0] = jnp.dot(heads[...], weight[...], preferred_element_type=jnp.float32).astype(jnp.bfloat16)


def mix(o1, lse1, o2, lse2, weight):
    depth, width = weight.shape
    block = width // 8
    whole = lambda shape: pl.BlockSpec(shape, lambda n: (0, 0))
    return pl.pallas_call(
        mix_kernel,
        grid=(8,),
        out_shape=jax.ShapeDtypeStruct((8, STEPS * ROWS, block), jnp.bfloat16),
        in_specs=[
            whole(o1.shape),
            whole(lse1.shape),
            whole(o2.shape),
            whole(lse2.shape),
            pl.BlockSpec((depth, block), lambda n: (0, n)),
        ],
        out_specs=pl.BlockSpec((1, STEPS * ROWS, block), lambda n: (n, 0, 0)),
        scratch_shapes=[pltpu.VMEM((STEPS * ROWS, depth), jnp.bfloat16)],
        compiler_params=pltpu.CompilerParams(vmem_limit_bytes=VMEM_LIMIT),
        name="merge_and_project",
    )(o1, lse1, o2, lse2, weight)


def routes(own, table, lengths, half):
    column = jnp.arange(MAXP, dtype=jnp.int32)[None, :]
    valid = column * PAGE < lengths[:, None]
    prompt = table < POOL + N_INST * PCAP
    px, mx = table - POOL, table - (POOL + N_INST * PCAP)
    source = jnp.where(prompt, px // PCAP, mx // MCAP)
    rank = jnp.where(prompt, px % PCAP, PCAP + mx % MCAP)
    group = (source >> 3) * 4 + (source & 3)
    arrived = (table >= POOL) & (((source >> 2) & 1) == half)
    if own:
        place = jnp.where(table < POOL, 1 + table, 1 + POOL + ROWS + group * SLOTS + rank)
        here = valid & (arrived | (table < POOL))
        fresh = 1 + POOL + jnp.arange(ROWS, dtype=jnp.int32)[:, None]
    else:
        place = 1 + group * SLOTS + rank
        here = valid & arrived
        fresh = jnp.zeros((ROWS, 1), jnp.int32)
    spare = POSITIONS - 1 - MAXP
    idx = jnp.concatenate([fresh, jnp.where(here, place, 0), jnp.zeros((ROWS, spare), jnp.int32)], axis=1)
    token = (column * PAGE)[:, :, None] + jnp.arange(PAGE, dtype=jnp.int32)[None, None, :]
    seen = (here[:, :, None] & (token < lengths[:, None, None])).reshape(ROWS, MAXP * PAGE)
    seen = jnp.concatenate(
        [jnp.full((ROWS, PAGE), own), seen, jnp.zeros((ROWS, spare * PAGE), jnp.bool_)], axis=1
    )
    return idx.reshape(-1), jnp.where(seen, 0.0, -jnp.inf).astype(jnp.float32)


def by_row(queries):
    return queries.transpose(1, 0, 2, 3).reshape(ROWS, QROWS, DH)


def per_device(
    queries,
    new_keys,
    new_values,
    pool_keys,
    pool_values,
    prompt_keys,
    prompt_values,
    moved_keys,
    moved_values,
    prompt_dest,
    moved_dest,
    block_table,
    context_len,
    out_weight,
):
    page = lambda x: x.reshape(x.shape[0], PAGE, DH)
    swap = [(0, 1), (1, 0)]
    half = lax.axis_index("izh")

    send = pack(
        prompt_dest, moved_dest, page(prompt_keys), page(prompt_values), page(moved_keys), page(moved_values)
    )
    send = send.reshape(N_HALF, 2 * SLOTS, 2, PAGE, DH)
    recv = lax.all_to_all(send, HALF, split_axis=0, concat_axis=0, tiled=True)
    recv = recv.reshape(N_HALF, 2, SLOTS, 2, PAGE, DH)

    tables = jnp.concatenate([block_table, context_len[:, None]], axis=1)
    mirror_q = lax.ppermute(queries, "izh", swap)
    mirror_tables = lax.ppermute(tables, "izh", swap)
    mirror_len = mirror_tables[:, MAXP]

    idx2, bias2 = routes(False, mirror_tables[:, :MAXP], mirror_len, half)
    o2, lse2 = attend(False, (1 - half)[None], mirror_len, idx2, bias2, by_row(mirror_q), recv)
    o2 = lax.ppermute(o2, "izh", swap)
    lse2 = lax.ppermute(lse2, "izh", swap)

    fresh = jnp.stack([new_keys, new_values], axis=0).reshape(2, STEPS, ROWS, DH).transpose(2, 0, 1, 3)
    fresh = jnp.pad(fresh, ((0, 0), (0, 0), (0, PAGE - STEPS), (0, 0)))
    idx1, bias1 = routes(True, block_table, context_len, half)
    o1, lse1 = attend(
        True, half[None], context_len, idx1, bias1, by_row(queries), recv, page(pool_keys), page(pool_values), fresh
    )

    terms = mix(o1, lse1, o2, lse2, out_weight)
    terms = terms.reshape(4, 2, STEPS * ROWS, -1)
    got = lax.all_to_all(terms, "ty", split_axis=0, concat_axis=0, tiled=True)
    column = got.astype(jnp.float32).sum(axis=0)
    side = lax.axis_index("tz")
    mine = jnp.where(side == 0, column[0], column[1])
    other = jnp.where(side == 0, column[1], column[0]).astype(jnp.bfloat16)
    other = lax.ppermute(other, "tz", swap)
    mixed = (mine + other.astype(jnp.float32)).astype(jnp.bfloat16)
    return mixed.reshape(STEPS, ROWS, -1)


def solution(mesh):
    fine = Mesh(mesh.devices.reshape(SIZES), NAMES)
    in_specs = (
        P(None, INST, TP, None),
        P(None, INST, TP, None),
        P(None, INST, TP, None),
        P(INST, TP, None, None),
        P(INST, TP, None, None),
        P(INST, TP, None, None),
        P(INST, TP, None, None),
        P(INST, TP, None, None),
        P(INST, TP, None, None),
        P(INST),
        P(INST),
        P(INST, None),
        P(INST),
        P(TP, None),
    )
    return jax.shard_map(
        per_device, mesh=fine, in_specs=in_specs, out_specs=P(None, INST, TP), check_vma=False
    )
```

time: 433 us -> 190 us (0.44)
  local copies, waits for them, and re-layouts: 116 us -> 13.7 us
  matrix products: 87.5 us -> 0 us
  Pallas kernels: 0 us -> 50.3 us
  waiting for transfers between devices: 141 us -> 98.9 us
  other arithmetic: 39.8 us -> 1.91 us
  between operations: 13.6 us -> 0.22 us
  starting transfers between devices: 31.8 us -> 24.9 us
    reduce_scatter x1 -> x0, waiting for transfers between devices: 125 us -> none  [per_device(): lax.psum_scatter(partial_terms, 'tp', scatter_dimension=1, tiled=True)]
    dot_general x5 -> x0, matrix products: 87.5 us -> none  [the longest x1 40.7 us: attention_weights(): jnp.einsum('srkgd,rpkod->srkgpo', query_block, keys_block, preferred_elem...]
    ppermute x0 -> x5, waiting for transfers between devices: none -> 72.2 us  [the longest x1 49.8 us: per_device(): mirror_tables = lax.ppermute(tables, 'izh', swap)]
    scatter x4 -> x0, local copies, waits for them, and re-layouts: 60.2 us -> none  [pack_pages(): return empty.at[target].set(pages)]
    pallas_call x0 -> x4, Pallas kernels: none -> 50.3 us  [the longest x2 41.5 us: attend(): pl.pallas_call(functools.partial(attend_kernel, own), out_shape=(jax.Shap...]
    gather x2 -> x0, local copies, waits for them, and re-layouts: 49.8 us -> none  [the longest x1 25.8 us: per_device(): keys_block = jnp.take(store_keys, block_table, axis=0)]
    reduce_sum x4 -> x1, other arithmetic: 26.5 us -> 0.34 us  [per_device(): column = got.astype(jnp.float32).sum(axis=0)]
    all_to_all x4 -> x2, starting transfers between devices: 31.6 us -> 10.8 us  [the longest x1 5.93 us: per_device(): recv = lax.all_to_all(send, HALF, split_axis=0, concat_axis=0, tiled=True)]
  transfers between devices with their start and end apart: 5 -> 7, of which waited for: 3 -> 6; matrix products, arithmetic and copies ran while one was open for 37% -> 2% of each run, Pallas kernels for 0% -> 11%
where the time goes in v1:
time: 190 us
  waiting for transfers between devices  98.9 us (52%)
  Pallas kernels  50.3 us (26%)
  starting transfers between devices  24.9 us (13%)
  local copies, waits for them, and re-layouts  13.7 us (7%)
  other arithmetic  1.91 us (1%)
    ppermute x1, waiting for transfers between devices, per_device(): mirror_tables = lax.ppermute(tables, 'izh', swap)  49.8 us
    pallas_call x2, Pallas kernels, attend(): pl.pallas_call(functools.partial(attend_kernel, own), out_shape=(jax.Shap...  41.5 us
    all_to_all x1, waiting for transfers between devices, per_device(): got = lax.all_to_all(terms, 'ty', split_axis=0, concat_axis=0, tiled=True)  23.8 us
    unnamed x30, local copies, waits for them, and re-layouts  11.2 us
    ppermute x1, waiting for transfers between devices, per_device(): other = lax.ppermute(other, 'tz', swap)  11 us
    ppermute x1, waiting for transfers between devices, per_device(): mirror_q = lax.ppermute(queries, 'izh', swap)  9.89 us
    ppermute x1, starting transfers between devices, per_device(): other = lax.ppermute(other, 'tz', swap)  7.5 us
    pallas_call x1, Pallas kernels, mix(): pl.pallas_call(mix_kernel, grid=(8,), out_shape=jax.ShapeDtypeStruct((8,...  6.22 us
  transfers between devices with their start and end apart: 7, of which 6 were waited for; matrix products, arithmetic and copies ran while one was open for 2% of the time, Pallas kernels for 11%

profile of v1, /device:TPU:8, one launch (start us, length us, event | category | flops | bytes accessed | tf_op | source)
XLA Modules:
  0.0 189.9 jit_solution(14155100460192780758)
XLA Ops:
  0.0 1.1 copy-done.4
  1.1 1.1 copy-done.5
  2.3 1.0 copy-done.6
  3.3 1.0 copy-done.7
  5.6 2.5 %pack_pages.1 = bf16[576,2,16,128]{3,2,1,0:T(8,128)(2,1)S(1)} custom-call(s32[192]{0:T(256)S(1)} %copy-done.9, s32[96]{0:T(128)S(1)} %copy-done.10, bf16[192,16,128]{2,1,0:T(8,128)(2,1)S(1)} %bitcast.47, bf16[192,16,128]{2,1,0:T(8,128)(2,1)S(1)} %bitcast.48, bf16[96,16,128]{2,1,0:T(8,128)(2,1)S(1)} %bitcast.49, bf16[96,16,128]{2,1,0:T(8,128)(2,1)S(1)} %bitcast.50), custom_call_target="tpu_custom_call" | custom-call | tf_op jit(solution)/shard_map/pack_pages/pallas_call | solution.py:65
  8.2 2.2 %copy-done = bf16[576,2,16,128]{3,2,1,0:T(8,128)(2,1)} copy-done((bf16[576,2,16,128]{3,2,1,0:T(8,128)(2,1)}, bf16[576,2,16,128]{3,2,1,0:T(8,128)(2,1)S(1)}, u32[]{:S(2)}) %copy-start) | copy-done | bytes 4718616
  10.3 5.9 %all-to-all-start = ((bf16[16,36,2,16,128]{4,3,2,1,0:T(8,128)(2,1)}), bf16[16,36,2,16,128]{4,3,2,1,0:T(8,128)(2,1)}, u32[]{:S(2)}, u32[]{:S(2)}) async-start(bf16[16,36,2,16,128]{4,3,2,1,0:T(8,128)(2,1)} %bitcast.44), calls=%async_computation | async-start | bytes 9437184 | tf_op jit(solution)/shard_map/all_to_all | solution.py:273
  16.3 3.4 %collective-permute-start = (s32[64,49]{0,1:T(8,128)S(1)}, s32[64,49]{0,1:T(8,128)S(1)}, u32[]{:S(2)}, u32[]{:S(2)}) collective-permute-start(s32[64,49]{0,1:T(8,128)S(1)} %pad_add_fusion), channel_id=1, source_target_pairs={{0,32},{32,0},{1,33},{33,1},{2,34},{34,2},{3,35},{35,3},{4,36},{36... | collective-permute-start | bytes 37640 | tf_op jit(solution)/shard_map/ppermute | solution.py:278
  20.3 49.8 %collective-permute-done = s32[64,49]{0,1:T(8,128)S(1)} collective-permute-done((s32[64,49]{0,1:T(8,128)S(1)}, s32[64,49]{0,1:T(8,128)S(1)}, u32[]{:S(2)}, u32[]{:S(2)}) %collective-permute-start) | collective-permute-done | bytes 12576 | tf_op jit(solution)/shard_map/ppermute | solution.py:278
  71.2 9.9 %collective-permute-done.1 = bf16[4,64,8,128]{3,2,1,0:T(8,128)(2,1)S(1)} collective-permute-done((bf16[4,64,8,128]{3,2,1,0:T(8,128)(2,1)S(1)}, bf16[4,64,8,128]{3,2,1,0:T(8,128)(2,1)S(1)}, u32[]{:S(2)}, u32[]{:S(2)}) %collective-permute-start.1) | collective-permute-done | bytes 524320 | tf_op jit(solution)/shard_map/ppermute | solution.py:277
  81.2 3.0 %all-to-all-done = bf16[16,36,2,16,128]{4,3,2,1,0:T(8,128)(2,1)} async-done(((bf16[16,36,2,16,128]{4,3,2,1,0:T(8,128)(2,1)}), bf16[16,36,2,16,128]{4,3,2,1,0:T(8,128)(2,1)}, u32[]{:S(2)}, u32[]{:S(2)}) %all-to-all-start) | async-done | bytes 4718624 | tf_op jit(solution)/shard_map/all_to_all | solution.py:273
  84.2 21.1 %attend_mirror.1 = (bf16[2048,128]{1,0:T(8,128)(2,1)}, f32[32,128]{1,0:T(8,128)S(1)}) custom-call(s32[1]{0:T(128)} %bitcast.16.half, s32[64]{0:T(128)S(1)} %slice_bitcast_fusion.ctx, s32[4096]{0:T(1024)S(1)} %reshape.113.idx, f32[64,1024]{1,0:T(8,128)S(1)} %get-tuple-element.19.bias, bf16[64,32,128]{2,1,0:T(8,128)(2,1)S(1)} %copy_bitcast_fusion.q, ...), custom_call_target="tpu_custom_call" | custom-call | flops 1000000000 | bytes 8000000 | tf_op jit(solution)/shard_map/attend_mirror/pallas_call | solution.py:159
  105.3 0.8 collective-permute-start.2
  106.4 1.1 copy_bitcast_fusion.1.q
  107.7 2.2 %collective-permute-start.3 = (f32[32,128]{1,0:T(8,128)S(1)}, f32[32,128]{1,0:T(8,128)S(1)}, u32[]{:S(2)}, u32[]{:S(2)}) collective-permute-start(f32[32,128]{1,0:T(8,128)S(1)} %get-tuple-element.12), channel_id=1, source_target_pairs={{0,32},{32,0},{1,33},{33,1},{2,34},{34,2},{3,35},{35,3},{4,36},{36... | collective-permute-start | bytes 49160 | tf_op jit(solution)/shard_map/ppermute | solution.py:284
  110.0 20.4 %attend_own.1 = (f32[2048,128]{1,0:T(8,128)S(1)}, f32[32,128]{1,0:T(8,128)S(1)}) custom-call(s32[1]{0:T(128)} %bitcast.half, s32[64]{0:T(128)S(1)} %copy-done.8, s32[4096]{0:T(1024)S(1)} %reshape.102.idx, f32[64,1024]{1,0:T(8,128)S(1)} %get-tuple-element.20.bias, bf16[64,32,128]{2,1,0:T(8,128)(2,1)S(1)} %copy_bitcast_fusion.1.q, ...), custom_call_target="tpu_custom_call" | custom-call | flops 1000000000 | bytes 8000000 | tf_op jit(solution)/shard_map/attend_own/pallas_call | solution.py:159
  130.4 1.6 collective-permute-done.3.lse2
  131.9 3.4 %copy-done.1 = bf16[1024,4096]{1,0:T(8,128)(2,1)S(1)} copy-done((bf16[1024,4096]{1,0:T(8,128)(2,1)S(1)}, bf16[1024,4096]{1,0:T(8,128)(2,1)}, u32[]{:S(2)}) %copy-start.1) | copy-done | bytes 8388632
  135.3 6.2 %merge_and_project.1 = bf16[8,256,512]{2,1,0:T(8,128)(2,1)} custom-call(f32[2048,128]{1,0:T(8,128)S(1)} %get-tuple-element.9.o1, f32[32,128]{1,0:T(8,128)S(1)} %get-tuple-element.10.lse1, bf16[2048,128]{1,0:T(8,128)(2,1)S(1)} %collective-permute-done.2.o2, f32[32,128]{1,0:T(8,128)S(1)} %collective-permute-done.3.lse2, bf16[1024,4096]{1,0:T(8,128)(2,1)S(1)} %copy-done.1), custom_call_target="tpu_custom_call" | custom-call | tf_op jit(solution)/shard_map/merge_and_project/pallas_call | solution.py:200
  141.5 4.9 %all-to-all-start.1 = ((bf16[4,2,256,512]{3,2,1,0:T(8,128)(2,1)}), bf16[4,2,256,512]{3,2,1,0:T(8,128)(2,1)S(1)}, u32[]{:S(2)}, u32[]{:S(2)}) async-start(bf16[4,2,256,512]{3,2,1,0:T(8,128)(2,1)} %bitcast.22), calls=%async_computation.1 | async-start | bytes 4194304 | tf_op jit(solution)/shard_map/all_to_all | solution.py:295
  146.4 23.8 %all-to-all-done.1 = bf16[4,2,256,512]{3,2,1,0:T(8,128)(2,1)S(1)} async-done(((bf16[4,2,256,512]{3,2,1,0:T(8,128)(2,1)}), bf16[4,2,256,512]{3,2,1,0:T(8,128)(2,1)S(1)}, u32[]{:S(2)}, u32[]{:S(2)}) %all-to-all-start.1) | async-done | bytes 2097184 | tf_op jit(solution)/shard_map/all_to_all | solution.py:295
  170.6 7.5 %collective-permute-start.4 = (bf16[256,512]{1,0:T(8,128)(2,1)S(1)}, bf16[256,512]{1,0:T(8,128)(2,1)S(1)}, u32[]{:S(2)}, u32[]{:S(2)}) collective-permute-start(bf16[256,512]{1,0:T(8,128)(2,1)S(1)} %fusion.1), channel_id=1, source_target_pairs={{0,1},{1,0},{2,3},{3,2},{4,5},{5,4},{6,7},{7,6},{8,9},{9,8},{10,11... | collective-permute-start | bytes 786440 | tf_op jit(solution)/shard_map/ppermute | solution.py:300
  178.1 11.0 %collective-permute-done.4 = bf16[256,512]{1,0:T(8,128)(2,1)S(1)} collective-permute-done((bf16[256,512]{1,0:T(8,128)(2,1)S(1)}, bf16[256,512]{1,0:T(8,128)(2,1)S(1)}, u32[]{:S(2)}, u32[]{:S(2)}) %collective-permute-start.4) | collective-permute-done | bytes 262176 | tf_op jit(solution)/shard_map/ppermute | solution.py:300
  189.1 0.8 fusion
  (62 shorter events, 3.9 us)
Async XLA Ops:
  0.0 1.1 copy-start.4
  1.1 1.1 copy-start.5
  2.3 1.0 copy-start.6
  3.3 1.0 copy-start.7
  4.3 0.7 copy-start.9
  4.9 0.7 copy-start.10
  8.1 2.2 %copy-start = (bf16[576,2,16,128]{3,2,1,0:T(8,128)(2,1)}, bf16[576,2,16,128]{3,2,1,0:T(8,128)(2,1)S(1)}, u32[]{:S(2)}) copy-start(bf16[576,2,16,128]{3,2,1,0:T(8,128)(2,1)S(1)} %pack_pages.1) | copy-start | bytes 14155780
  10.3 6.0 %copy-start.8 = (s32[64]{0:T(128)S(1)}, s32[64]{0:T(128)}, u32[]{:S(2)}) copy-start(s32[64]{0:T(128)} %ctx.1) | copy-start | bytes 772
  10.3 6.0 %copy-start.12 = (s32[64,48]{0,1:T(8,128)S(1)}, s32[64,48]{0,1:T(8,128)}, u32[]{:S(2)}) copy-start(s32[64,48]{0,1:T(8,128)} %param.25) | copy-start | bytes 36868
  10.3 9.4 %copy-start.11 = (bf16[4,64,8,128]{3,2,1,0:T(8,128)(2,1)S(1)}, bf16[4,64,8,128]{3,2,1,0:T(8,128)(2,1)}, u32[]{:S(2)}) copy-start(bf16[4,64,8,128]{3,2,1,0:T(8,128)(2,1)} %param.14) | copy-start | bytes 1572868
  10.3 73.8 %all-to-all-start = ((bf16[16,36,2,16,128]{4,3,2,1,0:T(8,128)(2,1)}), bf16[16,36,2,16,128]{4,3,2,1,0:T(8,128)(2,1)}, u32[]{:S(2)}, u32[]{:S(2)}) async-start(bf16[16,36,2,16,128]{4,3,2,1,0:T(8,128)(2,1)} %bitcast.44), calls=%async_computation | async-start | bytes 9437184 | tf_op jit(solution)/shard_map/all_to_all | solution.py:273
  16.3 53.7 %collective-permute-start = (s32[64,49]{0,1:T(8,128)S(1)}, s32[64,49]{0,1:T(8,128)S(1)}, u32[]{:S(2)}, u32[]{:S(2)}) collective-permute-start(s32[64,49]{0,1:T(8,128)S(1)} %pad_add_fusion), channel_id=1, source_target_pairs={{0,32},{32,0},{1,33},{33,1},{2,34},{34,2},{3,35},{35,3},{4,36},{36... | collective-permute-start | bytes 37640 | tf_op jit(solution)/shard_map/ppermute | solution.py:278
  19.7 61.4 %collective-permute-start.1 = (bf16[4,64,8,128]{3,2,1,0:T(8,128)(2,1)S(1)}, bf16[4,64,8,128]{3,2,1,0:T(8,128)(2,1)S(1)}, u32[]{:S(2)}, u32[]{:S(2)}) collective-permute-start(bf16[4,64,8,128]{3,2,1,0:T(8,128)(2,1)S(1)} %copy-done.11), channel_id=1, source_target_pairs={{0,32},{32,0},{1,33},{33,1},{2,34},{34,2},{3,35},{35,3},{4,36},{36... | collective-permute-start | bytes 1572872 | tf_op jit(solution)/shard_map/ppermute | solution.py:277
  19.9 86.2 %copy-start.13 = (bf16[4,64,1,128]{3,1,2,0:T(8,128)(2,1)S(1)}, bf16[4,64,1,128]{3,1,2,0:T(8,128)(2,1)}, u32[]{:S(2)}) copy-start(bf16[4,64,1,128]{3,1,2,0:T(8,128)(2,1)} %param.16) | copy-start | bytes 196612
  19.9 86.2 %copy-start.14 = (bf16[4,64,1,128]{3,1,2,0:T(8,128)(2,1)S(1)}, bf16[4,64,1,128]{3,1,2,0:T(8,128)(2,1)}, u32[]{:S(2)}) copy-start(bf16[4,64,1,128]{3,1,2,0:T(8,128)(2,1)} %param.15) | copy-start | bytes 196612
  81.2 28.8 %copy-start.2 = (bf16[192,1,16,128]{3,2,1,0:T(8,128)(2,1)S(1)}, bf16[192,1,16,128]{3,2,1,0:T(8,128)(2,1)}, u32[]{:S(2)}) copy-start(bf16[192,1,16,128]{3,2,1,0:T(8,128)(2,1)} %param.17) | copy-start | bytes 2359300
  81.2 28.8 %copy-start.3 = (bf16[192,1,16,128]{3,2,1,0:T(8,128)(2,1)S(1)}, bf16[192,1,16,128]{3,2,1,0:T(8,128)(2,1)}, u32[]{:S(2)}) copy-start(bf16[192,1,16,128]{3,2,1,0:T(8,128)(2,1)} %param.18) | copy-start | bytes 2359300
  105.3 26.6 %collective-permute-start.2 = (bf16[2048,128]{1,0:T(8,128)(2,1)}, bf16[2048,128]{1,0:T(8,128)(2,1)S(1)}, u32[]{:S(2)}, u32[]{:S(2)}) collective-permute-start(bf16[2048,128]{1,0:T(8,128)(2,1)} %get-tuple-element.11), channel_id=1, source_target_pairs={{0,32},{32,0},{1,33},{33,1},{2,34},{34,2},{3,35},{35,3},{4,36},{36... | collective-permute-start | bytes 1572872 | tf_op jit(solution)/shard_map/ppermute | solution.py:283
  107.7 24.2 %collective-permute-start.3 = (f32[32,128]{1,0:T(8,128)S(1)}, f32[32,128]{1,0:T(8,128)S(1)}, u32[]{:S(2)}, u32[]{:S(2)}) collective-permute-start(f32[32,128]{1,0:T(8,128)S(1)} %get-tuple-element.12), channel_id=1, source_target_pairs={{0,32},{32,0},{1,33},{33,1},{2,34},{34,2},{3,35},{35,3},{4,36},{36... | collective-permute-start | bytes 49160 | tf_op jit(solution)/shard_map/ppermute | solution.py:284
  131.9 3.4 %copy-start.1 = (bf16[1024,4096]{1,0:T(8,128)(2,1)S(1)}, bf16[1024,4096]{1,0:T(8,128)(2,1)}, u32[]{:S(2)}) copy-start(bf16[1024,4096]{1,0:T(8,128)(2,1)} %weight.1) | copy-start | bytes 25165828
  141.5 28.7 %all-to-all-start.1 = ((bf16[4,2,256,512]{3,2,1,0:T(8,128)(2,1)}), bf16[4,2,256,512]{3,2,1,0:T(8,128)(2,1)S(1)}, u32[]{:S(2)}, u32[]{:S(2)}) async-start(bf16[4,2,256,512]{3,2,1,0:T(8,128)(2,1)} %bitcast.22), calls=%async_computation.1 | async-start | bytes 4194304 | tf_op jit(solution)/shard_map/all_to_all | solution.py:295
  170.6 18.5 %collective-permute-start.4 = (bf16[256,512]{1,0:T(8,128)(2,1)S(1)}, bf16[256,512]{1,0:T(8,128)(2,1)S(1)}, u32[]{:S(2)}, u32[]{:S(2)}) collective-permute-start(bf16[256,512]{1,0:T(8,128)(2,1)S(1)} %fusion.1), channel_id=1, source_target_pairs={{0,1},{1,0},{2,3},{3,2},{4,5},{5,4},{6,7},{7,6},{8,9},{9,8},{10,11... | collective-permute-start | bytes 786440 | tf_op jit(solution)/shard_map/ppermute | solution.py:300

commit v2 on v1

v2 whole, which is shorter than its diff:
```python
import functools

import jax
import jax.numpy as jnp
from jax import lax
from jax.experimental import pallas as pl
from jax.experimental.pallas import tpu as pltpu
from jax.sharding import Mesh, PartitionSpec as P

NAMES = ("ix", "izh", "izl", "ic", "ty", "tz")
SIZES = (4, 2, 2, 2, 4, 2)
INST = ("ix", "izh", "izl", "ic")
HALF = ("ix", "izl", "ic")
TP = ("ty", "tz")

N_INST = 32
N_HALF = 16
STEPS, ROWS, GROUPS, DH = 4, 64, 8, 128
QROWS = STEPS * GROUPS
PAGE, MAXP = 16, 48
POOL, OUT, MIG = 192, 192, 96
PCAP, MCAP = 12, 6
SLOTS = PCAP + MCAP
RECV = N_HALF * SLOTS
NARROW = 8
WIDE = 16
WIDE_CHUNKS = 4
UNROLL = 2
POSITIONS = WIDE * WIDE_CHUNKS
TEAM = 4
TEAMS = ROWS // TEAM
LANES = TEAM * QROWS
SCALE = DH ** -0.5
VMEM_LIMIT = 60 * 1024 * 1024

SMEM = pl.BlockSpec(memory_space=pltpu.SMEM)
VMEM = pl.BlockSpec(memory_space=pltpu.VMEM)
ANY = pl.BlockSpec(memory_space=pl.ANY)
PARAMS = pltpu.CompilerParams(vmem_limit_bytes=VMEM_LIMIT)


def pack_kernel(half, pdest, mdest, pk, pv, mk, mv, far, near, pages, send, count, sems, out_sems):
    loads = [
        pltpu.make_async_copy(pk, pages.at[pl.ds(0, OUT), 0], sems.at[0]),
        pltpu.make_async_copy(pv, pages.at[pl.ds(0, OUT), 1], sems.at[1]),
        pltpu.make_async_copy(mk, pages.at[pl.ds(OUT, MIG), 0], sems.at[2]),
        pltpu.make_async_copy(mv, pages.at[pl.ds(OUT, MIG), 1], sems.at[3]),
    ]
    for load in loads:
        load.start()
    mine = half[0]

    def clear(i, carry):
        count[i] = 0
        return carry

    def place(dest, first, origin, j):
        d = dest[j]
        k = count[d]
        count[d] = k + 1
        group = (d >> 3) * 4 + (d & 3)
        here = jnp.where(((d >> 2) & 1) == mine, RECV, 0)
        slot = here + group * SLOTS + first + k
        send[slot] = pages[origin + j]

    def prompt(j, carry):
        place(pdest, 0, 0, j)
        return carry

    def moved(j, carry):
        place(mdest, PCAP, OUT, j)
        return carry

    lax.fori_loop(0, N_INST, clear, 0)
    loads[0].wait()
    loads[1].wait()
    lax.fori_loop(0, OUT, prompt, 0, unroll=4)
    lax.fori_loop(0, N_INST, clear, 0)
    loads[2].wait()
    loads[3].wait()
    lax.fori_loop(0, MIG, moved, 0, unroll=4)
    stores = [
        pltpu.make_async_copy(send.at[pl.ds(0, RECV)], far, out_sems.at[0]),
        pltpu.make_async_copy(send.at[pl.ds(RECV, RECV)], near, out_sems.at[1]),
    ]
    for store in stores:
        store.start()
    for store in stores:
        store.wait()


def pack(half, pdest, mdest, pk, pv, mk, mv):
    shape = jax.ShapeDtypeStruct((RECV, 2, PAGE, DH), jnp.bfloat16)
    return pl.pallas_call(
        pack_kernel,
        out_shape=(shape, shape),
        in_specs=[SMEM, SMEM, SMEM, ANY, ANY, ANY, ANY],
        out_specs=(ANY, ANY),
        scratch_shapes=[
            pltpu.VMEM((OUT + MIG, 2, PAGE, DH), jnp.bfloat16),
            pltpu.VMEM((2 * RECV, 2, PAGE, DH), jnp.bfloat16),
            pltpu.SMEM((N_INST,), jnp.int32),
            pltpu.SemaphoreType.DMA((4,)),
            pltpu.SemaphoreType.DMA((2,)),
        ],
        compiler_params=PARAMS,
        name="pack_pages",
    )(half, pdest, mdest, pk, pv, mk, mv)


def attention(fresh, idx, count, tokens, q, kv, out, lse, scores):
    lane = lax.broadcasted_iota(jnp.int32, (1, LANES), 1)
    team_row = lane // QROWS
    step = (lane % QROWS) // GROUPS

    def load(r, first, n, which):
        return [kv[idx[r * POSITIONS + first + p], which] for p in range(n)]

    def mask(s, first, limit):
        token = lax.broadcasted_iota(jnp.int32, s.shape, 0) + first
        seen = token < limit
        if fresh:
            seen = token < jnp.where(token < PAGE, step + 1, limit)
        return jnp.where(seen, s * SCALE, -jnp.inf)

    def dot_nt(a, b):
        return lax.dot_general(a, b, (((1,), (1,)), ((), ())), preferred_element_type=jnp.float32)

    def narrow(g):
        width = NARROW * PAGE
        rows = [g * TEAM + i for i in range(TEAM)]
        keys = jnp.concatenate([k for r in rows for k in load(r, 0, NARROW, 0)], axis=0)
        s_all = dot_nt(keys, q[g])
        s = s_all[:width]
        limit = jnp.full((1, LANES), tokens[rows[0]], jnp.int32)
        owner = lax.broadcasted_iota(jnp.int32, (width, LANES), 1) // QROWS
        for i in range(1, TEAM):
            s = jnp.where(owner == i, s_all[i * width : (i + 1) * width], s)
            limit = jnp.where(team_row == i, tokens[rows[i]], limit)
        s = mask(s, 0, limit)
        m = jnp.maximum(jnp.max(s, axis=0, keepdims=True), -1e30)
        e = jnp.exp(s - m)
        total = jnp.sum(e, axis=0, keepdims=True)
        safe = jnp.maximum(total, 1e-30)
        lse[pl.ds(g, 1), :] = jnp.where(total > 0.0, m + jnp.log(safe), -1e30)
        weights = (e * (1.0 / safe)).T.astype(jnp.bfloat16)
        for i in range(TEAM):
            values = jnp.concatenate(load(rows[i], 0, NARROW, 1), axis=0)
            part = weights[i * QROWS : (i + 1) * QROWS]
            first = pl.multiple_of(g * LANES + i * QROWS, QROWS)
            out[pl.ds(first, QROWS), :] = jnp.dot(part, values, preferred_element_type=jnp.float32)

    def narrow_body(n, carry):
        for u in range(UNROLL):
            narrow(n * UNROLL + u)
        return carry

    lax.fori_loop(0, TEAMS // UNROLL, narrow_body, 0)

    def wide(r):
        width = WIDE * PAGE
        chunks = (count[r] + WIDE - 1) // WIDE
        g, i = r // TEAM, r % TEAM

        def first_pass(c, m):
            keys = jnp.concatenate(load(r, c * WIDE, WIDE, 0), axis=0)
            s = mask(dot_nt(keys, q[g]), c * width, tokens[r])
            scores[c] = s
            return jnp.maximum(m, jnp.max(s, axis=0, keepdims=True))

        m = lax.fori_loop(0, chunks, first_pass, jnp.full((1, LANES), -1e30, jnp.float32))

        def second_pass(c, total):
            e = jnp.exp(scores[c] - m)
            scores[c] = e
            return total + jnp.sum(e, axis=0, keepdims=True)

        total = lax.fori_loop(0, chunks, second_pass, jnp.zeros((1, LANES), jnp.float32))
        safe = jnp.maximum(total, 1e-30)
        inverse = 1.0 / safe

        def third_pass(c, product):
            weights = (scores[c] * inverse).T.astype(jnp.bfloat16)
            values = jnp.concatenate(load(r, c * WIDE, WIDE, 1), axis=0)
            return product + jnp.dot(weights, values, preferred_element_type=jnp.float32)

        product = lax.fori_loop(0, chunks, third_pass, jnp.zeros((LANES, DH), jnp.float32))
        rows = pl.ds(pl.multiple_of(g * LANES, LANES), LANES)
        block = lax.broadcasted_iota(jnp.int32, (LANES, DH), 0) // QROWS
        out[rows, :] = jnp.where(block == i, product, out[rows, :])
        new = jnp.where(total > 0.0, m + jnp.log(safe), -1e30)
        lse[pl.ds(g, 1), :] = jnp.where(team_row == i, new, lse[pl.ds(g, 1), :])

    def wide_body(r, carry):
        pl.when(count[r] > NARROW)(lambda: wide(r))
        return carry

    lax.fori_loop(0, ROWS, wide_body, 0)


SCORES = pltpu.VMEM((WIDE_CHUNKS, WIDE * PAGE, LANES), jnp.float32)
RESULT = pltpu.VMEM((ROWS * QROWS, DH), jnp.float32)


def blank_page():
    return jnp.zeros((2, PAGE, DH), jnp.bfloat16)


def attend_local_kernel(idx, count, tokens, q, pool_k, pool_v, fresh, out, lse, kv, scores, sem):
    copies = [
        pltpu.make_async_copy(pool_k, kv.at[pl.ds(1, POOL), 0], sem),
        pltpu.make_async_copy(pool_v, kv.at[pl.ds(1, POOL), 1], sem),
        pltpu.make_async_copy(fresh, kv.at[pl.ds(1 + POOL, ROWS)], sem),
    ]
    for copy in copies:
        copy.start()
    kv[0] = blank_page()
    for copy in copies:
        copy.wait()
    attention(True, idx, count, tokens, q, kv, out, lse, scores)


def attend_local(lists, q, pool_k, pool_v, fresh):
    return pl.pallas_call(
        attend_local_kernel,
        out_shape=(
            jax.ShapeDtypeStruct((ROWS * QROWS, DH), jnp.float32),
            jax.ShapeDtypeStruct((TEAMS, LANES), jnp.float32),
        ),
        in_specs=[SMEM, SMEM, SMEM, VMEM, ANY, ANY, ANY],
        out_specs=(VMEM, VMEM),
        scratch_shapes=[
            pltpu.VMEM((1 + POOL + ROWS, 2, PAGE, DH), jnp.bfloat16),
            SCORES,
            pltpu.SemaphoreType.DMA,
        ],
        compiler_params=PARAMS,
        cost_estimate=pl.CostEstimate(flops=10**9, bytes_accessed=10**7, transcendentals=10**6),
        name="attend_local",
    )(*lists, q, pool_k, pool_v, fresh)


def attend_far_kernel(idx, count, tokens, q, recv, out, lse, kv, result, scores, sem):
    copy = pltpu.make_async_copy(recv, kv.at[pl.ds(1, RECV)], sem)
    copy.start()
    kv[0] = blank_page()
    copy.wait()
    attention(False, idx, count, tokens, q, kv, result, lse, scores)
    out[...] = result[...].astype(jnp.bfloat16)


def attend_far(lists, q, recv):
    return pl.pallas_call(
        attend_far_kernel,
        out_shape=(
            jax.ShapeDtypeStruct((ROWS * QROWS, DH), jnp.bfloat16),
            jax.ShapeDtypeStruct((TEAMS, LANES), jnp.float32),
        ),
        in_specs=[SMEM, SMEM, SMEM, VMEM, ANY],
        out_specs=(VMEM, VMEM),
        scratch_shapes=[
            pltpu.VMEM((1 + RECV, 2, PAGE, DH), jnp.bfloat16),
            RESULT,
            SCORES,
            pltpu.SemaphoreType.DMA,
        ],
        compiler_params=PARAMS,
        cost_estimate=pl.CostEstimate(flops=10**9, bytes_accessed=10**7, transcendentals=10**6),
        name="attend_far",
    )(*lists, q, recv)


def finish_kernel(
    idx, count, tokens, q, recv, o1, lse1, o2, lse2, weight, out,
    kv, lse3, result, scores, heads, w, terms, sem, w_sems, out_sems,
):
    copy = pltpu.make_async_copy(recv, kv.at[pl.ds(1, RECV)], sem)
    copy.start()
    tiles, _, block = terms.shape
    loads = [
        pltpu.make_async_copy(weight.at[:, pl.ds(n * block, block)], w.at[n], w_sems.at[n]) for n in range(tiles)
    ]
    for load in loads:
        load.start()
    kv[0] = blank_page()
    copy.wait()
    attention(False, idx, count, tokens, q, kv, result, lse3, scores)

    top = jnp.maximum(jnp.maximum(lse1[...], lse2[...]), lse3[...])
    parts = [jnp.exp(x[...] - top) for x in (lse1, lse2, lse3)]
    inverse = 1.0 / (parts[0] + parts[1] + parts[2])
    f1, f2, f3 = [(x * inverse).T for x in parts]
    for g in range(TEAMS):
        rows = pl.ds(g * LANES, LANES)
        merged = f1[:, g : g + 1] * o1[rows, :] + f2[:, g : g + 1] * o2[rows, :].astype(jnp.float32)
        result[rows, :] = merged + f3[:, g : g + 1] * result[rows, :]
    for j in range(QROWS):
        t, h = j // GROUPS, j % GROUPS
        column = result[pl.ds(j, ROWS, stride=QROWS), :]
        heads[pl.ds(t * ROWS, ROWS), pl.ds(h * DH, DH)] = column.astype(jnp.bfloat16)

    stores = [pltpu.make_async_copy(terms.at[n], out.at[n], out_sems.at[n]) for n in range(tiles)]
    for n in range(tiles):
        loads[n].wait()
        terms[n] = jnp.dot(heads[...], w[n], preferred_element_type=jnp.float32).astype(jnp.bfloat16)
        stores[n].start()
    for store in stores:
        store.wait()


def finish(lists, q, recv, o1, lse1, o2, lse2, weight):
    depth, width = weight.shape
    tiles = 8
    block = width // tiles
    return pl.pallas_call(
        finish_kernel,
        out_shape=jax.ShapeDtypeStruct((tiles, STEPS * ROWS, block), jnp.bfloat16),
        in_specs=[SMEM, SMEM, SMEM, VMEM, ANY, VMEM, VMEM, VMEM, VMEM, ANY],
        out_specs=ANY,
        scratch_shapes=[
            pltpu.VMEM((1 + RECV, 2, PAGE, DH), jnp.bfloat16),
            pltpu.VMEM((TEAMS, LANES), jnp.float32),
            RESULT,
            SCORES,
            pltpu.VMEM((STEPS * ROWS, depth), jnp.bfloat16),
            pltpu.VMEM((tiles, depth, block), jnp.bfloat16),
            pltpu.VMEM((tiles, STEPS * ROWS, block), jnp.bfloat16),
            pltpu.SemaphoreType.DMA,
            pltpu.SemaphoreType.DMA((tiles,)),
            pltpu.SemaphoreType.DMA((tiles,)),
        ],
        compiler_params=PARAMS,
        name="attend_merge_project",
    )(*lists, q, recv, o1, lse1, o2, lse2, weight)


def page_lists(here, place, lengths, fresh=None):
    column = jnp.arange(MAXP, dtype=jnp.int32)[None, :]
    here = here & (column * PAGE < lengths[:, None])
    kept = here.astype(jnp.int32)
    rank = jnp.cumsum(kept, axis=1) - 1
    slot = jnp.arange(MAXP, dtype=jnp.int32)[None, :, None]
    chosen = here[:, None, :] & (rank[:, None, :] == slot)
    idx = jnp.sum(jnp.where(chosen, place[:, None, :], 0), axis=2)
    count = jnp.sum(kept, axis=1)
    tokens = jnp.sum(kept * jnp.minimum(PAGE, lengths[:, None] - column * PAGE), axis=1)
    if fresh is not None:
        idx = jnp.concatenate([fresh, idx], axis=1)
        count, tokens = count + 1, tokens + PAGE
    idx = jnp.pad(idx, ((0, 0), (0, POSITIONS - idx.shape[1])))
    return idx.reshape(-1), count, tokens


def local_lists(table, lengths):
    fresh = 1 + POOL + jnp.arange(ROWS, dtype=jnp.int32)[:, None]
    return page_lists(table < POOL, 1 + table, lengths, fresh)


def arrived_lists(table, lengths, half):
    prompt = table < POOL + N_INST * PCAP
    px, mx = table - POOL, table - (POOL + N_INST * PCAP)
    source = jnp.where(prompt, px // PCAP, mx // MCAP)
    rank = jnp.where(prompt, px % PCAP, PCAP + mx % MCAP)
    group = (source >> 3) * 4 + (source & 3)
    here = (table >= POOL) & (((source >> 2) & 1) == half)
    return page_lists(here, 1 + group * SLOTS + rank, lengths)


def by_team(queries):
    return queries.transpose(1, 0, 2, 3).reshape(TEAMS, LANES, DH)


def per_device(
    queries,
    new_keys,
    new_values,
    pool_keys,
    pool_values,
    prompt_keys,
    prompt_values,
    moved_keys,
    moved_values,
    prompt_dest,
    moved_dest,
    block_table,
    context_len,
    out_weight,
):
    page = lambda x: x.reshape(x.shape[0], PAGE, DH)
    swap = [(0, 1), (1, 0)]
    half = lax.axis_index("izh")

    def exchange(send):
        send = send.reshape(N_HALF, SLOTS, 2, PAGE, DH)
        recv = lax.all_to_all(send, HALF, split_axis=0, concat_axis=0, tiled=True)
        return recv.reshape(RECV, 2, PAGE, DH)

    far_q = lax.ppermute(queries, "izh", swap)
    far_send, near_send = pack(
        half[None], prompt_dest, moved_dest,
        page(prompt_keys), page(prompt_values), page(moved_keys), page(moved_values),
    )
    far_recv = exchange(far_send)
    near_recv = exchange(near_send)

    tables = jnp.concatenate([block_table, context_len[:, None]], axis=1)
    far_tables = lax.ppermute(tables, "izh", swap)
    fresh = jnp.stack([new_keys, new_values], axis=0).reshape(2, STEPS, ROWS, DH).transpose(2, 0, 1, 3)
    fresh = jnp.pad(fresh, ((0, 0), (0, 0), (0, PAGE - STEPS), (0, 0)))
    q = by_team(queries)
    o1, lse1 = attend_local(local_lists(block_table, context_len), q, page(pool_keys), page(pool_values), fresh)

    far_lists = arrived_lists(far_tables[:, :MAXP], far_tables[:, MAXP], half)
    o2, lse2 = attend_far(far_lists, by_team(far_q), far_recv)
    o2 = lax.ppermute(o2, "izh", swap)
    lse2 = lax.ppermute(lse2, "izh", swap)

    near_lists = arrived_lists(block_table, context_len, half)
    terms = finish(near_lists, q, near_recv, o1, lse1, o2, lse2, out_weight)
    terms = terms.reshape(4, 2, STEPS * ROWS, -1)
    got = lax.all_to_all(terms, "ty", split_axis=0, concat_axis=0, tiled=True)
    column = got.astype(jnp.float32).sum(axis=0)
    side = lax.axis_index("tz")
    mine = jnp.where(side == 0, column[0], column[1])
    other = jnp.where(side == 0, column[1], column[0]).astype(jnp.bfloat16)
    other = lax.ppermute(other, "tz", swap)
    mixed = (mine + other.astype(jnp.float32)).astype(jnp.bfloat16)
    return mixed.reshape(STEPS, ROWS, -1)


def solution(mesh):
    fine = Mesh(mesh.devices.reshape(SIZES), NAMES)
    in_specs = (
        P(None, INST, TP, None),
        P(None, INST, TP, None),
        P(None, INST, TP, None),
        P(INST, TP, None, None),
        P(INST, TP, None, None),
        P(INST, TP, None, None),
        P(INST, TP, None, None),
        P(INST, TP, None, None),
        P(INST, TP, None, None),
        P(INST),
        P(INST),
        P(INST, None),
        P(INST),
        P(TP, None),
    )
    return jax.shard_map(
        per_device, mesh=fine, in_specs=in_specs, out_specs=P(None, INST, TP), check_vma=False
    )
```

time: 190 us -> 190 us (level)
  blocking collectives: 0 us -> 36.4 us
  waiting for transfers between devices: 98.9 us -> 71.1 us
  Pallas kernels: 50.3 us -> 43 us
  other arithmetic: 1.91 us -> 7.72 us
  local copies, waits for them, and re-layouts: 13.7 us -> 8.02 us
  starting transfers between devices: 24.9 us -> 22.1 us
    all_to_all x0 -> x1, blocking collectives: none -> 36.4 us  [exchange(): recv = lax.all_to_all(send, HALF, split_axis=0, concat_axis=0, tiled=True)]
    ppermute x2, waiting for transfers between devices: 59.7 us -> 25.8 us  [the longest x1 21.6 us: per_device(): far_tables = lax.ppermute(tables, 'izh', swap)]
    unnamed x30 -> x33, local copies, waits for them, and re-layouts: 11.2 us -> 1.09 us
    ppermute x1, waiting for transfers between devices: 1.55 us -> 10.8 us  [per_device(): lse2 = lax.ppermute(lse2, 'izh', swap)]
    pallas_call x4, Pallas kernels: 50.3 us -> 43 us  [the longest x1 17.2 us: finish(): pl.pallas_call(finish_kernel, out_shape=jax.ShapeDtypeStruct((tiles, STEP...]
    add x2 -> x4, other arithmetic: 0.01 us -> 3.39 us  [the longest x1 1.5 us: local_lists(): return page_lists(table < POOL, 1 + table, lengths, fresh)]
    all_to_all x1, waiting for transfers between devices: 2.98 us -> 0.01 us  [exchange(): recv = lax.all_to_all(send, HALF, split_axis=0, concat_axis=0, tiled=True)]
    ppermute x1, starting transfers between devices: 0.8 us -> 3.47 us  [per_device(): o2 = lax.ppermute(o2, 'izh', swap)]
  transfers between devices with their start and end apart: 7 -> 7, of which waited for: 6 -> 5; matrix products, arithmetic and copies ran while one was open for 2% -> 7% of each run, Pallas kernels for 11% -> 10%
where the time goes in v2:
time: 190 us; the launch traced here: 189 us
  waiting for transfers between devices  71.1 us (37%)
  Pallas kernels  43 us (23%)
  blocking collectives  36.4 us (19%)
  starting transfers between devices  22.1 us (12%)
  local copies, waits for them, and re-layouts  8.02 us (4%)
  other arithmetic  7.72 us (4%)
    all_to_all x1, blocking collectives, exchange(): recv = lax.all_to_all(send, HALF, split_axis=0, concat_axis=0, tiled=True)  36.4 us
    all_to_all x1, waiting for transfers between devices, per_device(): got = lax.all_to_all(terms, 'ty', split_axis=0, concat_axis=0, tiled=True)  24.3 us
    ppermute x1, waiting for transfers between devices, per_device(): far_tables = lax.ppermute(tables, 'izh', swap)  21.6 us
    pallas_call x1, Pallas kernels, finish(): pl.pallas_call(finish_kernel, out_shape=jax.ShapeDtypeStruct((tiles, STEP...  17.2 us
    ppermute x1, waiting for transfers between devices, per_device(): lse2 = lax.ppermute(lse2, 'izh', swap)  10.8 us
    ppermute x1, waiting for transfers between devices, per_device(): other = lax.ppermute(other, 'tz', swap)  10.1 us
    pallas_call x1, Pallas kernels, attend_local(): pl.pallas_call(attend_local_kernel, out_shape=(jax.ShapeDtypeStruct((ROWS...  10 us
    pallas_call x1, Pallas kernels, attend_far(): pl.pallas_call(attend_far_kernel, out_shape=(jax.ShapeDtypeStruct((ROWS *...  9.59 us
  transfers between devices with their start and end apart: 7, of which 5 were waited for; matrix products, arithmetic and copies ran while one was open for 7% of the time, Pallas kernels for 10%

profile of v2, /device:TPU:8, one launch (start us, length us, event | category | flops | bytes accessed | tf_op | source)
XLA Modules:
  0.0 188.5 jit_solution(14273773740133180878)
XLA Ops:
  0.0 6.1 %pack_pages.1 = (bf16[288,2,16,128]{3,2,1,0:T(8,128)(2,1)}, bf16[288,2,16,128]{3,2,1,0:T(8,128)(2,1)}) custom-call(s32[1]{0:T(128)} %bitcast.2.half, s32[192]{0:T(256)} %pdest.1, s32[96]{0:T(128)} %mdest.1, bf16[192,16,128]{2,1,0:T(8,128)(2,1)} %bitcast.41, bf16[192,16,128]{2,1,0:T(8,128)(2,1)} %bitcast.42, bf16[96,16,128]{2,1,0:T(8,128)(2,1)} %bitcast.46, ...), custom_call_target="tpu_custom_call" | custom-call | tf_op jit(solution)/shard_map/pack_pages/pallas_call | solution.py:94
  6.1 36.4 %all_to_all.15 = bf16[16,18,2,16,128]{4,3,2,1,0:T(8,128)(2,1)} all-to-all(bf16[16,18,2,16,128]{4,3,2,1,0:T(8,128)(2,1)} %bitcast.38), channel_id=1, replica_groups=mesh['ix'=4,'izh'=2,'izl'=2,'ic'=2,'ty'=4,'tz'=2] {'ix','izl','ic'}, dimensions={0} | all-to-all | bytes 4718592 | tf_op jit(solution)/shard_map/all_to_all | solution.py:395
  42.5 3.9 %all-to-all-start = ((bf16[16,18,2,16,128]{4,3,2,1,0:T(8,128)(2,1)}), bf16[16,18,2,16,128]{4,3,2,1,0:T(8,128)(2,1)S(1)}, u32[]{:S(2)}, u32[]{:S(2)}) async-start(bf16[16,18,2,16,128]{4,3,2,1,0:T(8,128)(2,1)} %bitcast.36), calls=%async_computation | async-start | bytes 4718592 | tf_op jit(solution)/shard_map/all_to_all | solution.py:395
  46.5 3.4 %collective-permute-start = (s32[64,49]{0,1:T(8,128)S(1)}, s32[64,49]{0,1:T(8,128)S(1)}, u32[]{:S(2)}, u32[]{:S(2)}) collective-permute-start(s32[64,49]{0,1:T(8,128)S(1)} %pad_add_fusion.1), channel_id=1, source_target_pairs={{0,32},{32,0},{1,33},{33,1},{2,34},{34,2},{3,35},{35,3},{4,36},{36... | collective-permute-start | bytes 37640 | tf_op jit(solution)/shard_map/ppermute | solution.py:407
  49.9 0.9 copy_bitcast_fusion
  51.5 0.9 copy.87
  52.5 0.9 pad.17.fresh
  53.3 21.6 %collective-permute-done = s32[64,49]{0,1:T(8,128)S(1)} collective-permute-done((s32[64,49]{0,1:T(8,128)S(1)}, s32[64,49]{0,1:T(8,128)S(1)}, u32[]{:S(2)}, u32[]{:S(2)}) %collective-permute-start) | collective-permute-done | bytes 12576 | tf_op jit(solution)/shard_map/ppermute | solution.py:407
  75.9 1.5 broadcast_add_fusion.3
  77.4 0.8 fusion.11
  78.3 1.0 select_reduce_fusion
  80.4 0.8 copy.88
  81.6 4.3 %collective-permute-done.1 = bf16[4,64,8,128]{3,2,1,0:T(8,128)(2,1)S(1)} collective-permute-done((bf16[4,64,8,128]{3,2,1,0:T(8,128)(2,1)S(1)}, bf16[4,64,8,128]{3,2,1,0:T(8,128)(2,1)S(1)}, u32[]{:S(2)}, u32[]{:S(2)}) %collective-permute-start.1) | collective-permute-done | bytes 524320 | tf_op jit(solution)/shard_map/ppermute | solution.py:398
  85.8 0.9 copy.96
  86.7 9.6 %attend_far.1 = (bf16[2048,128]{1,0:T(8,128)(2,1)}, f32[16,128]{1,0:T(8,128)}) custom-call(s32[4096]{0:T(1024)} %reshape.112.idx, s32[64]{0:T(128)} %get-tuple-element.42.count, s32[64]{0:T(128)} %get-tuple-element.43.tokens, bf16[16,128,128]{2,1,0:T(8,128)(2,1)} %bitcast.45, bf16[288,2,16,128]{3,2,1,0:T(8,128)(2,1)} %bitcast.37), custom_call_target="tpu_custom_call" | custom-call | flops 1000000000 | bytes 10000000 | tf_op jit(solution)/shard_map/attend_far/pallas_call | solution.py:253
  96.3 3.5 %collective-permute-start.2 = (bf16[2048,128]{1,0:T(8,128)(2,1)}, bf16[2048,128]{1,0:T(8,128)(2,1)S(1)}, u32[]{:S(2)}, u32[]{:S(2)}) collective-permute-start(bf16[2048,128]{1,0:T(8,128)(2,1)} %get-tuple-element.15), channel_id=1, source_target_pairs={{0,32},{32,0},{1,33},{33,1},{2,34},{34,2},{3,35},{35,3},{4,36},{36... | collective-permute-start | bytes 1572872 | tf_op jit(solution)/shard_map/ppermute | solution.py:415
  101.8 10.0 %attend_local.1 = (f32[2048,128]{1,0:T(8,128)}, f32[16,128]{1,0:T(8,128)}) custom-call(s32[4096]{0:T(1024)} %reshape.108.idx, s32[64]{0:T(128)} %get-tuple-element.50.count, s32[64]{0:T(128)} %get-tuple-element.49.tokens, bf16[16,128,128]{2,1,0:T(8,128)(2,1)} %bitcast.39, bf16[192,16,128]{2,1,0:T(8,128)(2,1)} %bitcast.49, bf16[192,16,128]{2,1,0:T(8,128)(2,1)} %bitcast.50, ...), custom_call_target="tpu_custom_call" | custom-call | flops 1000000000 | bytes 10000000 | tf_op jit(solution)/shard_map/attend_local/pallas_call | solution.py:224
  112.7 10.8 %collective-permute-done.3.lse2 = f32[16,128]{1,0:T(8,128)S(1)} collective-permute-done((f32[16,128]{1,0:T(8,128)}, f32[16,128]{1,0:T(8,128)S(1)}, u32[]{:S(2)}, u32[]{:S(2)}) %collective-permute-start.3) | collective-permute-done | bytes 8224 | tf_op jit(solution)/shard_map/ppermute | solution.py:416
  124.3 17.2 %attend_merge_project.1 = bf16[8,256,512]{2,1,0:T(8,128)(2,1)} custom-call(s32[4096]{0:T(1024)} %reshape.100.idx, s32[64]{0:T(128)} %get-tuple-element.39.count, s32[64]{0:T(128)} %get-tuple-element.40.tokens, bf16[16,128,128]{2,1,0:T(8,128)(2,1)} %bitcast.40, bf16[288,2,16,128]{3,2,1,0:T(8,128)(2,1)} %bitcast.34, f32[2048,128]{1,0:T(8,128)} %get-tuple-element.12.o1, ...), custom_call_target="tpu_custom_call" | custom-call | tf_op jit(solution)/shard_map/attend_merge_project/pallas_call | solution.py:315
  141.5 4.9 %all-to-all-start.2 = ((bf16[4,2,256,512]{3,2,1,0:T(8,128)(2,1)}), bf16[4,2,256,512]{3,2,1,0:T(8,128)(2,1)S(1)}, u32[]{:S(2)}, u32[]{:S(2)}) async-start(bf16[4,2,256,512]{3,2,1,0:T(8,128)(2,1)} %bitcast.35), calls=%async_computation.2 | async-start | bytes 4194304 | tf_op jit(solution)/shard_map/all_to_all | solution.py:421
  146.5 24.3 %all-to-all-done.2 = bf16[4,2,256,512]{3,2,1,0:T(8,128)(2,1)S(1)} async-done(((bf16[4,2,256,512]{3,2,1,0:T(8,128)(2,1)}), bf16[4,2,256,512]{3,2,1,0:T(8,128)(2,1)S(1)}, u32[]{:S(2)}, u32[]{:S(2)}) %all-to-all-start.2) | async-done | bytes 2097184 | tf_op jit(solution)/shard_map/all_to_all | solution.py:421
  171.1 6.4 %collective-permute-start.4 = (bf16[256,512]{1,0:T(8,128)(2,1)S(1)}, bf16[256,512]{1,0:T(8,128)(2,1)S(1)}, u32[]{:S(2)}, u32[]{:S(2)}) collective-permute-start(bf16[256,512]{1,0:T(8,128)(2,1)S(1)} %fusion.4), channel_id=1, source_target_pairs={{0,1},{1,0},{2,3},{3,2},{4,5},{5,4},{6,7},{7,6},{8,9},{9,8},{10,11... | collective-permute-start | bytes 786440 | tf_op jit(solution)/shard_map/ppermute | solution.py:426
  177.5 10.1 %collective-permute-done.4 = bf16[256,512]{1,0:T(8,128)(2,1)S(1)} collective-permute-done((bf16[256,512]{1,0:T(8,128)(2,1)S(1)}, bf16[256,512]{1,0:T(8,128)(2,1)S(1)}, u32[]{:S(2)}, u32[]{:S(2)}) %collective-permute-start.4) | collective-permute-done | bytes 262176 | tf_op jit(solution)/shard_map/ppermute | solution.py:426
  187.7 0.8 fusion.3
  (65 shorter events, 7.2 us)
Async XLA Ops:
  42.5 3.9 %copy-start.3 = (s32[64,48]{0,1:T(8,128)S(1)}, s32[64,48]{0,1:T(8,128)}, u32[]{:S(2)}) copy-start(s32[64,48]{0,1:T(8,128)} %param.25) | copy-start | bytes 36868
  42.5 3.9 %copy-start.9 = (s32[64]{0:T(128)S(1)}, s32[64]{0:T(128)}, u32[]{:S(2)}) copy-start(s32[64]{0:T(128)} %param.26) | copy-start | bytes 772
  42.5 7.3 %copy-start.1 = (bf16[4,64,8,128]{3,2,1,0:T(8,128)(2,1)S(1)}, bf16[4,64,8,128]{3,2,1,0:T(8,128)(2,1)}, u32[]{:S(2)}) copy-start(bf16[4,64,8,128]{3,2,1,0:T(8,128)(2,1)} %param.14) | copy-start | bytes 1572868
  42.5 7.4 %copy-start.5 = (bf16[4,64,1,128]{3,1,2,0:T(8,128)(2,1)S(1)}, bf16[4,64,1,128]{3,1,2,0:T(8,128)(2,1)}, u32[]{:S(2)}) copy-start(bf16[4,64,1,128]{3,1,2,0:T(8,128)(2,1)} %param.16) | copy-start | bytes 196612
  42.5 70.1 %all-to-all-start = ((bf16[16,18,2,16,128]{4,3,2,1,0:T(8,128)(2,1)}), bf16[16,18,2,16,128]{4,3,2,1,0:T(8,128)(2,1)S(1)}, u32[]{:S(2)}, u32[]{:S(2)}) async-start(bf16[16,18,2,16,128]{4,3,2,1,0:T(8,128)(2,1)} %bitcast.36), calls=%async_computation | async-start | bytes 4718592 | tf_op jit(solution)/shard_map/all_to_all | solution.py:395
  46.5 28.4 %collective-permute-start = (s32[64,49]{0,1:T(8,128)S(1)}, s32[64,49]{0,1:T(8,128)S(1)}, u32[]{:S(2)}, u32[]{:S(2)}) collective-permute-start(s32[64,49]{0,1:T(8,128)S(1)} %pad_add_fusion.1), channel_id=1, source_target_pairs={{0,32},{32,0},{1,33},{33,1},{2,34},{34,2},{3,35},{35,3},{4,36},{36... | collective-permute-start | bytes 37640 | tf_op jit(solution)/shard_map/ppermute | solution.py:407
  49.8 36.0 %collective-permute-start.1 = (bf16[4,64,8,128]{3,2,1,0:T(8,128)(2,1)S(1)}, bf16[4,64,8,128]{3,2,1,0:T(8,128)(2,1)S(1)}, u32[]{:S(2)}, u32[]{:S(2)}) collective-permute-start(bf16[4,64,8,128]{3,2,1,0:T(8,128)(2,1)S(1)} %copy-done.1), channel_id=1, source_target_pairs={{0,32},{32,0},{1,33},{33,1},{2,34},{34,2},{3,35},{35,3},{4,36},{36... | collective-permute-start | bytes 1572872 | tf_op jit(solution)/shard_map/ppermute | solution.py:398
  49.9 25.7 %copy-start.10 = (s32[48]{0:T(128)}, s32[48]{0:T(128)S(1)}, u32[]{:S(2)}) copy-start(s32[48]{0:T(128)S(1)} %iota_multiply_fusion) | copy-start | bytes 580
  74.9 0.7 copy-start.4
  74.9 1.1 copy-start.11
  75.6 4.8 %copy-start.6 = (pred[64,48]{0,1:T(8,128)(4,1)}, pred[64,48]{0,1:T(8,128)(4,1)S(1)}, u32[]{:S(2)}) copy-start(pred[64,48]{0,1:T(8,128)(4,1)S(1)} %get-tuple-element.33) | copy-start | bytes 9220
  86.7 13.1 %copy-start.7 = (pred[64,48]{0,1:T(8,128)(4,1)S(1)}, pred[64,48]{0,1:T(8,128)(4,1)}, u32[]{:S(2)}) copy-start(pred[64,48]{0,1:T(8,128)(4,1)} %copy-done.6) | copy-start | bytes 9220
  86.7 13.8 %copy-start.14 = (s32[64,1]{0,1:T(1,128)S(1)}, s32[64,1]{0,1:T(1,128)}, u32[]{:S(2)}) copy-start(s32[64,1]{0,1:T(1,128)} %iota_add_fusion) | copy-start | bytes 772
  86.7 14.6 %copy-start.12 = (s32[64]{0:T(128)S(1)}, s32[64]{0:T(128)}, u32[]{:S(2)}) copy-start(s32[64]{0:T(128)} %get-tuple-element.37) | copy-start | bytes 772
  86.7 14.6 %copy-start.13 = (s32[64]{0:T(128)S(1)}, s32[64]{0:T(128)}, u32[]{:S(2)}) copy-start(s32[64]{0:T(128)} %get-tuple-element.38) | copy-start | bytes 772
  96.3 27.2 %collective-permute-start.2 = (bf16[2048,128]{1,0:T(8,128)(2,1)}, bf16[2048,128]{1,0:T(8,128)(2,1)S(1)}, u32[]{:S(2)}, u32[]{:S(2)}) collective-permute-start(bf16[2048,128]{1,0:T(8,128)(2,1)} %get-tuple-element.15), channel_id=1, source_target_pairs={{0,32},{32,0},{1,33},{33,1},{2,34},{34,2},{3,35},{35,3},{4,36},{36... | collective-permute-start | bytes 1572872 | tf_op jit(solution)/shard_map/ppermute | solution.py:415
  101.8 21.7 %collective-permute-start.3 = (f32[16,128]{1,0:T(8,128)}, f32[16,128]{1,0:T(8,128)S(1)}, u32[]{:S(2)}, u32[]{:S(2)}) collective-permute-start(f32[16,128]{1,0:T(8,128)} %get-tuple-element.16), channel_id=1, source_target_pairs={{0,32},{32,0},{1,33},{33,1},{2,34},{34,2},{3,35},{35,3},{4,36},{36... | collective-permute-start | bytes 24584 | tf_op jit(solution)/shard_map/ppermute | solution.py:416
  112.7 10.8 %copy-start = (bf16[16,18,2,16,128]{4,3,2,1,0:T(8,128)(2,1)}, bf16[16,18,2,16,128]{4,3,2,1,0:T(8,128)(2,1)S(1)}, u32[]{:S(2)}) copy-start(bf16[16,18,2,16,128]{4,3,2,1,0:T(8,128)(2,1)S(1)} %all-to-all-done) | copy-start | bytes 7077892
  123.5 0.6 copy-start.8
  123.5 0.8 copy-start.2
  141.5 29.2 %all-to-all-start.2 = ((bf16[4,2,256,512]{3,2,1,0:T(8,128)(2,1)}), bf16[4,2,256,512]{3,2,1,0:T(8,128)(2,1)S(1)}, u32[]{:S(2)}, u32[]{:S(2)}) async-start(bf16[4,2,256,512]{3,2,1,0:T(8,128)(2,1)} %bitcast.35), calls=%async_computation.2 | async-start | bytes 4194304 | tf_op jit(solution)/shard_map/all_to_all | solution.py:421
  171.1 16.5 %collective-permute-start.4 = (bf16[256,512]{1,0:T(8,128)(2,1)S(1)}, bf16[256,512]{1,0:T(8,128)(2,1)S(1)}, u32[]{:S(2)}, u32[]{:S(2)}) collective-permute-start(bf16[256,512]{1,0:T(8,128)(2,1)S(1)} %fusion.4), channel_id=1, source_target_pairs={{0,1},{1,0},{2,3},{3,2},{4,5},{5,4},{6,7},{7,6},{8,9},{9,8},{10,11... | collective-permute-start | bytes 786440 | tf_op jit(solution)/shard_map/ppermute | solution.py:426

commit v3 on v2

--- a/solution.py
+++ b/solution.py
@@ -31,7 +31,7 @@
 TEAMS = ROWS // TEAM
 LANES = TEAM * QROWS
 SCALE = DH ** -0.5
-VMEM_LIMIT = 60 * 1024 * 1024
+VMEM_LIMIT = 63 * 1024 * 1024
 
 SMEM = pl.BlockSpec(memory_space=pltpu.SMEM)
 VMEM = pl.BlockSpec(memory_space=pltpu.VMEM)
@@ -39,7 +39,8 @@
 PARAMS = pltpu.CompilerParams(vmem_limit_bytes=VMEM_LIMIT)
 
 
-def pack_kernel(half, pdest, mdest, pk, pv, mk, mv, far, near, pages, send, count, sems, out_sems):
+def pack_kernel(half, pdest, mdest, pk, pv, mk, mv, *refs):
+    out, pages, send, count, sems, out_sem = refs[-6:]
     loads = [
         pltpu.make_async_copy(pk, pages.at[pl.ds(0, OUT), 0], sems.at[0]),
         pltpu.make_async_copy(pv, pages.at[pl.ds(0, OUT), 1], sems.at[1]),
@@ -48,7 +49,7 @@
     ]
     for load in loads:
         load.start()
-    mine = half[0]
+    wanted = half[0]
 
     def clear(i, carry):
         count[i] = 0
@@ -59,8 +60,7 @@
         k = count[d]
         count[d] = k + 1
         group = (d >> 3) * 4 + (d & 3)
-        here = jnp.where(((d >> 2) & 1) == mine, RECV, 0)
-        slot = here + group * SLOTS + first + k
+        slot = jnp.where(((d >> 2) & 1) == wanted, group * SLOTS + first + k, RECV)
         send[slot] = pages[origin + j]
 
     def prompt(j, carry):
@@ -79,42 +79,58 @@
     loads[2].wait()
     loads[3].wait()
     lax.fori_loop(0, MIG, moved, 0, unroll=4)
-    stores = [
-        pltpu.make_async_copy(send.at[pl.ds(0, RECV)], far, out_sems.at[0]),
-        pltpu.make_async_copy(send.at[pl.ds(RECV, RECV)], near, out_sems.at[1]),
-    ]
-    for store in stores:
-        store.start()
-    for store in stores:
-        store.wait()
-
-
-def pack(half, pdest, mdest, pk, pv, mk, mv):
-    shape = jax.ShapeDtypeStruct((RECV, 2, PAGE, DH), jnp.bfloat16)
+    store = pltpu.make_async_copy(send.at[pl.ds(0, RECV)], out, out_sem)
+    store.start()
+    store.wait()
+
+
+def pack(half, pdest, mdest, pk, pv, mk, mv, *after):
     return pl.pallas_call(
         pack_kernel,
-        out_shape=(shape, shape),
-        in_specs=[SMEM, SMEM, SMEM, ANY, ANY, ANY, ANY],
-        out_specs=(ANY, ANY),
+        out_shape=jax.ShapeDtypeStruct((RECV, 2, PAGE, DH), jnp.bfloat16),
+        in_specs=[SMEM, SMEM, SMEM] + [ANY] * (4 + len(after)),
+        out_specs=ANY,
         scratch_shapes=[
             pltpu.VMEM((OUT + MIG, 2, PAGE, DH), jnp.bfloat16),
-            pltpu.VMEM((2 * RECV, 2, PAGE, DH), jnp.bfloat16),
+            pltpu.VMEM((RECV + 1, 2, PAGE, DH), jnp.bfloat16),
             pltpu.SMEM((N_INST,), jnp.int32),
             pltpu.SemaphoreType.DMA((4,)),
-            pltpu.SemaphoreType.DMA((2,)),
+            pltpu.SemaphoreType.DMA,
         ],
         compiler_params=PARAMS,
+        cost_estimate=pl.CostEstimate(flops=10**6, bytes_accessed=10**7, transcendentals=0),
         name="pack_pages",
-    )(half, pdest, mdest, pk, pv, mk, mv)
-
-
-def attention(fresh, idx, count, tokens, q, kv, out, lse, scores):
+    )(half, pdest, mdest, pk, pv, mk, mv, *after)
+
+
+def gate_kernel(x, *refs):
+    pass
+
+
+def gate(x, *after):
+    return pl.pallas_call(
+        gate_kernel,
+        out_shape=jax.ShapeDtypeStruct(x.shape, x.dtype),
+        in_specs=[ANY] * (1 + len(after)),
+        out_specs=ANY,
+        input_output_aliases={0: 0},
+        name="gate",
+    )(x, *after)
+
+
+def attention(fresh, lists, q, kv, out, lse, scores):
     lane = lax.broadcasted_iota(jnp.int32, (1, LANES), 1)
     team_row = lane // QROWS
     step = (lane % QROWS) // GROUPS
 
     def load(r, first, n, which):
-        return [kv[idx[r * POSITIONS + first + p], which] for p in range(n)]
+        return [kv[lists[r * POSITIONS + first + p], which] for p in range(n)]
+
+    def count(r):
+        return lists[ROWS * POSITIONS + r]
+
+    def tokens(r):
+        return lists[ROWS * POSITIONS + ROWS + r]
 
     def mask(s, first, limit):
         token = lax.broadcasted_iota(jnp.int32, s.shape, 0) + first
@@ -132,11 +148,11 @@
         keys = jnp.concatenate([k for r in rows for k in load(r, 0, NARROW, 0)], axis=0)
         s_all = dot_nt(keys, q[g])
         s = s_all[:width]
-        limit = jnp.full((1, LANES), tokens[rows[0]], jnp.int32)
+        limit = jnp.full((1, LANES), tokens(rows[0]), jnp.int32)
         owner = lax.broadcasted_iota(jnp.int32, (width, LANES), 1) // QROWS
         for i in range(1, TEAM):
             s = jnp.where(owner == i, s_all[i * width : (i + 1) * width], s)
-            limit = jnp.where(team_row == i, tokens[rows[i]], limit)
+            limit = jnp.where(team_row == i, tokens(rows[i]), limit)
         s = mask(s, 0, limit)
         m = jnp.maximum(jnp.max(s, axis=0, keepdims=True), -1e30)
         e = jnp.exp(s - m)
@@ -159,12 +175,12 @@
 
     def wide(r):
         width = WIDE * PAGE
-        chunks = (count[r] + WIDE - 1) // WIDE
+        chunks = (count(r) + WIDE - 1) // WIDE
         g, i = r // TEAM, r % TEAM
 
         def first_pass(c, m):
             keys = jnp.concatenate(load(r, c * WIDE, WIDE, 0), axis=0)
-            s = mask(dot_nt(keys, q[g]), c * width, tokens[r])
+            s = mask(dot_nt(keys, q[g]), c * width, tokens(r))
             scores[c] = s
             return jnp.maximum(m, jnp.max(s, axis=0, keepdims=True))
 
@@ -192,7 +208,7 @@
         lse[pl.ds(g, 1), :] = jnp.where(team_row == i, new, lse[pl.ds(g, 1), :])
 
     def wide_body(r, carry):
-        pl.when(count[r] > NARROW)(lambda: wide(r))
+        pl.when(count(r) > NARROW)(lambda: wide(r))
         return carry
 
     lax.fori_loop(0, ROWS, wide_body, 0)
@@ -206,7 +222,7 @@
     return jnp.zeros((2, PAGE, DH), jnp.bfloat16)
 
 
-def attend_local_kernel(idx, count, tokens, q, pool_k, pool_v, fresh, out, lse, kv, scores, sem):
+def attend_local_kernel(lists, q, pool_k, pool_v, fresh, out, lse, kv, scores, sem):
     copies = [
         pltpu.make_async_copy(pool_k, kv.at[pl.ds(1, POOL), 0], sem),
         pltpu.make_async_copy(pool_v, kv.at[pl.ds(1, POOL), 1], sem),
@@ -217,7 +233,7 @@
     kv[0] = blank_page()
     for copy in copies:
         copy.wait()
-    attention(True, idx, count, tokens, q, kv, out, lse, scores)
+    attention(True, lists, q, kv, out, lse, scores)
 
 
 def attend_local(lists, q, pool_k, pool_v, fresh):
@@ -227,7 +243,7 @@
             jax.ShapeDtypeStruct((ROWS * QROWS, DH), jnp.float32),
             jax.ShapeDtypeStruct((TEAMS, LANES), jnp.float32),
         ),
-        in_specs=[SMEM, SMEM, SMEM, VMEM, ANY, ANY, ANY],
+        in_specs=[SMEM, VMEM, ANY, ANY, ANY],
         out_specs=(VMEM, VMEM),
         scratch_shapes=[
             pltpu.VMEM((1 + POOL + ROWS, 2, PAGE, DH), jnp.bfloat16),
@@ -237,15 +253,15 @@
         compiler_params=PARAMS,
         cost_estimate=pl.CostEstimate(flops=10**9, bytes_accessed=10**7, transcendentals=10**6),
         name="attend_local",
-    )(*lists, q, pool_k, pool_v, fresh)
-
-
-def attend_far_kernel(idx, count, tokens, q, recv, out, lse, kv, result, scores, sem):
+    )(lists, q, pool_k, pool_v, fresh)
+
+
+def attend_far_kernel(lists, q, recv, out, lse, kv, result, scores, sem):
     copy = pltpu.make_async_copy(recv, kv.at[pl.ds(1, RECV)], sem)
     copy.start()
     kv[0] = blank_page()
     copy.wait()
-    attention(False, idx, count, tokens, q, kv, result, lse, scores)
+    attention(False, lists, q, kv, result, lse, scores)
     out[...] = result[...].astype(jnp.bfloat16)
 
 
@@ -256,7 +272,7 @@
             jax.ShapeDtypeStruct((ROWS * QROWS, DH), jnp.bfloat16),
             jax.ShapeDtypeStruct((TEAMS, LANES), jnp.float32),
         ),
-        in_specs=[SMEM, SMEM, SMEM, VMEM, ANY],
+        in_specs=[SMEM, VMEM, ANY],
         out_specs=(VMEM, VMEM),
         scratch_shapes=[
             pltpu.VMEM((1 + RECV, 2, PAGE, DH), jnp.bfloat16),
@@ -267,24 +283,59 @@
         compiler_params=PARAMS,
         cost_estimate=pl.CostEstimate(flops=10**9, bytes_accessed=10**7, transcendentals=10**6),
         name="attend_far",
-    )(*lists, q, recv)
-
-
-def finish_kernel(
-    idx, count, tokens, q, recv, o1, lse1, o2, lse2, weight, out,
-    kv, lse3, result, scores, heads, w, terms, sem, w_sems, out_sems,
-):
-    copy = pltpu.make_async_copy(recv, kv.at[pl.ds(1, RECV)], sem)
-    copy.start()
-    tiles, _, block = terms.shape
+    )(lists, q, recv)
+
+
+SHIFTS = (2, 1, 3, 0)
+BLOCK = 512
+
+
+def column_tile(place, side, shift, weight):
+    y = lax.rem(place[0] + shift, 4)
+    z = place[1] if side == 0 else 1 - place[1]
+    return weight.at[:, pl.ds(pl.multiple_of((y * 2 + z) * BLOCK, BLOCK), BLOCK)]
+
+
+def start_tiles(place, side, weight, w, w_sems):
     loads = [
-        pltpu.make_async_copy(weight.at[:, pl.ds(n * block, block)], w.at[n], w_sems.at[n]) for n in range(tiles)
+        pltpu.make_async_copy(column_tile(place, side, shift, weight), w.at[n], w_sems.at[n])
+        for n, shift in enumerate(SHIFTS)
     ]
     for load in loads:
         load.start()
+    return loads
+
+
+def project(loads, heads, w, outs, terms, out_sems):
+    stores = []
+    for n, load in enumerate(loads):
+        load.wait()
+        terms[n] = jnp.dot(heads[...], w[n], preferred_element_type=jnp.float32).astype(jnp.bfloat16)
+        store = pltpu.make_async_copy(terms.at[n], outs[n], out_sems.at[n])
+        store.start()
+        stores.append(store)
+    for store in stores:
+        store.wait()
+
+
+TILES = len(SHIFTS)
+TERMS = (jax.ShapeDtypeStruct((STEPS * ROWS, BLOCK), jnp.bfloat16),) * TILES
+PROJECT_SCRATCH = [
+    pltpu.VMEM((TILES, GROUPS * DH, BLOCK), jnp.bfloat16),
+    pltpu.VMEM((TILES, STEPS * ROWS, BLOCK), jnp.bfloat16),
+    pltpu.SemaphoreType.DMA((TILES,)),
+    pltpu.SemaphoreType.DMA((TILES,)),
+]
+
+
+def finish_kernel(place, lists, q, recv, o1, lse1, o2, lse2, weight, heads, *refs):
+    outs, (kv, lse3, result, scores, sem, w, terms, w_sems, out_sems) = refs[:TILES], refs[TILES:]
+    copy = pltpu.make_async_copy(recv, kv.at[pl.ds(1, RECV)], sem)
+    copy.start()
+    loads = start_tiles(place, 1, weight, w, w_sems)
     kv[0] = blank_page()
     copy.wait()
-    attention(False, idx, count, tokens, q, kv, result, lse3, scores)
+    attention(False, lists, q, kv, result, lse3, scores)
 
     top = jnp.maximum(jnp.maximum(lse1[...], lse2[...]), lse3[...])
     parts = [jnp.exp(x[...] - top) for x in (lse1, lse2, lse3)]
@@ -298,40 +349,54 @@
         t, h = j // GROUPS, j % GROUPS
         column = result[pl.ds(j, ROWS, stride=QROWS), :]
         heads[pl.ds(t * ROWS, ROWS), pl.ds(h * DH, DH)] = column.astype(jnp.bfloat16)
-
-    stores = [pltpu.make_async_copy(terms.at[n], out.at[n], out_sems.at[n]) for n in range(tiles)]
-    for n in range(tiles):
-        loads[n].wait()
-        terms[n] = jnp.dot(heads[...], w[n], preferred_element_type=jnp.float32).astype(jnp.bfloat16)
-        stores[n].start()
-    for store in stores:
-        store.wait()
-
-
-def finish(lists, q, recv, o1, lse1, o2, lse2, weight):
-    depth, width = weight.shape
-    tiles = 8
-    block = width // tiles
-    return pl.pallas_call(
+    project(loads, heads, w, outs, terms, out_sems)
+
+
+def finish(place, lists, q, recv, o1, lse1, o2, lse2, weight):
+    heads = jax.ShapeDtypeStruct((STEPS * ROWS, GROUPS * DH), jnp.bfloat16)
+    heads, *terms = pl.pallas_call(
         finish_kernel,
-        out_shape=jax.ShapeDtypeStruct((tiles, STEPS * ROWS, block), jnp.bfloat16),
-        in_specs=[SMEM, SMEM, SMEM, VMEM, ANY, VMEM, VMEM, VMEM, VMEM, ANY],
-        out_specs=ANY,
+        out_shape=(heads,) + TERMS,
+        in_specs=[SMEM, SMEM, VMEM, ANY, VMEM, VMEM, VMEM, VMEM, ANY],
+        out_specs=(VMEM,) + (ANY,) * TILES,
         scratch_shapes=[
             pltpu.VMEM((1 + RECV, 2, PAGE, DH), jnp.bfloat16),
             pltpu.VMEM((TEAMS, LANES), jnp.float32),
             RESULT,
             SCORES,
-            pltpu.VMEM((STEPS * ROWS, depth), jnp.bfloat16),
-            pltpu.VMEM((tiles, depth, block), jnp.bfloat16),
-            pltpu.VMEM((tiles, STEPS * ROWS, block), jnp.bfloat16),
             pltpu.SemaphoreType.DMA,
-            pltpu.SemaphoreType.DMA((tiles,)),
-            pltpu.SemaphoreType.DMA((tiles,)),
-        ],
+        ] + PROJECT_SCRATCH,
         compiler_params=PARAMS,
         name="attend_merge_project",
-    )(*lists, q, recv, o1, lse1, o2, lse2, weight)
+    )(place, lists, q, recv, o1, lse1, o2, lse2, weight)
+    return heads, terms
+
+
+def project_kernel(place, heads, weight, *refs):
+    outs, (w, terms, w_sems, out_sems) = refs[:TILES], refs[TILES:]
+    project(start_tiles(place, 0, weight, w, w_sems), heads, w, outs, terms, out_sems)
+
+
+def project_mine(place, heads, weight):
+    return pl.pallas_call(
+        project_kernel,
+        out_shape=TERMS,
+        in_specs=[SMEM, VMEM, ANY],
+        out_specs=(ANY,) * TILES,
+        scratch_shapes=PROJECT_SCRATCH,
+        compiler_params=PARAMS,
+        cost_estimate=pl.CostEstimate(flops=10**9, bytes_accessed=6 * 10**6, transcendentals=0),
+        name="project_mine",
+    )(place, heads, weight)
+
+
+def sum_over_y(terms):
+    total = terms[SHIFTS.index(0)].astype(jnp.float32)
+    for term, shift in zip(terms, SHIFTS):
+        if shift:
+            moved = lax.ppermute(term, "ty", [(i, (i + shift) % 4) for i in range(4)])
+            total = total + moved.astype(jnp.float32)
+    return total
 
 
 def page_lists(here, place, lengths, fresh=None):
@@ -348,7 +413,7 @@
         idx = jnp.concatenate([fresh, idx], axis=1)
         count, tokens = count + 1, tokens + PAGE
     idx = jnp.pad(idx, ((0, 0), (0, POSITIONS - idx.shape[1])))
-    return idx.reshape(-1), count, tokens
+    return jnp.concatenate([idx.reshape(-1), count, tokens])
 
 
 def local_lists(table, lengths):
@@ -395,37 +460,28 @@
         recv = lax.all_to_all(send, HALF, split_axis=0, concat_axis=0, tiled=True)
         return recv.reshape(RECV, 2, PAGE, DH)
 
-    far_q = lax.ppermute(queries, "izh", swap)
-    far_send, near_send = pack(
-        half[None], prompt_dest, moved_dest,
-        page(prompt_keys), page(prompt_values), page(moved_keys), page(moved_values),
-    )
-    far_recv = exchange(far_send)
-    near_recv = exchange(near_send)
-
-    tables = jnp.concatenate([block_table, context_len[:, None]], axis=1)
-    far_tables = lax.ppermute(tables, "izh", swap)
+    pages = (page(prompt_keys), page(prompt_values), page(moved_keys), page(moved_values))
+    far_recv = exchange(pack((1 - half)[None], prompt_dest, moved_dest, *pages))
+    far_q = by_team(lax.ppermute(queries, "izh", swap))
+    far_lists = lax.ppermute(arrived_lists(block_table, context_len, 1 - half), "izh", swap)
+    near_lists = arrived_lists(block_table, context_len, half)
+
     fresh = jnp.stack([new_keys, new_values], axis=0).reshape(2, STEPS, ROWS, DH).transpose(2, 0, 1, 3)
     fresh = jnp.pad(fresh, ((0, 0), (0, 0), (0, PAGE - STEPS), (0, 0)))
     q = by_team(queries)
     o1, lse1 = attend_local(local_lists(block_table, context_len), q, page(pool_keys), page(pool_values), fresh)
-
-    far_lists = arrived_lists(far_tables[:, :MAXP], far_tables[:, MAXP], half)
-    o2, lse2 = attend_far(far_lists, by_team(far_q), far_recv)
+    near_send = pack(half[None], prompt_dest, moved_dest, *pages, lse1)
+    near_recv = exchange(gate(near_send, far_q, far_lists, near_lists))
+
+    o2, lse2 = attend_far(far_lists, far_q, far_recv)
     o2 = lax.ppermute(o2, "izh", swap)
     lse2 = lax.ppermute(lse2, "izh", swap)
 
-    near_lists = arrived_lists(block_table, context_len, half)
-    terms = finish(near_lists, q, near_recv, o1, lse1, o2, lse2, out_weight)
-    terms = terms.reshape(4, 2, STEPS * ROWS, -1)
-    got = lax.all_to_all(terms, "ty", split_axis=0, concat_axis=0, tiled=True)
-    column = got.astype(jnp.float32).sum(axis=0)
-    side = lax.axis_index("tz")
-    mine = jnp.where(side == 0, column[0], column[1])
-    other = jnp.where(side == 0, column[1], column[0]).astype(jnp.bfloat16)
-    other = lax.ppermute(other, "tz", swap)
-    mixed = (mine + other.astype(jnp.float32)).astype(jnp.bfloat16)
-    return mixed.reshape(STEPS, ROWS, -1)
+    place = jnp.stack([lax.axis_index("ty"), lax.axis_index("tz")]).astype(jnp.int32)
+    heads, terms = finish(place, near_lists, q, near_recv, o1, lse1, o2, lse2, out_weight)
+    other = lax.ppermute(sum_over_y(terms).astype(jnp.bfloat16), "tz", swap)
+    mine = sum_over_y(project_mine(place, heads, out_weight))
+    return (mine + other.astype(jnp.float32)).astype(jnp.bfloat16).reshape(STEPS, ROWS, -1)
 
 
 def solution(mesh):

time: 190 us -> 156 us (0.82)
  blocking collectives: 36.4 us -> 0 us
  starting transfers between devices: 22.1 us -> 33.6 us
  waiting for transfers between devices: 71.1 us -> 59.8 us
  Pallas kernels: 43 us -> 49.5 us
  other arithmetic: 7.72 us -> 4.64 us
    all_to_all x1 -> x0, blocking collectives: 36.4 us -> none  [exchange(): recv = lax.all_to_all(send, HALF, split_axis=0, concat_axis=0, tiled=True)]
    all_to_all x1 -> x0, waiting for transfers between devices: 24.3 us -> none  [per_device(): got = lax.all_to_all(terms, 'ty', split_axis=0, concat_axis=0, tiled=True)]
    ppermute x1, waiting for transfers between devices: 10.8 us -> 25.8 us  [per_device(): lse2 = lax.ppermute(lse2, 'izh', swap)]
    all_to_all x1 -> x2, starting transfers between devices: 3.87 us -> 14.1 us  [exchange(): recv = lax.all_to_all(send, HALF, split_axis=0, concat_axis=0, tiled=True)]
    ppermute x3 -> x9, starting transfers between devices: 9.86 us -> 16.5 us  [the longest x6 8.52 us: sum_over_y(): moved = lax.ppermute(term, 'ty', [(i, (i + shift) % 4) for i in range(4)])]
    pallas_call x2 -> x5, Pallas kernels: 23.3 us -> 29.8 us  [the longest x1 14.3 us: finish(): pl.pallas_call(finish_kernel, out_shape=(heads,) + TERMS, in_specs=[SMEM,...]
    ppermute x3 -> x9, waiting for transfers between devices: 35.9 us -> 30.5 us  [the longest x1 14 us: per_device(): far_q = by_team(lax.ppermute(queries, 'izh', swap))]
    all_to_all x1 -> x0, starting transfers between devices: 4.92 us -> none  [per_device(): got = lax.all_to_all(terms, 'ty', split_axis=0, concat_axis=0, tiled=True)]
  transfers between devices with their start and end apart: 7 -> 13, of which waited for: 5 -> 8; matrix products, arithmetic and copies ran while one was open for 7% -> 6% of each run, Pallas kernels for 10% -> 19%
where the time goes in v3:
time: 156 us; the launch traced here: 155 us
  waiting for transfers between devices  59.8 us (38%)
  Pallas kernels  49.5 us (32%)
  starting transfers between devices  33.6 us (22%)
  local copies, waits for them, and re-layouts  7.7 us (5%)
  other arithmetic  4.64 us (3%)
    ppermute x1, waiting for transfers between devices, per_device(): lse2 = lax.ppermute(lse2, 'izh', swap)  25.8 us
    pallas_call x1, Pallas kernels, finish(): pl.pallas_call(finish_kernel, out_shape=(heads,) + TERMS, in_specs=[SMEM,...  14.3 us
    all_to_all x2, starting transfers between devices, exchange(): recv = lax.all_to_all(send, HALF, split_axis=0, concat_axis=0, tiled=True)  14.1 us
    ppermute x1, waiting for transfers between devices, per_device(): far_q = by_team(lax.ppermute(queries, 'izh', swap))  14 us
    pallas_call x2, Pallas kernels, pack(): pl.pallas_call(pack_kernel, out_shape=jax.ShapeDtypeStruct((RECV, 2, PAGE...  10.6 us
    pallas_call x1, Pallas kernels, attend_local(): pl.pallas_call(attend_local_kernel, out_shape=(jax.ShapeDtypeStruct((ROWS...  10.1 us
    pallas_call x1, Pallas kernels, attend_far(): pl.pallas_call(attend_far_kernel, out_shape=(jax.ShapeDtypeStruct((ROWS *...  9.63 us
    ppermute x1, waiting for transfers between devices, per_device(): other = lax.ppermute(sum_over_y(terms).astype(jnp.bfloat16), 'tz', swap)  8.87 us
  transfers between devices with their start and end apart: 13, of which 8 were waited for; matrix products, arithmetic and copies ran while one was open for 6% of the time, Pallas kernels for 19%

profile of v3, /device:TPU:8, one launch (start us, length us, event | category | flops | bytes accessed | tf_op | source)
XLA Modules:
  0.0 155.5 jit_solution(12284929867842029260)
XLA Ops:
  0.0 5.3 %pack_pages.3 = bf16[288,2,16,128]{3,2,1,0:T(8,128)(2,1)} custom-call(s32[1]{0:T(128)} %bitcast.19.half, s32[192]{0:T(256)} %pdest.3, s32[96]{0:T(128)} %mdest.3, bf16[192,16,128]{2,1,0:T(8,128)(2,1)} %bitcast.29, bf16[192,16,128]{2,1,0:T(8,128)(2,1)} %bitcast.31, bf16[96,16,128]{2,1,0:T(8,128)(2,1)} %bitcast.37, bf16[96,16,128]{2,1,0:T(8,128)(2,1)} %bitcast.39), custom_call_target="tpu_custom_call" | custom-call | flops 1000000 | bytes 10000000 | tf_op jit(solution)/shard_map/pack_pages/pallas_call | solution.py:88
  5.3 5.8 %all-to-all-start.1 = ((bf16[16,18,2,16,128]{4,3,2,1,0:T(8,128)(2,1)}), bf16[16,18,2,16,128]{4,3,2,1,0:T(8,128)(2,1)}, u32[]{:S(2)}, u32[]{:S(2)}) async-start(bf16[16,18,2,16,128]{4,3,2,1,0:T(8,128)(2,1)} %bitcast.28), calls=%async_computation.1 | async-start | bytes 4718592 | tf_op jit(solution)/shard_map/all_to_all | solution.py:460
  12.6 1.0 select_reduce_fusion
  13.9 3.3 %collective-permute-start.1 = (s32[4224]{0:T(1024)S(1)}, s32[4224]{0:T(1024)S(1)}, u32[]{:S(2)}, u32[]{:S(2)}) collective-permute-start(s32[4224]{0:T(1024)S(1)} %concatenate.15), channel_id=1, source_target_pairs={{0,32},{32,0},{1,33},{33,1},{2,34},{34,2},{3,35},{35,3},{4,36},{36... | collective-permute-start | bytes 50696 | tf_op jit(solution)/shard_map/ppermute | solution.py:466
  20.2 10.1 %attend_local.1 = (f32[2048,128]{1,0:T(8,128)}, f32[16,128]{1,0:T(8,128)}) custom-call(s32[4224]{0:T(1024)} %concatenate.14.lists, bf16[16,128,128]{2,1,0:T(8,128)(2,1)} %bitcast.33, bf16[192,16,128]{2,1,0:T(8,128)(2,1)} %bitcast.42, bf16[192,16,128]{2,1,0:T(8,128)(2,1)} %bitcast.43, bf16[64,2,16,128]{3,2,1,0:T(8,128)(2,1)} %pad.17.fresh), custom_call_target="tpu_custom_call" | custom-call | flops 1000000000 | bytes 10000000 | tf_op jit(solution)/shard_map/attend_local/pallas_call | solution.py:240
  31.2 5.3 %pack_pages.2.x = bf16[288,2,16,128]{3,2,1,0:T(8,128)(2,1)} custom-call(s32[1]{0:T(128)} %bitcast.4.half, s32[192]{0:T(256)} %pdest.3, s32[96]{0:T(128)} %mdest.3, bf16[192,16,128]{2,1,0:T(8,128)(2,1)} %bitcast.30, bf16[192,16,128]{2,1,0:T(8,128)(2,1)} %bitcast.32, bf16[96,16,128]{2,1,0:T(8,128)(2,1)} %bitcast.38, bf16[96,16,128]{2,1,0:T(8,128)(2,1)} %bitcast.40, ...), custom_call_target="tpu_custom_call" | custom-call | flops 1000000 | bytes 10000000 | tf_op jit(solution)/shard_map/pack_pages/pallas_call | solution.py:88
  36.5 14.0 %collective-permute-done = bf16[4,64,8,128]{3,2,1,0:T(8,128)(2,1)} collective-permute-done((bf16[4,64,8,128]{3,2,1,0:T(8,128)(2,1)S(1)}, bf16[4,64,8,128]{3,2,1,0:T(8,128)(2,1)}, u32[]{:S(2)}, u32[]{:S(2)}) %collective-permute-start) | collective-permute-done | bytes 524320 | tf_op jit(solution)/shard_map/ppermute | solution.py:465
  50.5 1.9 %copy.74 = bf16[64,4,8,128]{3,2,1,0:T(8,128)(2,1)} copy(bf16[64,4,8,128]{3,2,0,1:T(8,128)(2,1)} %bitcast.15) | data formatting | bytes 1048576 | tf_op jit(solution)/shard_map/transpose | solution.py:435
  53.5 8.3 %all-to-all-start = ((bf16[16,18,2,16,128]{4,3,2,1,0:T(8,128)(2,1)}), bf16[16,18,2,16,128]{4,3,2,1,0:T(8,128)(2,1)}, u32[]{:S(2)}, u32[]{:S(2)}) async-start(bf16[16,18,2,16,128]{4,3,2,1,0:T(8,128)(2,1)} %bitcast.27), calls=%async_computation | async-start | bytes 4718592 | tf_op jit(solution)/shard_map/all_to_all | solution.py:460
  61.8 9.6 %attend_far.1 = (bf16[2048,128]{1,0:T(8,128)(2,1)}, f32[16,128]{1,0:T(8,128)}) custom-call(s32[4224]{0:T(1024)} %copy-done.7, bf16[16,128,128]{2,1,0:T(8,128)(2,1)} %bitcast.36, bf16[288,2,16,128]{3,2,1,0:T(8,128)(2,1)} %bitcast.21.recv), custom_call_target="tpu_custom_call" | custom-call | flops 1000000000 | bytes 10000000 | tf_op jit(solution)/shard_map/attend_far/pallas_call | solution.py:269
  71.5 2.9 %collective-permute-start.3 = (f32[16,128]{1,0:T(8,128)}, f32[16,128]{1,0:T(8,128)S(1)}, u32[]{:S(2)}, u32[]{:S(2)}) collective-permute-start(f32[16,128]{1,0:T(8,128)} %get-tuple-element.21), channel_id=1, source_target_pairs={{0,32},{32,0},{1,33},{33,1},{2,34},{34,2},{3,35},{35,3},{4,36},{36... | collective-permute-start | bytes 24584 | tf_op jit(solution)/shard_map/ppermute | solution.py:478
  75.1 25.8 %collective-permute-done.3.lse2 = f32[16,128]{1,0:T(8,128)S(1)} collective-permute-done((f32[16,128]{1,0:T(8,128)}, f32[16,128]{1,0:T(8,128)S(1)}, u32[]{:S(2)}, u32[]{:S(2)}) %collective-permute-start.3) | collective-permute-done | bytes 8224 | tf_op jit(solution)/shard_map/ppermute | solution.py:478
  100.9 3.0 %all-to-all-done = bf16[16,18,2,16,128]{4,3,2,1,0:T(8,128)(2,1)} async-done(((bf16[16,18,2,16,128]{4,3,2,1,0:T(8,128)(2,1)}), bf16[16,18,2,16,128]{4,3,2,1,0:T(8,128)(2,1)}, u32[]{:S(2)}, u32[]{:S(2)}) %all-to-all-start) | async-done | bytes 2359328 | tf_op jit(solution)/shard_map/all_to_all | solution.py:460
  104.7 14.3 %attend_merge_project.1 = (bf16[256,1024]{1,0:T(8,128)(2,1)}, bf16[256,512]{1,0:T(8,128)(2,1)}, bf16[256,512]{1,0:T(8,128)(2,1)}, bf16[256,512]{1,0:T(8,128)(2,1)}, bf16[256,512]{1,0:T(8,128)(2,1)}) custom-call(s32[2]{0:T(128)} %pad_add_fusion.1.place, s32[4224]{0:T(1024)} %concatenate.12.refs_2_.lists, bf16[16,128,128]{2,1,0:T(8,128)(2,1)} %bitcast.34, ...), custom_call_target="tpu_custom_call" | custom-call | tf_op jit(solution)/shard_map/attend_merge_project/pallas_call | solution.py:357
  119.0 2.4 %collective-permute-start.7 = (bf16[256,512]{1,0:T(8,128)(2,1)}, bf16[256,512]{1,0:T(8,128)(2,1)S(1)}, u32[]{:S(2)}, u32[]{:S(2)}) collective-permute-start(bf16[256,512]{1,0:T(8,128)(2,1)} %get-tuple-element.28), channel_id=1, source_target_pairs={{0,4},{2,6},{4,0},{6,2},{1,5},{3,7},{5,1},{7,3},{8,12},{10,14},{12... | collective-permute-start | bytes 786440 | tf_op jit(solution)/shard_map/ppermute | solution.py:397
  121.4 2.0 %collective-permute-start.9 = (bf16[256,512]{1,0:T(8,128)(2,1)}, bf16[256,512]{1,0:T(8,128)(2,1)}, u32[]{:S(2)}, u32[]{:S(2)}) collective-permute-start(bf16[256,512]{1,0:T(8,128)(2,1)} %get-tuple-element.30), channel_id=1, source_target_pairs={{0,6},{2,0},{4,2},{6,4},{1,7},{3,1},{5,3},{7,5},{8,14},{10,8},{12,... | collective-permute-start | bytes 786440 | tf_op jit(solution)/shard_map/ppermute | solution.py:397
  123.4 4.9 %project_mine.1 = (bf16[256,512]{1,0:T(8,128)(2,1)}, bf16[256,512]{1,0:T(8,128)(2,1)}, bf16[256,512]{1,0:T(8,128)(2,1)}, bf16[256,512]{1,0:T(8,128)(2,1)}) custom-call(s32[2]{0:T(128)} %pad_add_fusion.1.place, bf16[256,1024]{1,0:T(8,128)(2,1)} %get-tuple-element.22.heads, bf16[1024,4096]{1,0:T(8,128)(2,1)} %weight.3), custom_call_target="tpu_custom_call" | custom-call | flops 1000000000 | bytes 6000000 | tf_op jit(solution)/shard_map/project_mine/pallas_call | solution.py:381
  128.3 1.5 collective-permute-start.4
  129.8 2.6 %collective-permute-start.5 = (bf16[256,512]{1,0:T(8,128)(2,1)}, bf16[256,512]{1,0:T(8,128)(2,1)S(1)}, u32[]{:S(2)}, u32[]{:S(2)}) collective-permute-start(bf16[256,512]{1,0:T(8,128)(2,1)} %get-tuple-element.25), channel_id=1, source_target_pairs={{0,2},{2,4},{4,6},{6,0},{1,3},{3,5},{5,7},{7,1},{8,10},{10,12},{12... | collective-permute-start | bytes 786440 | tf_op jit(solution)/shard_map/ppermute | solution.py:397
  132.4 3.4 %collective-permute-done.8 = bf16[256,512]{1,0:T(8,128)(2,1)S(1)} collective-permute-done((bf16[256,512]{1,0:T(8,128)(2,1)}, bf16[256,512]{1,0:T(8,128)(2,1)S(1)}, u32[]{:S(2)}, u32[]{:S(2)}) %collective-permute-start.8) | collective-permute-done | bytes 262176 | tf_op jit(solution)/shard_map/ppermute | solution.py:397
  135.9 1.1 add_convert_fusion.1
  136.9 4.6 %collective-permute-start.10 = (bf16[256,512]{1,0:T(8,128)(2,1)S(1)}, bf16[256,512]{1,0:T(8,128)(2,1)S(1)}, u32[]{:S(2)}, u32[]{:S(2)}) collective-permute-start(bf16[256,512]{1,0:T(8,128)(2,1)S(1)} %add_convert_fusion.1), channel_id=1, source_target_pairs={{0,1},{1,0},{2,3},{3,2},{4,5},{5,4},{6,7},{7,6},{8,9},{9,8},{10,11... | collective-permute-start | bytes 786440 | tf_op jit(solution)/shard_map/ppermute | solution.py:482
  141.5 4.2 %collective-permute-done.5 = bf16[256,512]{1,0:T(8,128)(2,1)S(1)} collective-permute-done((bf16[256,512]{1,0:T(8,128)(2,1)}, bf16[256,512]{1,0:T(8,128)(2,1)S(1)}, u32[]{:S(2)}, u32[]{:S(2)}) %collective-permute-start.5) | collective-permute-done | bytes 262176 | tf_op jit(solution)/shard_map/ppermute | solution.py:397
  145.7 8.9 %collective-permute-done.10 = bf16[256,512]{1,0:T(8,128)(2,1)S(1)} collective-permute-done((bf16[256,512]{1,0:T(8,128)(2,1)S(1)}, bf16[256,512]{1,0:T(8,128)(2,1)S(1)}, u32[]{:S(2)}, u32[]{:S(2)}) %collective-permute-start.10) | collective-permute-done | bytes 262176 | tf_op jit(solution)/shard_map/ppermute | solution.py:482
  (71 shorter events, 9.1 us)
Async XLA Ops:
  5.3 5.9 %copy-start.4 = (s32[64,48]{0,1:T(8,128)S(1)}, s32[64,48]{0,1:T(8,128)}, u32[]{:S(2)}) copy-start(s32[64,48]{0,1:T(8,128)} %param.25) | copy-start | bytes 36868
  5.3 5.9 %copy-start.9 = (s32[64]{0:T(128)S(1)}, s32[64]{0:T(128)}, u32[]{:S(2)}) copy-start(s32[64]{0:T(128)} %param.26) | copy-start | bytes 772
  5.3 48.2 %all-to-all-start.1 = ((bf16[16,18,2,16,128]{4,3,2,1,0:T(8,128)(2,1)}), bf16[16,18,2,16,128]{4,3,2,1,0:T(8,128)(2,1)}, u32[]{:S(2)}, u32[]{:S(2)}) async-start(bf16[16,18,2,16,128]{4,3,2,1,0:T(8,128)(2,1)} %bitcast.28), calls=%async_computation.1 | async-start | bytes 4718592 | tf_op jit(solution)/shard_map/all_to_all | solution.py:460
  11.1 6.1 %copy-start.1 = (bf16[4,64,8,128]{3,2,1,0:T(8,128)(2,1)S(1)}, bf16[4,64,8,128]{3,2,1,0:T(8,128)(2,1)}, u32[]{:S(2)}) copy-start(bf16[4,64,8,128]{3,2,1,0:T(8,128)(2,1)} %param.14) | copy-start | bytes 1572868
  11.2 6.2 %copy-start.5 = (bf16[4,64,1,128]{3,1,2,0:T(8,128)(2,1)S(1)}, bf16[4,64,1,128]{3,1,2,0:T(8,128)(2,1)}, u32[]{:S(2)}) copy-start(bf16[4,64,1,128]{3,1,2,0:T(8,128)(2,1)} %param.16) | copy-start | bytes 196612
  11.2 6.1 %copy-start.6 = (bf16[4,64,1,128]{3,1,2,0:T(8,128)(2,1)S(1)}, bf16[4,64,1,128]{3,1,2,0:T(8,128)(2,1)}, u32[]{:S(2)}) copy-start(bf16[4,64,1,128]{3,1,2,0:T(8,128)(2,1)} %param.15) | copy-start | bytes 196612
  13.9 38.5 %collective-permute-start.1 = (s32[4224]{0:T(1024)S(1)}, s32[4224]{0:T(1024)S(1)}, u32[]{:S(2)}, u32[]{:S(2)}) collective-permute-start(s32[4224]{0:T(1024)S(1)} %concatenate.15), channel_id=1, source_target_pairs={{0,32},{32,0},{1,33},{33,1},{2,34},{34,2},{3,35},{35,3},{4,36},{36... | collective-permute-start | bytes 50696 | tf_op jit(solution)/shard_map/ppermute | solution.py:466
  17.2 33.3 %collective-permute-start = (bf16[4,64,8,128]{3,2,1,0:T(8,128)(2,1)S(1)}, bf16[4,64,8,128]{3,2,1,0:T(8,128)(2,1)}, u32[]{:S(2)}, u32[]{:S(2)}) collective-permute-start(bf16[4,64,8,128]{3,2,1,0:T(8,128)(2,1)S(1)} %copy-done.1), channel_id=1, source_target_pairs={{0,32},{32,0},{1,33},{33,1},{2,34},{34,2},{3,35},{35,3},{4,36},{36... | collective-permute-start | bytes 1572872 | tf_op jit(solution)/shard_map/ppermute | solution.py:465
  52.4 0.6 copy-start.7
  53.5 50.4 %all-to-all-start = ((bf16[16,18,2,16,128]{4,3,2,1,0:T(8,128)(2,1)}), bf16[16,18,2,16,128]{4,3,2,1,0:T(8,128)(2,1)}, u32[]{:S(2)}, u32[]{:S(2)}) async-start(bf16[16,18,2,16,128]{4,3,2,1,0:T(8,128)(2,1)} %bitcast.27), calls=%async_computation | async-start | bytes 4718592 | tf_op jit(solution)/shard_map/all_to_all | solution.py:460
  71.4 32.4 %collective-permute-start.2 = (bf16[2048,128]{1,0:T(8,128)(2,1)}, bf16[2048,128]{1,0:T(8,128)(2,1)S(1)}, u32[]{:S(2)}, u32[]{:S(2)}) collective-permute-start(bf16[2048,128]{1,0:T(8,128)(2,1)} %get-tuple-element.20), channel_id=1, source_target_pairs={{0,32},{32,0},{1,33},{33,1},{2,34},{34,2},{3,35},{35,3},{4,36},{36... | collective-permute-start | bytes 1572872 | tf_op jit(solution)/shard_map/ppermute | solution.py:477
  71.5 29.3 %collective-permute-start.3 = (f32[16,128]{1,0:T(8,128)}, f32[16,128]{1,0:T(8,128)S(1)}, u32[]{:S(2)}, u32[]{:S(2)}) collective-permute-start(f32[16,128]{1,0:T(8,128)} %get-tuple-element.21), channel_id=1, source_target_pairs={{0,32},{32,0},{1,33},{33,1},{2,34},{34,2},{3,35},{35,3},{4,36},{36... | collective-permute-start | bytes 24584 | tf_op jit(solution)/shard_map/ppermute | solution.py:478
  100.9 3.0 %copy-start.8 = (f32[16,128]{1,0:T(8,128)}, f32[16,128]{1,0:T(8,128)S(1)}, u32[]{:S(2)}) copy-start(f32[16,128]{1,0:T(8,128)S(1)} %collective-permute-done.3.lse2) | copy-start | bytes 24580
  103.9 0.8 copy-start
  119.0 13.4 %collective-permute-start.7 = (bf16[256,512]{1,0:T(8,128)(2,1)}, bf16[256,512]{1,0:T(8,128)(2,1)S(1)}, u32[]{:S(2)}, u32[]{:S(2)}) collective-permute-start(bf16[256,512]{1,0:T(8,128)(2,1)} %get-tuple-element.28), channel_id=1, source_target_pairs={{0,4},{2,6},{4,0},{6,2},{1,5},{3,7},{5,1},{7,3},{8,12},{10,14},{12... | collective-permute-start | bytes 786440 | tf_op jit(solution)/shard_map/ppermute | solution.py:397
  121.4 14.4 %collective-permute-start.8 = (bf16[256,512]{1,0:T(8,128)(2,1)}, bf16[256,512]{1,0:T(8,128)(2,1)S(1)}, u32[]{:S(2)}, u32[]{:S(2)}) collective-permute-start(bf16[256,512]{1,0:T(8,128)(2,1)} %get-tuple-element.29), channel_id=1, source_target_pairs={{0,2},{2,4},{4,6},{6,0},{1,3},{3,5},{5,7},{7,1},{8,10},{10,12},{12... | collective-permute-start | bytes 786440 | tf_op jit(solution)/shard_map/ppermute | solution.py:397
  121.4 14.5 %collective-permute-start.9 = (bf16[256,512]{1,0:T(8,128)(2,1)}, bf16[256,512]{1,0:T(8,128)(2,1)}, u32[]{:S(2)}, u32[]{:S(2)}) collective-permute-start(bf16[256,512]{1,0:T(8,128)(2,1)} %get-tuple-element.30), channel_id=1, source_target_pairs={{0,6},{2,0},{4,2},{6,4},{1,7},{3,1},{5,3},{7,5},{8,14},{10,8},{12,... | collective-permute-start | bytes 786440 | tf_op jit(solution)/shard_map/ppermute | solution.py:397
  123.4 12.4 %copy-start.2 = (bf16[256,512]{1,0:T(8,128)(2,1)S(1)}, bf16[256,512]{1,0:T(8,128)(2,1)}, u32[]{:S(2)}) copy-start(bf16[256,512]{1,0:T(8,128)(2,1)} %get-tuple-element.27) | copy-start | bytes 786436
  128.3 26.3 %copy-start.3 = (bf16[256,512]{1,0:T(8,128)(2,1)S(1)}, bf16[256,512]{1,0:T(8,128)(2,1)}, u32[]{:S(2)}) copy-start(bf16[256,512]{1,0:T(8,128)(2,1)} %get-tuple-element.23) | copy-start | bytes 786436
  128.3 13.2 %collective-permute-start.4 = (bf16[256,512]{1,0:T(8,128)(2,1)}, bf16[256,512]{1,0:T(8,128)(2,1)S(1)}, u32[]{:S(2)}, u32[]{:S(2)}) collective-permute-start(bf16[256,512]{1,0:T(8,128)(2,1)} %get-tuple-element.24), channel_id=1, source_target_pairs={{0,4},{2,6},{4,0},{6,2},{1,5},{3,7},{5,1},{7,3},{8,12},{10,14},{12... | collective-permute-start | bytes 786440 | tf_op jit(solution)/shard_map/ppermute | solution.py:397
  129.8 15.9 %collective-permute-start.5 = (bf16[256,512]{1,0:T(8,128)(2,1)}, bf16[256,512]{1,0:T(8,128)(2,1)S(1)}, u32[]{:S(2)}, u32[]{:S(2)}) collective-permute-start(bf16[256,512]{1,0:T(8,128)(2,1)} %get-tuple-element.25), channel_id=1, source_target_pairs={{0,2},{2,4},{4,6},{6,0},{1,3},{3,5},{5,7},{7,1},{8,10},{10,12},{12... | collective-permute-start | bytes 786440 | tf_op jit(solution)/shard_map/ppermute | solution.py:397
  132.4 13.3 %collective-permute-start.6 = (bf16[256,512]{1,0:T(8,128)(2,1)}, bf16[256,512]{1,0:T(8,128)(2,1)S(1)}, u32[]{:S(2)}, u32[]{:S(2)}) collective-permute-start(bf16[256,512]{1,0:T(8,128)(2,1)} %get-tuple-element.26), channel_id=1, source_target_pairs={{0,6},{2,0},{4,2},{6,4},{1,7},{3,1},{5,3},{7,5},{8,14},{10,8},{12,... | collective-permute-start | bytes 786440 | tf_op jit(solution)/shard_map/ppermute | solution.py:397
  136.9 17.6 %collective-permute-start.10 = (bf16[256,512]{1,0:T(8,128)(2,1)S(1)}, bf16[256,512]{1,0:T(8,128)(2,1)S(1)}, u32[]{:S(2)}, u32[]{:S(2)}) collective-permute-start(bf16[256,512]{1,0:T(8,128)(2,1)S(1)} %add_convert_fusion.1), channel_id=1, source_target_pairs={{0,1},{1,0},{2,3},{3,2},{4,5},{5,4},{6,7},{7,6},{8,9},{9,8},{10,11... | collective-permute-start | bytes 786440 | tf_op jit(solution)/shard_map/ppermute | solution.py:482

commit v4 on v3

--- a/solution.py
+++ b/solution.py
@@ -25,8 +25,8 @@
 NARROW = 8
 WIDE = 16
 WIDE_CHUNKS = 4
-UNROLL = 2
 POSITIONS = WIDE * WIDE_CHUNKS
+LIST = ROWS * (POSITIONS + 2)
 TEAM = 4
 TEAMS = ROWS // TEAM
 LANES = TEAM * QROWS
@@ -39,63 +39,71 @@
 PARAMS = pltpu.CompilerParams(vmem_limit_bytes=VMEM_LIMIT)
 
 
+def start_all(pairs, sems):
+    copies = [pltpu.make_async_copy(src, dst, sems.at[n]) for n, (src, dst) in enumerate(pairs)]
+    for copy in copies:
+        copy.start()
+    return copies
+
+
+def wait_all(copies):
+    for copy in copies:
+        copy.wait()
+
+
 def pack_kernel(half, pdest, mdest, pk, pv, mk, mv, *refs):
-    out, pages, send, count, sems, out_sem = refs[-6:]
-    loads = [
-        pltpu.make_async_copy(pk, pages.at[pl.ds(0, OUT), 0], sems.at[0]),
-        pltpu.make_async_copy(pv, pages.at[pl.ds(0, OUT), 1], sems.at[1]),
-        pltpu.make_async_copy(mk, pages.at[pl.ds(OUT, MIG), 0], sems.at[2]),
-        pltpu.make_async_copy(mv, pages.at[pl.ds(OUT, MIG), 1], sems.at[3]),
-    ]
-    for load in loads:
-        load.start()
+    out, pages, send, pdest_s, mdest_s, slots, count, sems, out_sem = refs[-9:]
+    loads = start_all(
+        [
+            (pdest, pdest_s),
+            (mdest, mdest_s),
+            (pk, pages.at[pl.ds(0, OUT), 0]),
+            (pv, pages.at[pl.ds(0, OUT), 1]),
+            (mk, pages.at[pl.ds(OUT, MIG), 0]),
+            (mv, pages.at[pl.ds(OUT, MIG), 1]),
+        ],
+        sems,
+    )
     wanted = half[0]
-
-    def clear(i, carry):
-        count[i] = 0
+    for d in range(N_INST):
+        count[d] = 0
+        count[N_INST + d] = PCAP
+    wait_all(loads[:2])
+
+    def rank(dest, kind, first, j, carry):
+        d = dest[j]
+        k = count[kind + d]
+        count[kind + d] = k + 1
+        group = (d >> 3) * 4 + (d & 3)
+        slots[first + j] = jnp.where(((d >> 2) & 1) == wanted, group * SLOTS + k, RECV)
         return carry
 
-    def place(dest, first, origin, j):
-        d = dest[j]
-        k = count[d]
-        count[d] = k + 1
-        group = (d >> 3) * 4 + (d & 3)
-        slot = jnp.where(((d >> 2) & 1) == wanted, group * SLOTS + first + k, RECV)
-        send[slot] = pages[origin + j]
-
-    def prompt(j, carry):
-        place(pdest, 0, 0, j)
+    def copy_page(j, carry):
+        send[slots[j]] = pages[j]
         return carry
 
-    def moved(j, carry):
-        place(mdest, PCAP, OUT, j)
-        return carry
-
-    lax.fori_loop(0, N_INST, clear, 0)
-    loads[0].wait()
-    loads[1].wait()
-    lax.fori_loop(0, OUT, prompt, 0, unroll=4)
-    lax.fori_loop(0, N_INST, clear, 0)
-    loads[2].wait()
-    loads[3].wait()
-    lax.fori_loop(0, MIG, moved, 0, unroll=4)
-    store = pltpu.make_async_copy(send.at[pl.ds(0, RECV)], out, out_sem)
-    store.start()
-    store.wait()
+    lax.fori_loop(0, OUT, functools.partial(rank, pdest_s, 0, 0), 0, unroll=8)
+    lax.fori_loop(0, MIG, functools.partial(rank, mdest_s, N_INST, OUT), 0, unroll=8)
+    wait_all(loads[2:])
+    lax.fori_loop(0, OUT + MIG, copy_page, 0, unroll=8)
+    wait_all(start_all([(send.at[pl.ds(0, RECV)], out)], out_sem))
 
 
 def pack(half, pdest, mdest, pk, pv, mk, mv, *after):
     return pl.pallas_call(
         pack_kernel,
         out_shape=jax.ShapeDtypeStruct((RECV, 2, PAGE, DH), jnp.bfloat16),
-        in_specs=[SMEM, SMEM, SMEM] + [ANY] * (4 + len(after)),
+        in_specs=[SMEM] + [ANY] * (6 + len(after)),
         out_specs=ANY,
         scratch_shapes=[
             pltpu.VMEM((OUT + MIG, 2, PAGE, DH), jnp.bfloat16),
             pltpu.VMEM((RECV + 1, 2, PAGE, DH), jnp.bfloat16),
-            pltpu.SMEM((N_INST,), jnp.int32),
-            pltpu.SemaphoreType.DMA((4,)),
-            pltpu.SemaphoreType.DMA,
+            pltpu.SMEM((OUT,), jnp.int32),
+            pltpu.SMEM((MIG,), jnp.int32),
+            pltpu.SMEM((OUT + MIG,), jnp.int32),
+            pltpu.SMEM((2 * N_INST,), jnp.int32),
+            pltpu.SemaphoreType.DMA((6,)),
+            pltpu.SemaphoreType.DMA((1,)),
         ],
         compiler_params=PARAMS,
         cost_estimate=pl.CostEstimate(flops=10**6, bytes_accessed=10**7, transcendentals=0),
@@ -120,8 +128,8 @@
 
 def attention(fresh, lists, q, kv, out, lse, scores):
     lane = lax.broadcasted_iota(jnp.int32, (1, LANES), 1)
-    team_row = lane // QROWS
-    step = (lane % QROWS) // GROUPS
+    team_row = (lane // GROUPS) % TEAM
+    step = lane // (TEAM * GROUPS)
 
     def load(r, first, n, which):
         return [kv[lists[r * POSITIONS + first + p], which] for p in range(n)]
@@ -131,6 +139,13 @@
 
     def tokens(r):
         return lists[ROWS * POSITIONS + ROWS + r]
+
+    def team(t, g):
+        first = t * ROWS * GROUPS + g * TEAM * GROUPS
+        return pl.ds(first if isinstance(g, int) else pl.multiple_of(first, TEAM * GROUPS), TEAM * GROUPS)
+
+    def queries(g):
+        return jnp.concatenate([q[team(t, g), :] for t in range(STEPS)], axis=0)
 
     def mask(s, first, limit):
         token = lax.broadcasted_iota(jnp.int32, s.shape, 0) + first
@@ -146,10 +161,10 @@
         width = NARROW * PAGE
         rows = [g * TEAM + i for i in range(TEAM)]
         keys = jnp.concatenate([k for r in rows for k in load(r, 0, NARROW, 0)], axis=0)
-        s_all = dot_nt(keys, q[g])
+        s_all = dot_nt(keys, queries(g))
         s = s_all[:width]
         limit = jnp.full((1, LANES), tokens(rows[0]), jnp.int32)
-        owner = lax.broadcasted_iota(jnp.int32, (width, LANES), 1) // QROWS
+        owner = (lax.broadcasted_iota(jnp.int32, (width, LANES), 1) // GROUPS) % TEAM
         for i in range(1, TEAM):
             s = jnp.where(owner == i, s_all[i * width : (i + 1) * width], s)
             limit = jnp.where(team_row == i, tokens(rows[i]), limit)
@@ -159,19 +174,18 @@
         total = jnp.sum(e, axis=0, keepdims=True)
         safe = jnp.maximum(total, 1e-30)
         lse[pl.ds(g, 1), :] = jnp.where(total > 0.0, m + jnp.log(safe), -1e30)
-        weights = (e * (1.0 / safe)).T.astype(jnp.bfloat16)
+        weights = (e * (1.0 / safe)).T
         for i in range(TEAM):
             values = jnp.concatenate(load(rows[i], 0, NARROW, 1), axis=0)
-            part = weights[i * QROWS : (i + 1) * QROWS]
-            first = pl.multiple_of(g * LANES + i * QROWS, QROWS)
-            out[pl.ds(first, QROWS), :] = jnp.dot(part, values, preferred_element_type=jnp.float32)
-
-    def narrow_body(n, carry):
-        for u in range(UNROLL):
-            narrow(n * UNROLL + u)
-        return carry
-
-    lax.fori_loop(0, TEAMS // UNROLL, narrow_body, 0)
+            pieces = [weights[(t * TEAM + i) * GROUPS : (t * TEAM + i + 1) * GROUPS] for t in range(STEPS)]
+            part = jnp.concatenate(pieces, axis=0).astype(jnp.bfloat16)
+            product = jnp.dot(part, values, preferred_element_type=jnp.float32)
+            for t in range(STEPS):
+                first = (t * ROWS + rows[i]) * GROUPS
+                out[pl.ds(first, GROUPS), :] = product[t * GROUPS : (t + 1) * GROUPS]
+
+    for g in range(TEAMS):
+        narrow(g)
 
     def wide(r):
         width = WIDE * PAGE
@@ -180,7 +194,7 @@
 
         def first_pass(c, m):
             keys = jnp.concatenate(load(r, c * WIDE, WIDE, 0), axis=0)
-            s = mask(dot_nt(keys, q[g]), c * width, tokens(r))
+            s = mask(dot_nt(keys, queries(g)), c * width, tokens(r))
             scores[c] = s
             return jnp.maximum(m, jnp.max(s, axis=0, keepdims=True))
 
@@ -201,9 +215,11 @@
             return product + jnp.dot(weights, values, preferred_element_type=jnp.float32)
 
         product = lax.fori_loop(0, chunks, third_pass, jnp.zeros((LANES, DH), jnp.float32))
-        rows = pl.ds(pl.multiple_of(g * LANES, LANES), LANES)
-        block = lax.broadcasted_iota(jnp.int32, (LANES, DH), 0) // QROWS
-        out[rows, :] = jnp.where(block == i, product, out[rows, :])
+        size = TEAM * GROUPS
+        owner = lax.broadcasted_iota(jnp.int32, (size, DH), 0) // GROUPS
+        for t in range(STEPS):
+            rows = team(t, g)
+            out[rows, :] = jnp.where(owner == i, product[t * size : (t + 1) * size], out[rows, :])
         new = jnp.where(total > 0.0, m + jnp.log(safe), -1e30)
         lse[pl.ds(g, 1), :] = jnp.where(team_row == i, new, lse[pl.ds(g, 1), :])
 
@@ -214,26 +230,35 @@
     lax.fori_loop(0, ROWS, wide_body, 0)
 
 
+QUERIES = pltpu.VMEM((ROWS * QROWS, DH), jnp.bfloat16)
 SCORES = pltpu.VMEM((WIDE_CHUNKS, WIDE * PAGE, LANES), jnp.float32)
 RESULT = pltpu.VMEM((ROWS * QROWS, DH), jnp.float32)
+LSE = pltpu.VMEM((TEAMS, LANES), jnp.float32)
+LISTS = pltpu.SMEM((LIST,), jnp.int32)
+
+
+def pages_scratch(n):
+    return pltpu.VMEM((1 + n, 2, PAGE, DH), jnp.bfloat16)
 
 
 def blank_page():
     return jnp.zeros((2, PAGE, DH), jnp.bfloat16)
 
 
-def attend_local_kernel(lists, q, pool_k, pool_v, fresh, out, lse, kv, scores, sem):
-    copies = [
-        pltpu.make_async_copy(pool_k, kv.at[pl.ds(1, POOL), 0], sem),
-        pltpu.make_async_copy(pool_v, kv.at[pl.ds(1, POOL), 1], sem),
-        pltpu.make_async_copy(fresh, kv.at[pl.ds(1 + POOL, ROWS)], sem),
-    ]
-    for copy in copies:
-        copy.start()
+def attend_local_kernel(lists, q, pool_k, pool_v, fresh, out, lse, lists_s, q_s, kv, scores, sems):
+    copies = start_all(
+        [
+            (lists, lists_s),
+            (q, q_s),
+            (pool_k, kv.at[pl.ds(1, POOL), 0]),
+            (pool_v, kv.at[pl.ds(1, POOL), 1]),
+            (fresh, kv.at[pl.ds(1 + POOL, ROWS)]),
+        ],
+        sems,
+    )
     kv[0] = blank_page()
-    for copy in copies:
-        copy.wait()
-    attention(True, lists, q, kv, out, lse, scores)
+    wait_all(copies)
+    attention(True, lists_s, q_s, kv, out, lse, scores)
 
 
 def attend_local(lists, q, pool_k, pool_v, fresh):
@@ -243,25 +268,20 @@
             jax.ShapeDtypeStruct((ROWS * QROWS, DH), jnp.float32),
             jax.ShapeDtypeStruct((TEAMS, LANES), jnp.float32),
         ),
-        in_specs=[SMEM, VMEM, ANY, ANY, ANY],
+        in_specs=[ANY] * 5,
         out_specs=(VMEM, VMEM),
-        scratch_shapes=[
-            pltpu.VMEM((1 + POOL + ROWS, 2, PAGE, DH), jnp.bfloat16),
-            SCORES,
-            pltpu.SemaphoreType.DMA,
-        ],
+        scratch_shapes=[LISTS, QUERIES, pages_scratch(POOL + ROWS), SCORES, pltpu.SemaphoreType.DMA((5,))],
         compiler_params=PARAMS,
         cost_estimate=pl.CostEstimate(flops=10**9, bytes_accessed=10**7, transcendentals=10**6),
         name="attend_local",
     )(lists, q, pool_k, pool_v, fresh)
 
 
-def attend_far_kernel(lists, q, recv, out, lse, kv, result, scores, sem):
-    copy = pltpu.make_async_copy(recv, kv.at[pl.ds(1, RECV)], sem)
-    copy.start()
+def attend_far_kernel(lists, q, recv, out, lse, lists_s, q_s, kv, result, scores, sems):
+    copies = start_all([(lists, lists_s), (q, q_s), (recv, kv.at[pl.ds(1, RECV)])], sems)
     kv[0] = blank_page()
-    copy.wait()
-    attention(False, lists, q, kv, result, lse, scores)
+    wait_all(copies)
+    attention(False, lists_s, q_s, kv, result, lse, scores)
     out[...] = result[...].astype(jnp.bfloat16)
 
 
@@ -272,14 +292,9 @@
             jax.ShapeDtypeStruct((ROWS * QROWS, DH), jnp.bfloat16),
             jax.ShapeDtypeStruct((TEAMS, LANES), jnp.float32),
         ),
-        in_specs=[SMEM, VMEM, ANY],
+        in_specs=[ANY] * 3,
         out_specs=(VMEM, VMEM),
-        scratch_shapes=[
-            pltpu.VMEM((1 + RECV, 2, PAGE, DH), jnp.bfloat16),
-            RESULT,
-            SCORES,
-            pltpu.SemaphoreType.DMA,
-        ],
+        scratch_shapes=[LISTS, QUERIES, pages_scratch(RECV), RESULT, SCORES, pltpu.SemaphoreType.DMA((3,))],
         compiler_params=PARAMS,
         cost_estimate=pl.CostEstimate(flops=10**9, bytes_accessed=10**7, transcendentals=10**6),
         name="attend_far",
@@ -329,26 +344,40 @@
 
 
 def finish_kernel(place, lists, q, recv, o1, lse1, o2, lse2, weight, heads, *refs):
-    outs, (kv, lse3, result, scores, sem, w, terms, w_sems, out_sems) = refs[:TILES], refs[TILES:]
-    copy = pltpu.make_async_copy(recv, kv.at[pl.ds(1, RECV)], sem)
-    copy.start()
+    outs, refs = refs[:TILES], refs[TILES:]
+    lists_s, q_s, kv, o1_s, lse1_s, o2_s, lse2_s, lse3, result, scores, sems, w, terms, w_sems, out_sems = refs
+    copies = start_all(
+        [
+            (lists, lists_s),
+            (q, q_s),
+            (recv, kv.at[pl.ds(1, RECV)]),
+            (lse1, lse1_s),
+            (lse2, lse2_s),
+            (o1, o1_s),
+            (o2, o2_s),
+        ],
+        sems,
+    )
+    kv[0] = blank_page()
+    wait_all(copies[:3])
     loads = start_tiles(place, 1, weight, w, w_sems)
-    kv[0] = blank_page()
-    copy.wait()
-    attention(False, lists, q, kv, result, lse3, scores)
-
-    top = jnp.maximum(jnp.maximum(lse1[...], lse2[...]), lse3[...])
-    parts = [jnp.exp(x[...] - top) for x in (lse1, lse2, lse3)]
+    attention(False, lists_s, q_s, kv, result, lse3, scores)
+    wait_all(copies[3:])
+
+    top = jnp.maximum(jnp.maximum(lse1_s[...], lse2_s[...]), lse3[...])
+    parts = [jnp.exp(x[...] - top) for x in (lse1_s, lse2_s, lse3)]
     inverse = 1.0 / (parts[0] + parts[1] + parts[2])
     f1, f2, f3 = [(x * inverse).T for x in parts]
-    for g in range(TEAMS):
-        rows = pl.ds(g * LANES, LANES)
-        merged = f1[:, g : g + 1] * o1[rows, :] + f2[:, g : g + 1] * o2[rows, :].astype(jnp.float32)
-        result[rows, :] = merged + f3[:, g : g + 1] * result[rows, :]
-    for j in range(QROWS):
-        t, h = j // GROUPS, j % GROUPS
-        column = result[pl.ds(j, ROWS, stride=QROWS), :]
-        heads[pl.ds(t * ROWS, ROWS), pl.ds(h * DH, DH)] = column.astype(jnp.bfloat16)
+    size = TEAM * GROUPS
+    for t in range(STEPS):
+        for g in range(TEAMS):
+            rows = pl.ds((t * TEAMS + g) * size, size)
+            lanes = slice(t * size, (t + 1) * size)
+            merged = f1[lanes, g : g + 1] * o1_s[rows, :] + f2[lanes, g : g + 1] * o2_s[rows, :].astype(jnp.float32)
+            result[rows, :] = merged + f3[lanes, g : g + 1] * result[rows, :]
+        for h in range(GROUPS):
+            column = result[pl.ds(t * ROWS * GROUPS + h, ROWS, stride=GROUPS), :]
+            heads[pl.ds(t * ROWS, ROWS), pl.ds(h * DH, DH)] = column.astype(jnp.bfloat16)
     project(loads, heads, w, outs, terms, out_sems)
 
 
@@ -357,14 +386,11 @@
     heads, *terms = pl.pallas_call(
         finish_kernel,
         out_shape=(heads,) + TERMS,
-        in_specs=[SMEM, SMEM, VMEM, ANY, VMEM, VMEM, VMEM, VMEM, ANY],
+        in_specs=[SMEM] + [ANY] * 8,
         out_specs=(VMEM,) + (ANY,) * TILES,
         scratch_shapes=[
-            pltpu.VMEM((1 + RECV, 2, PAGE, DH), jnp.bfloat16),
-            pltpu.VMEM((TEAMS, LANES), jnp.float32),
-            RESULT,
-            SCORES,
-            pltpu.SemaphoreType.DMA,
+            LISTS, QUERIES, pages_scratch(RECV), RESULT, LSE, QUERIES, LSE, LSE, RESULT, SCORES,
+            pltpu.SemaphoreType.DMA((7,)),
         ] + PROJECT_SCRATCH,
         compiler_params=PARAMS,
         name="attend_merge_project",
@@ -429,10 +455,6 @@
     group = (source >> 3) * 4 + (source & 3)
     here = (table >= POOL) & (((source >> 2) & 1) == half)
     return page_lists(here, 1 + group * SLOTS + rank, lengths)
-
-
-def by_team(queries):
-    return queries.transpose(1, 0, 2, 3).reshape(TEAMS, LANES, DH)
 
 
 def per_device(
@@ -462,13 +484,13 @@
 
     pages = (page(prompt_keys), page(prompt_values), page(moved_keys), page(moved_values))
     far_recv = exchange(pack((1 - half)[None], prompt_dest, moved_dest, *pages))
-    far_q = by_team(lax.ppermute(queries, "izh", swap))
+    q = queries.reshape(ROWS * QROWS, DH)
+    far_q = lax.ppermute(q, "izh", swap)
     far_lists = lax.ppermute(arrived_lists(block_table, context_len, 1 - half), "izh", swap)
     near_lists = arrived_lists(block_table, context_len, half)
 
     fresh = jnp.stack([new_keys, new_values], axis=0).reshape(2, STEPS, ROWS, DH).transpose(2, 0, 1, 3)
     fresh = jnp.pad(fresh, ((0, 0), (0, 0), (0, PAGE - STEPS), (0, 0)))
-    q = by_team(queries)
     o1, lse1 = attend_local(local_lists(block_table, context_len), q, page(pool_keys), page(pool_values), fresh)
     near_send = pack(half[None], prompt_dest, moved_dest, *pages, lse1)
     near_recv = exchange(gate(near_send, far_q, far_lists, near_lists))

time: 156 us -> 148 us (0.949)
  Pallas kernels: 49.5 us -> 35.9 us
  waiting for transfers between devices: 59.8 us -> 70.8 us
  local copies, waits for them, and re-layouts: 7.7 us -> 4.22 us
  starting transfers between devices: 33.6 us -> 31.6 us
    ppermute x1, waiting for transfers between devices: 0.01 us -> 8.31 us  [per_device(): lax.ppermute(arrived_lists(block_table, context_len, 1 - half), 'izh', swap)]
    pallas_call x1, Pallas kernels: 14.3 us -> 10.1 us  [finish(): pl.pallas_call(finish_kernel, out_shape=(heads,) + TERMS, in_specs=[SMEM]...]
    pallas_call x1, Pallas kernels: 9.63 us -> 5.76 us  [attend_far(): pl.pallas_call(attend_far_kernel, out_shape=(jax.ShapeDtypeStruct((ROWS *...]
    ppermute x1, waiting for transfers between devices: 25.8 us -> 29.7 us  [per_device(): lse2 = lax.ppermute(lse2, 'izh', swap)]
    pallas_call x1, Pallas kernels: 10.1 us -> 6.69 us  [attend_local(): pl.pallas_call(attend_local_kernel, out_shape=(jax.ShapeDtypeStruct((ROWS...]
    ppermute x1, waiting for transfers between devices: 14 us -> 11 us  [per_device(): far_q = lax.ppermute(q, 'izh', swap)]
    transpose x2 -> x0, local copies, waits for them, and re-layouts: 2.88 us -> none  [by_team(): return queries.transpose(1, 0, 2, 3).reshape(TEAMS, LANES, DH)]
    all_to_all x2, waiting for transfers between devices: 3.45 us -> 6.01 us  [exchange(): recv = lax.all_to_all(send, HALF, split_axis=0, concat_axis=0, tiled=True)]
  transfers between devices with their start and end apart: 13 -> 13, of which waited for: 8 -> 9; matrix products, arithmetic and copies ran while one was open for 6% -> 5% of each run, Pallas kernels for 19% -> 15%
where the time goes in v4:
time: 148 us; the launch traced here: 147 us
  waiting for transfers between devices  70.8 us (48%)
  Pallas kernels  35.9 us (24%)
  starting transfers between devices  31.6 us (21%)
  other arithmetic  4.64 us (3%)
  local copies, waits for them, and re-layouts  4.22 us (3%)
    ppermute x1, waiting for transfers between devices, per_device(): lse2 = lax.ppermute(lse2, 'izh', swap)  29.7 us
    all_to_all x2, starting transfers between devices, exchange(): recv = lax.all_to_all(send, HALF, split_axis=0, concat_axis=0, tiled=True)  11.6 us
    ppermute x1, waiting for transfers between devices, per_device(): far_q = lax.ppermute(q, 'izh', swap)  11 us
    pallas_call x1, Pallas kernels, finish(): pl.pallas_call(finish_kernel, out_shape=(heads,) + TERMS, in_specs=[SMEM]...  10.1 us
    ppermute x1, waiting for transfers between devices, per_device(): other = lax.ppermute(sum_over_y(terms).astype(jnp.bfloat16), 'tz', swap)  9.19 us
    pallas_call x2, Pallas kernels, pack(): pl.pallas_call(pack_kernel, out_shape=jax.ShapeDtypeStruct((RECV, 2, PAGE...  8.52 us
    ppermute x6, starting transfers between devices, sum_over_y(): moved = lax.ppermute(term, 'ty', [(i, (i + shift) % 4) for i in range(4)])  8.52 us
    ppermute x1, waiting for transfers between devices, per_device(): lax.ppermute(arrived_lists(block_table, context_len, 1 - half), 'izh', swap)  8.31 us
  transfers between devices with their start and end apart: 13, of which 9 were waited for; matrix products, arithmetic and copies ran while one was open for 5% of the time, Pallas kernels for 15%

profile of v4, /device:TPU:8, one launch (start us, length us, event | category | flops | bytes accessed | tf_op | source)
XLA Modules:
  0.0 147.5 jit_solution(10682620793273213556)
XLA Ops:
  0.0 4.2 %pack_pages.3 = bf16[288,2,16,128]{3,2,1,0:T(8,128)(2,1)} custom-call(s32[1]{0:T(128)} %bitcast.16.half, s32[192]{0:T(256)} %pdest.3, s32[96]{0:T(128)} %mdest.3, bf16[192,16,128]{2,1,0:T(8,128)(2,1)} %bitcast.26, bf16[192,16,128]{2,1,0:T(8,128)(2,1)} %bitcast.28, bf16[96,16,128]{2,1,0:T(8,128)(2,1)} %bitcast.30, bf16[96,16,128]{2,1,0:T(8,128)(2,1)} %bitcast.32), custom_call_target="tpu_custom_call" | custom-call | flops 1000000 | bytes 10000000 | tf_op jit(solution)/shard_map/pack_pages/pallas_call | solution.py:93
  4.3 5.8 %all-to-all-start.1 = ((bf16[16,18,2,16,128]{4,3,2,1,0:T(8,128)(2,1)}), bf16[16,18,2,16,128]{4,3,2,1,0:T(8,128)(2,1)}, u32[]{:S(2)}, u32[]{:S(2)}) async-start(bf16[16,18,2,16,128]{4,3,2,1,0:T(8,128)(2,1)} %bitcast.25), calls=%async_computation.1 | async-start | bytes 4718592 | tf_op jit(solution)/shard_map/all_to_all | solution.py:482
  12.9 3.3 %collective-permute-start.1 = (s32[4224]{0:T(1024)S(1)}, s32[4224]{0:T(1024)S(1)}, u32[]{:S(2)}, u32[]{:S(2)}) collective-permute-start(s32[4224]{0:T(1024)S(1)} %concatenate.15), channel_id=1, source_target_pairs={{0,32},{32,0},{1,33},{33,1},{2,34},{34,2},{3,35},{35,3},{4,36},{36... | collective-permute-start | bytes 50696 | tf_op jit(solution)/shard_map/ppermute | solution.py:489
  18.3 6.7 %attend_local.1 = (f32[2048,128]{1,0:T(8,128)}, f32[16,128]{1,0:T(8,128)}) custom-call(s32[4224]{0:T(1024)} %concatenate.14.lists, bf16[2048,128]{1,0:T(8,128)(2,1)} %bitcast.34, bf16[192,16,128]{2,1,0:T(8,128)(2,1)} %bitcast.37, bf16[192,16,128]{2,1,0:T(8,128)(2,1)} %bitcast.38, bf16[64,2,16,128]{3,2,1,0:T(8,128)(2,1)} %pad.17.fresh), custom_call_target="tpu_custom_call" | custom-call | flops 1000000000 | bytes 10000000 | tf_op jit(solution)/shard_map/attend_local/pallas_call | solution.py:265
  25.8 4.3 %pack_pages.2.x = bf16[288,2,16,128]{3,2,1,0:T(8,128)(2,1)} custom-call(s32[1]{0:T(128)} %bitcast.3.half, s32[192]{0:T(256)} %pdest.3, s32[96]{0:T(128)} %mdest.3, bf16[192,16,128]{2,1,0:T(8,128)(2,1)} %bitcast.27, bf16[192,16,128]{2,1,0:T(8,128)(2,1)} %bitcast.29, bf16[96,16,128]{2,1,0:T(8,128)(2,1)} %bitcast.31, bf16[96,16,128]{2,1,0:T(8,128)(2,1)} %bitcast.33, ...), custom_call_target="tpu_custom_call" | custom-call | flops 1000000 | bytes 10000000 | tf_op jit(solution)/shard_map/pack_pages/pallas_call | solution.py:93
  30.1 8.3 %collective-permute-done.1.refs_1_.lists = s32[4224]{0:T(1024)S(1)} collective-permute-done((s32[4224]{0:T(1024)S(1)}, s32[4224]{0:T(1024)S(1)}, u32[]{:S(2)}, u32[]{:S(2)}) %collective-permute-start.1) | collective-permute-done | bytes 16928 | tf_op jit(solution)/shard_map/ppermute | solution.py:489
  38.4 11.0 %collective-permute-done.refs_0_.q = bf16[2048,128]{1,0:T(8,128)(2,1)} collective-permute-done((bf16[2048,128]{1,0:T(8,128)(2,1)S(1)}, bf16[2048,128]{1,0:T(8,128)(2,1)}, u32[]{:S(2)}, u32[]{:S(2)}) %collective-permute-start) | collective-permute-done | bytes 524320 | tf_op jit(solution)/shard_map/ppermute | solution.py:488
  49.4 3.0 %all-to-all-done.1 = bf16[16,18,2,16,128]{4,3,2,1,0:T(8,128)(2,1)} async-done(((bf16[16,18,2,16,128]{4,3,2,1,0:T(8,128)(2,1)}), bf16[16,18,2,16,128]{4,3,2,1,0:T(8,128)(2,1)}, u32[]{:S(2)}, u32[]{:S(2)}) %all-to-all-start.1) | async-done | bytes 2359328 | tf_op jit(solution)/shard_map/all_to_all | solution.py:482
  52.4 5.7 %all-to-all-start = ((bf16[16,18,2,16,128]{4,3,2,1,0:T(8,128)(2,1)}), bf16[16,18,2,16,128]{4,3,2,1,0:T(8,128)(2,1)}, u32[]{:S(2)}, u32[]{:S(2)}) async-start(bf16[16,18,2,16,128]{4,3,2,1,0:T(8,128)(2,1)} %bitcast.24), calls=%async_computation | async-start | bytes 4718592 | tf_op jit(solution)/shard_map/all_to_all | solution.py:482
  58.2 5.8 %attend_far.1 = (bf16[2048,128]{1,0:T(8,128)(2,1)}, f32[16,128]{1,0:T(8,128)}) custom-call(s32[4224]{0:T(1024)} %copy-done.7, bf16[2048,128]{1,0:T(8,128)(2,1)} %collective-permute-done.refs_0_.q, bf16[288,2,16,128]{3,2,1,0:T(8,128)(2,1)} %bitcast.18.recv), custom_call_target="tpu_custom_call" | custom-call | flops 1000000000 | bytes 10000000 | tf_op jit(solution)/shard_map/attend_far/pallas_call | solution.py:289
  64.4 2.6 %collective-permute-start.3 = (f32[16,128]{1,0:T(8,128)}, f32[16,128]{1,0:T(8,128)S(1)}, u32[]{:S(2)}, u32[]{:S(2)}) collective-permute-start(f32[16,128]{1,0:T(8,128)} %get-tuple-element.21), channel_id=1, source_target_pairs={{0,32},{32,0},{1,33},{33,1},{2,34},{34,2},{3,35},{35,3},{4,36},{36... | collective-permute-start | bytes 24584 | tf_op jit(solution)/shard_map/ppermute | solution.py:500
  67.6 29.7 %collective-permute-done.3.lse2 = f32[16,128]{1,0:T(8,128)S(1)} collective-permute-done((f32[16,128]{1,0:T(8,128)}, f32[16,128]{1,0:T(8,128)S(1)}, u32[]{:S(2)}, u32[]{:S(2)}) %collective-permute-start.3) | collective-permute-done | bytes 8224 | tf_op jit(solution)/shard_map/ppermute | solution.py:500
  97.3 3.0 %all-to-all-done = bf16[16,18,2,16,128]{4,3,2,1,0:T(8,128)(2,1)} async-done(((bf16[16,18,2,16,128]{4,3,2,1,0:T(8,128)(2,1)}), bf16[16,18,2,16,128]{4,3,2,1,0:T(8,128)(2,1)}, u32[]{:S(2)}, u32[]{:S(2)}) %all-to-all-start) | async-done | bytes 2359328 | tf_op jit(solution)/shard_map/all_to_all | solution.py:482
  101.1 10.1 %attend_merge_project.1 = (bf16[256,1024]{1,0:T(8,128)(2,1)}, bf16[256,512]{1,0:T(8,128)(2,1)}, bf16[256,512]{1,0:T(8,128)(2,1)}, bf16[256,512]{1,0:T(8,128)(2,1)}, bf16[256,512]{1,0:T(8,128)(2,1)}) custom-call(s32[2]{0:T(128)} %pad_add_fusion.1.place, s32[4224]{0:T(1024)} %concatenate.12.refs_2_.lists, bf16[2048,128]{1,0:T(8,128)(2,1)} %bitcast.35, ...), custom_call_target="tpu_custom_call" | custom-call | tf_op jit(solution)/shard_map/attend_merge_project/pallas_call | solution.py:386
  111.2 2.4 %collective-permute-start.7 = (bf16[256,512]{1,0:T(8,128)(2,1)}, bf16[256,512]{1,0:T(8,128)(2,1)S(1)}, u32[]{:S(2)}, u32[]{:S(2)}) collective-permute-start(bf16[256,512]{1,0:T(8,128)(2,1)} %get-tuple-element.28), channel_id=1, source_target_pairs={{0,4},{2,6},{4,0},{6,2},{1,5},{3,7},{5,1},{7,3},{8,12},{10,14},{12... | collective-permute-start | bytes 786440 | tf_op jit(solution)/shard_map/ppermute | solution.py:423
  113.6 2.0 %collective-permute-start.9 = (bf16[256,512]{1,0:T(8,128)(2,1)}, bf16[256,512]{1,0:T(8,128)(2,1)}, u32[]{:S(2)}, u32[]{:S(2)}) collective-permute-start(bf16[256,512]{1,0:T(8,128)(2,1)} %get-tuple-element.30), channel_id=1, source_target_pairs={{0,6},{2,0},{4,2},{6,4},{1,7},{3,1},{5,3},{7,5},{8,14},{10,8},{12,... | collective-permute-start | bytes 786440 | tf_op jit(solution)/shard_map/ppermute | solution.py:423
  115.6 4.9 %project_mine.1 = (bf16[256,512]{1,0:T(8,128)(2,1)}, bf16[256,512]{1,0:T(8,128)(2,1)}, bf16[256,512]{1,0:T(8,128)(2,1)}, bf16[256,512]{1,0:T(8,128)(2,1)}) custom-call(s32[2]{0:T(128)} %pad_add_fusion.1.place, bf16[256,1024]{1,0:T(8,128)(2,1)} %get-tuple-element.22.heads, bf16[1024,4096]{1,0:T(8,128)(2,1)} %weight.3), custom_call_target="tpu_custom_call" | custom-call | flops 1000000000 | bytes 6000000 | tf_op jit(solution)/shard_map/project_mine/pallas_call | solution.py:407
  120.5 1.5 %collective-permute-start.4 = (bf16[256,512]{1,0:T(8,128)(2,1)}, bf16[256,512]{1,0:T(8,128)(2,1)S(1)}, u32[]{:S(2)}, u32[]{:S(2)}) collective-permute-start(bf16[256,512]{1,0:T(8,128)(2,1)} %get-tuple-element.24), channel_id=1, source_target_pairs={{0,4},{2,6},{4,0},{6,2},{1,5},{3,7},{5,1},{7,3},{8,12},{10,14},{12... | collective-permute-start | bytes 786440 | tf_op jit(solution)/shard_map/ppermute | solution.py:423
  122.0 2.6 %collective-permute-start.5 = (bf16[256,512]{1,0:T(8,128)(2,1)}, bf16[256,512]{1,0:T(8,128)(2,1)S(1)}, u32[]{:S(2)}, u32[]{:S(2)}) collective-permute-start(bf16[256,512]{1,0:T(8,128)(2,1)} %get-tuple-element.25), channel_id=1, source_target_pairs={{0,2},{2,4},{4,6},{6,0},{1,3},{3,5},{5,7},{7,1},{8,10},{10,12},{12... | collective-permute-start | bytes 786440 | tf_op jit(solution)/shard_map/ppermute | solution.py:423
  124.6 3.4 %collective-permute-done.8 = bf16[256,512]{1,0:T(8,128)(2,1)S(1)} collective-permute-done((bf16[256,512]{1,0:T(8,128)(2,1)}, bf16[256,512]{1,0:T(8,128)(2,1)S(1)}, u32[]{:S(2)}, u32[]{:S(2)}) %collective-permute-start.8) | collective-permute-done | bytes 262176 | tf_op jit(solution)/shard_map/ppermute | solution.py:423
  128.1 1.1 add_convert_fusion.1
  129.2 5.1 %collective-permute-start.10 = (bf16[256,512]{1,0:T(8,128)(2,1)S(1)}, bf16[256,512]{1,0:T(8,128)(2,1)S(1)}, u32[]{:S(2)}, u32[]{:S(2)}) collective-permute-start(bf16[256,512]{1,0:T(8,128)(2,1)S(1)} %add_convert_fusion.1), channel_id=1, source_target_pairs={{0,1},{1,0},{2,3},{3,2},{4,5},{5,4},{6,7},{7,6},{8,9},{9,8},{10,11... | collective-permute-start | bytes 786440 | tf_op jit(solution)/shard_map/ppermute | solution.py:504
  134.2 3.1 %collective-permute-done.5 = bf16[256,512]{1,0:T(8,128)(2,1)S(1)} collective-permute-done((bf16[256,512]{1,0:T(8,128)(2,1)}, bf16[256,512]{1,0:T(8,128)(2,1)S(1)}, u32[]{:S(2)}, u32[]{:S(2)}) %collective-permute-start.5) | collective-permute-done | bytes 262176 | tf_op jit(solution)/shard_map/ppermute | solution.py:423
  137.4 9.2 %collective-permute-done.10 = bf16[256,512]{1,0:T(8,128)(2,1)S(1)} collective-permute-done((bf16[256,512]{1,0:T(8,128)(2,1)S(1)}, bf16[256,512]{1,0:T(8,128)(2,1)S(1)}, u32[]{:S(2)}, u32[]{:S(2)}) %collective-permute-start.10) | collective-permute-done | bytes 262176 | tf_op jit(solution)/shard_map/ppermute | solution.py:504
  (69 shorter events, 8.4 us)
Async XLA Ops:
  4.3 5.9 %copy-start.4 = (s32[64,48]{0,1:T(8,128)S(1)}, s32[64,48]{0,1:T(8,128)}, u32[]{:S(2)}) copy-start(s32[64,48]{0,1:T(8,128)} %param.25) | copy-start | bytes 36868
  4.3 5.9 %copy-start.9 = (s32[64]{0:T(128)S(1)}, s32[64]{0:T(128)}, u32[]{:S(2)}) copy-start(s32[64]{0:T(128)} %param.26) | copy-start | bytes 772
  4.3 48.2 %all-to-all-start.1 = ((bf16[16,18,2,16,128]{4,3,2,1,0:T(8,128)(2,1)}), bf16[16,18,2,16,128]{4,3,2,1,0:T(8,128)(2,1)}, u32[]{:S(2)}, u32[]{:S(2)}) async-start(bf16[16,18,2,16,128]{4,3,2,1,0:T(8,128)(2,1)} %bitcast.25), calls=%async_computation.1 | async-start | bytes 4718592 | tf_op jit(solution)/shard_map/all_to_all | solution.py:482
  10.1 6.1 %copy-start = (bf16[4,64,8,128]{3,2,1,0:T(8,128)(2,1)S(1)}, bf16[4,64,8,128]{3,2,1,0:T(8,128)(2,1)}, u32[]{:S(2)}) copy-start(bf16[4,64,8,128]{3,2,1,0:T(8,128)(2,1)} %param.14) | copy-start | bytes 1572868
  10.1 6.2 %copy-start.5 = (bf16[4,64,1,128]{3,1,2,0:T(8,128)(2,1)S(1)}, bf16[4,64,1,128]{3,1,2,0:T(8,128)(2,1)}, u32[]{:S(2)}) copy-start(bf16[4,64,1,128]{3,1,2,0:T(8,128)(2,1)} %param.16) | copy-start | bytes 196612
  10.1 6.1 %copy-start.6 = (bf16[4,64,1,128]{3,1,2,0:T(8,128)(2,1)S(1)}, bf16[4,64,1,128]{3,1,2,0:T(8,128)(2,1)}, u32[]{:S(2)}) copy-start(bf16[4,64,1,128]{3,1,2,0:T(8,128)(2,1)} %param.15) | copy-start | bytes 196612
  12.9 25.5 %collective-permute-start.1 = (s32[4224]{0:T(1024)S(1)}, s32[4224]{0:T(1024)S(1)}, u32[]{:S(2)}, u32[]{:S(2)}) collective-permute-start(s32[4224]{0:T(1024)S(1)} %concatenate.15), channel_id=1, source_target_pairs={{0,32},{32,0},{1,33},{33,1},{2,34},{34,2},{3,35},{35,3},{4,36},{36... | collective-permute-start | bytes 50696 | tf_op jit(solution)/shard_map/ppermute | solution.py:489
  16.2 33.3 %collective-permute-start = (bf16[2048,128]{1,0:T(8,128)(2,1)S(1)}, bf16[2048,128]{1,0:T(8,128)(2,1)}, u32[]{:S(2)}, u32[]{:S(2)}) collective-permute-start(bf16[2048,128]{1,0:T(8,128)(2,1)S(1)} %bitcast.36), channel_id=1, source_target_pairs={{0,32},{32,0},{1,33},{33,1},{2,34},{34,2},{3,35},{35,3},{4,36},{36... | collective-permute-start | bytes 1572872 | tf_op jit(solution)/shard_map/ppermute | solution.py:488
  38.4 11.1 %copy-start.7 = (s32[4224]{0:T(1024)}, s32[4224]{0:T(1024)S(1)}, u32[]{:S(2)}) copy-start(s32[4224]{0:T(1024)S(1)} %collective-permute-done.1.refs_1_.lists) | copy-start | bytes 50692
  52.4 47.8 %all-to-all-start = ((bf16[16,18,2,16,128]{4,3,2,1,0:T(8,128)(2,1)}), bf16[16,18,2,16,128]{4,3,2,1,0:T(8,128)(2,1)}, u32[]{:S(2)}, u32[]{:S(2)}) async-start(bf16[16,18,2,16,128]{4,3,2,1,0:T(8,128)(2,1)} %bitcast.24), calls=%async_computation | async-start | bytes 4718592 | tf_op jit(solution)/shard_map/all_to_all | solution.py:482
  64.0 36.3 %collective-permute-start.2 = (bf16[2048,128]{1,0:T(8,128)(2,1)}, bf16[2048,128]{1,0:T(8,128)(2,1)S(1)}, u32[]{:S(2)}, u32[]{:S(2)}) collective-permute-start(bf16[2048,128]{1,0:T(8,128)(2,1)} %get-tuple-element.20), channel_id=1, source_target_pairs={{0,32},{32,0},{1,33},{33,1},{2,34},{34,2},{3,35},{35,3},{4,36},{36... | collective-permute-start | bytes 1572872 | tf_op jit(solution)/shard_map/ppermute | solution.py:499
  64.4 32.9 %collective-permute-start.3 = (f32[16,128]{1,0:T(8,128)}, f32[16,128]{1,0:T(8,128)S(1)}, u32[]{:S(2)}, u32[]{:S(2)}) collective-permute-start(f32[16,128]{1,0:T(8,128)} %get-tuple-element.21), channel_id=1, source_target_pairs={{0,32},{32,0},{1,33},{33,1},{2,34},{34,2},{3,35},{35,3},{4,36},{36... | collective-permute-start | bytes 24584 | tf_op jit(solution)/shard_map/ppermute | solution.py:500
  97.3 3.0 %copy-start.8 = (f32[16,128]{1,0:T(8,128)}, f32[16,128]{1,0:T(8,128)S(1)}, u32[]{:S(2)}) copy-start(f32[16,128]{1,0:T(8,128)S(1)} %collective-permute-done.3.lse2) | copy-start | bytes 24580
  100.3 0.8 copy-start.1
  111.2 13.4 %collective-permute-start.7 = (bf16[256,512]{1,0:T(8,128)(2,1)}, bf16[256,512]{1,0:T(8,128)(2,1)S(1)}, u32[]{:S(2)}, u32[]{:S(2)}) collective-permute-start(bf16[256,512]{1,0:T(8,128)(2,1)} %get-tuple-element.28), channel_id=1, source_target_pairs={{0,4},{2,6},{4,0},{6,2},{1,5},{3,7},{5,1},{7,3},{8,12},{10,14},{12... | collective-permute-start | bytes 786440 | tf_op jit(solution)/shard_map/ppermute | solution.py:423
  113.6 14.4 %collective-permute-start.8 = (bf16[256,512]{1,0:T(8,128)(2,1)}, bf16[256,512]{1,0:T(8,128)(2,1)S(1)}, u32[]{:S(2)}, u32[]{:S(2)}) collective-permute-start(bf16[256,512]{1,0:T(8,128)(2,1)} %get-tuple-element.29), channel_id=1, source_target_pairs={{0,2},{2,4},{4,6},{6,0},{1,3},{3,5},{5,7},{7,1},{8,10},{10,12},{12... | collective-permute-start | bytes 786440 | tf_op jit(solution)/shard_map/ppermute | solution.py:423
  113.6 14.5 %collective-permute-start.9 = (bf16[256,512]{1,0:T(8,128)(2,1)}, bf16[256,512]{1,0:T(8,128)(2,1)}, u32[]{:S(2)}, u32[]{:S(2)}) collective-permute-start(bf16[256,512]{1,0:T(8,128)(2,1)} %get-tuple-element.30), channel_id=1, source_target_pairs={{0,6},{2,0},{4,2},{6,4},{1,7},{3,1},{5,3},{7,5},{8,14},{10,8},{12,... | collective-permute-start | bytes 786440 | tf_op jit(solution)/shard_map/ppermute | solution.py:423
  115.6 12.5 %copy-start.2 = (bf16[256,512]{1,0:T(8,128)(2,1)S(1)}, bf16[256,512]{1,0:T(8,128)(2,1)}, u32[]{:S(2)}) copy-start(bf16[256,512]{1,0:T(8,128)(2,1)} %get-tuple-element.27) | copy-start | bytes 786436
  120.5 26.1 %copy-start.3 = (bf16[256,512]{1,0:T(8,128)(2,1)S(1)}, bf16[256,512]{1,0:T(8,128)(2,1)}, u32[]{:S(2)}) copy-start(bf16[256,512]{1,0:T(8,128)(2,1)} %get-tuple-element.23) | copy-start | bytes 786436
  120.5 13.8 %collective-permute-start.4 = (bf16[256,512]{1,0:T(8,128)(2,1)}, bf16[256,512]{1,0:T(8,128)(2,1)S(1)}, u32[]{:S(2)}, u32[]{:S(2)}) collective-permute-start(bf16[256,512]{1,0:T(8,128)(2,1)} %get-tuple-element.24), channel_id=1, source_target_pairs={{0,4},{2,6},{4,0},{6,2},{1,5},{3,7},{5,1},{7,3},{8,12},{10,14},{12... | collective-permute-start | bytes 786440 | tf_op jit(solution)/shard_map/ppermute | solution.py:423
  122.0 15.4 %collective-permute-start.5 = (bf16[256,512]{1,0:T(8,128)(2,1)}, bf16[256,512]{1,0:T(8,128)(2,1)S(1)}, u32[]{:S(2)}, u32[]{:S(2)}) collective-permute-start(bf16[256,512]{1,0:T(8,128)(2,1)} %get-tuple-element.25), channel_id=1, source_target_pairs={{0,2},{2,4},{4,6},{6,0},{1,3},{3,5},{5,7},{7,1},{8,10},{10,12},{12... | collective-permute-start | bytes 786440 | tf_op jit(solution)/shard_map/ppermute | solution.py:423
  124.6 12.8 %collective-permute-start.6 = (bf16[256,512]{1,0:T(8,128)(2,1)}, bf16[256,512]{1,0:T(8,128)(2,1)S(1)}, u32[]{:S(2)}, u32[]{:S(2)}) collective-permute-start(bf16[256,512]{1,0:T(8,128)(2,1)} %get-tuple-element.26), channel_id=1, source_target_pairs={{0,6},{2,0},{4,2},{6,4},{1,7},{3,1},{5,3},{7,5},{8,14},{10,8},{12,... | collective-permute-start | bytes 786440 | tf_op jit(solution)/shard_map/ppermute | solution.py:423
  129.2 17.4 %collective-permute-start.10 = (bf16[256,512]{1,0:T(8,128)(2,1)S(1)}, bf16[256,512]{1,0:T(8,128)(2,1)S(1)}, u32[]{:S(2)}, u32[]{:S(2)}) collective-permute-start(bf16[256,512]{1,0:T(8,128)(2,1)S(1)} %add_convert_fusion.1), channel_id=1, source_target_pairs={{0,1},{1,0},{2,3},{3,2},{4,5},{5,4},{6,7},{7,6},{8,9},{9,8},{10,11... | collective-permute-start | bytes 786440 | tf_op jit(solution)/shard_map/ppermute | solution.py:504

commit v5 on v4

--- a/solution.py
+++ b/solution.py
@@ -26,7 +26,8 @@
 WIDE = 16
 WIDE_CHUNKS = 4
 POSITIONS = WIDE * WIDE_CHUNKS
-LIST = ROWS * (POSITIONS + 2)
+LIST = ROWS * (POSITIONS + 4)
+LIST_ROWS = 40
 TEAM = 4
 TEAMS = ROWS // TEAM
 LANES = TEAM * QROWS
@@ -131,14 +132,17 @@
     team_row = (lane // GROUPS) % TEAM
     step = lane // (TEAM * GROUPS)
 
+    def entry(i):
+        return lists[i // DH, i % DH] if isinstance(i, int) else lists[i >> 7, i & 127]
+
     def load(r, first, n, which):
-        return [kv[lists[r * POSITIONS + first + p], which] for p in range(n)]
+        return [kv[entry(r * POSITIONS + first + p), which] for p in range(n)]
 
     def count(r):
-        return lists[ROWS * POSITIONS + r]
+        return entry(ROWS * POSITIONS + r)
 
     def tokens(r):
-        return lists[ROWS * POSITIONS + ROWS + r]
+        return entry(ROWS * (POSITIONS + 1) + r)
 
     def team(t, g):
         first = t * ROWS * GROUPS + g * TEAM * GROUPS
@@ -187,34 +191,8 @@
     for g in range(TEAMS):
         narrow(g)
 
-    def wide(r):
-        width = WIDE * PAGE
-        chunks = (count(r) + WIDE - 1) // WIDE
+    def put(r, product, m, total, safe):
         g, i = r // TEAM, r % TEAM
-
-        def first_pass(c, m):
-            keys = jnp.concatenate(load(r, c * WIDE, WIDE, 0), axis=0)
-            s = mask(dot_nt(keys, queries(g)), c * width, tokens(r))
-            scores[c] = s
-            return jnp.maximum(m, jnp.max(s, axis=0, keepdims=True))
-
-        m = lax.fori_loop(0, chunks, first_pass, jnp.full((1, LANES), -1e30, jnp.float32))
-
-        def second_pass(c, total):
-            e = jnp.exp(scores[c] - m)
-            scores[c] = e
-            return total + jnp.sum(e, axis=0, keepdims=True)
-
-        total = lax.fori_loop(0, chunks, second_pass, jnp.zeros((1, LANES), jnp.float32))
-        safe = jnp.maximum(total, 1e-30)
-        inverse = 1.0 / safe
-
-        def third_pass(c, product):
-            weights = (scores[c] * inverse).T.astype(jnp.bfloat16)
-            values = jnp.concatenate(load(r, c * WIDE, WIDE, 1), axis=0)
-            return product + jnp.dot(weights, values, preferred_element_type=jnp.float32)
-
-        product = lax.fori_loop(0, chunks, third_pass, jnp.zeros((LANES, DH), jnp.float32))
         size = TEAM * GROUPS
         owner = lax.broadcasted_iota(jnp.int32, (size, DH), 0) // GROUPS
         for t in range(STEPS):
@@ -223,18 +201,61 @@
         new = jnp.where(total > 0.0, m + jnp.log(safe), -1e30)
         lse[pl.ds(g, 1), :] = jnp.where(team_row == i, new, lse[pl.ds(g, 1), :])
 
-    def wide_body(r, carry):
-        pl.when(count(r) > NARROW)(lambda: wide(r))
+    def chunk_scores(r, c):
+        keys = jnp.concatenate(load(r, c * WIDE, WIDE, 0), axis=0)
+        return mask(dot_nt(keys, queries(r // TEAM)), c * WIDE * PAGE, tokens(r))
+
+    def chunk_out(r, c, weights):
+        values = jnp.concatenate(load(r, c * WIDE, WIDE, 1), axis=0)
+        return jnp.dot(weights.T.astype(jnp.bfloat16), values, preferred_element_type=jnp.float32)
+
+    def one_chunk(r):
+        s = chunk_scores(r, 0)
+        m = jnp.maximum(jnp.max(s, axis=0, keepdims=True), -1e30)
+        e = jnp.exp(s - m)
+        total = jnp.sum(e, axis=0, keepdims=True)
+        safe = jnp.maximum(total, 1e-30)
+        put(r, chunk_out(r, 0, e * (1.0 / safe)), m, total, safe)
+
+    def more_chunks(r):
+        chunks = (count(r) + WIDE - 1) // WIDE
+
+        def first_pass(c, m):
+            s = chunk_scores(r, c)
+            scores[c] = s
+            return jnp.maximum(m, jnp.max(s, axis=0, keepdims=True))
+
+        m = lax.fori_loop(0, chunks, first_pass, jnp.full((1, LANES), -1e30, jnp.float32))
+
+        def second_pass(c, total):
+            e = jnp.exp(scores[c] - m)
+            scores[c] = e
+            return total + jnp.sum(e, axis=0, keepdims=True)
+
+        total = lax.fori_loop(0, chunks, second_pass, jnp.zeros((1, LANES), jnp.float32))
+        safe = jnp.maximum(total, 1e-30)
+        inverse = 1.0 / safe
+
+        def third_pass(c, product):
+            return product + chunk_out(r, c, scores[c] * inverse)
+
+        product = lax.fori_loop(0, chunks, third_pass, jnp.zeros((LANES, DH), jnp.float32))
+        put(r, product, m, total, safe)
+
+    def wide_body(k, carry):
+        r = entry(ROWS * (POSITIONS + 2) + k)
+        pl.when(count(r) <= WIDE)(lambda: one_chunk(r))
+        pl.when(count(r) > WIDE)(lambda: more_chunks(r))
         return carry
 
-    lax.fori_loop(0, ROWS, wide_body, 0)
+    lax.fori_loop(0, entry(ROWS * (POSITIONS + 3)), wide_body, 0)
 
 
 QUERIES = pltpu.VMEM((ROWS * QROWS, DH), jnp.bfloat16)
 SCORES = pltpu.VMEM((WIDE_CHUNKS, WIDE * PAGE, LANES), jnp.float32)
 RESULT = pltpu.VMEM((ROWS * QROWS, DH), jnp.float32)
 LSE = pltpu.VMEM((TEAMS, LANES), jnp.float32)
-LISTS = pltpu.SMEM((LIST,), jnp.int32)
+LISTS = pltpu.SMEM((LIST_ROWS, DH), jnp.int32)
 
 
 def pages_scratch(n):
@@ -245,7 +266,7 @@
     return jnp.zeros((2, PAGE, DH), jnp.bfloat16)
 
 
-def attend_local_kernel(lists, q, pool_k, pool_v, fresh, out, lse, lists_s, q_s, kv, scores, sems):
+def attend_local_kernel(lists, q, pool_k, pool_v, fresh, after, out, lse, lists_s, q_s, kv, scores, sems):
     copies = start_all(
         [
             (lists, lists_s),
@@ -261,44 +282,66 @@
     attention(True, lists_s, q_s, kv, out, lse, scores)
 
 
-def attend_local(lists, q, pool_k, pool_v, fresh):
+def attend_local(lists, q, pool_k, pool_v, fresh, after):
     return pl.pallas_call(
         attend_local_kernel,
         out_shape=(
             jax.ShapeDtypeStruct((ROWS * QROWS, DH), jnp.float32),
             jax.ShapeDtypeStruct((TEAMS, LANES), jnp.float32),
         ),
-        in_specs=[ANY] * 5,
+        in_specs=[ANY] * 6,
         out_specs=(VMEM, VMEM),
         scratch_shapes=[LISTS, QUERIES, pages_scratch(POOL + ROWS), SCORES, pltpu.SemaphoreType.DMA((5,))],
         compiler_params=PARAMS,
-        cost_estimate=pl.CostEstimate(flops=10**9, bytes_accessed=10**7, transcendentals=10**6),
+        cost_estimate=pl.CostEstimate(flops=10**11, bytes_accessed=10**8, transcendentals=10**6),
         name="attend_local",
-    )(lists, q, pool_k, pool_v, fresh)
-
-
-def attend_far_kernel(lists, q, recv, out, lse, lists_s, q_s, kv, result, scores, sems):
-    copies = start_all([(lists, lists_s), (q, q_s), (recv, kv.at[pl.ds(1, RECV)])], sems)
+    )(lists, q, pool_k, pool_v, fresh, after)
+
+
+def attend_far_kernel(letter, recv, out, lse, lists_s, lists_v, coded, q_s, kv, result, scores, sems):
+    copies = start_all(
+        [
+            (letter.at[pl.ds(ROWS * QROWS, 2 * LIST_ROWS)], coded),
+            (letter.at[pl.ds(0, ROWS * QROWS)], q_s),
+            (recv, kv.at[pl.ds(1, RECV)]),
+        ],
+        sems,
+    )
     kv[0] = blank_page()
-    wait_all(copies)
+    copies[0].wait()
+    numbers = coded[...].astype(jnp.float32)
+    lists_v[...] = (numbers[:LIST_ROWS] * 256.0 + numbers[LIST_ROWS:]).astype(jnp.int32)
+    lists_copy = pltpu.make_async_copy(lists_v, lists_s, sems.at[3])
+    lists_copy.start()
+    lists_copy.wait()
+    wait_all(copies[1:])
     attention(False, lists_s, q_s, kv, result, lse, scores)
     out[...] = result[...].astype(jnp.bfloat16)
 
 
-def attend_far(lists, q, recv):
+def attend_far(letter, recv):
     return pl.pallas_call(
         attend_far_kernel,
         out_shape=(
             jax.ShapeDtypeStruct((ROWS * QROWS, DH), jnp.bfloat16),
             jax.ShapeDtypeStruct((TEAMS, LANES), jnp.float32),
         ),
-        in_specs=[ANY] * 3,
+        in_specs=[ANY] * 2,
         out_specs=(VMEM, VMEM),
-        scratch_shapes=[LISTS, QUERIES, pages_scratch(RECV), RESULT, SCORES, pltpu.SemaphoreType.DMA((3,))],
+        scratch_shapes=[
+            LISTS,
+            pltpu.VMEM((LIST_ROWS, DH), jnp.int32),
+            pltpu.VMEM((2 * LIST_ROWS, DH), jnp.bfloat16),
+            QUERIES,
+            pages_scratch(RECV),
+            RESULT,
+            SCORES,
+            pltpu.SemaphoreType.DMA((4,)),
+        ],
         compiler_params=PARAMS,
-        cost_estimate=pl.CostEstimate(flops=10**9, bytes_accessed=10**7, transcendentals=10**6),
+        cost_estimate=pl.CostEstimate(flops=10**11, bytes_accessed=10**8, transcendentals=10**6),
         name="attend_far",
-    )(lists, q, recv)
+    )(letter, recv)
 
 
 SHIFTS = (2, 1, 3, 0)
@@ -345,24 +388,14 @@
 
 def finish_kernel(place, lists, q, recv, o1, lse1, o2, lse2, weight, heads, *refs):
     outs, refs = refs[:TILES], refs[TILES:]
-    lists_s, q_s, kv, o1_s, lse1_s, o2_s, lse2_s, lse3, result, scores, sems, w, terms, w_sems, out_sems = refs
-    copies = start_all(
-        [
-            (lists, lists_s),
-            (q, q_s),
-            (recv, kv.at[pl.ds(1, RECV)]),
-            (lse1, lse1_s),
-            (lse2, lse2_s),
-            (o1, o1_s),
-            (o2, o2_s),
-        ],
-        sems,
-    )
+    lists_s, q_s, kv, o1_s, lse1_s, o2_s, lse2_s, lse3, result, scores, sems, part_sems, w, terms, w_sems, out_sems = refs
+    copies = start_all([(lists, lists_s), (q, q_s), (recv, kv.at[pl.ds(1, RECV)])], sems)
+    parts = start_all([(lse1, lse1_s), (lse2, lse2_s), (o1, o1_s), (o2, o2_s)], part_sems)
     kv[0] = blank_page()
-    wait_all(copies[:3])
+    wait_all(copies)
     loads = start_tiles(place, 1, weight, w, w_sems)
     attention(False, lists_s, q_s, kv, result, lse3, scores)
-    wait_all(copies[3:])
+    wait_all(parts)
 
     top = jnp.maximum(jnp.maximum(lse1_s[...], lse2_s[...]), lse3[...])
     parts = [jnp.exp(x[...] - top) for x in (lse1_s, lse2_s, lse3)]
@@ -390,7 +423,8 @@
         out_specs=(VMEM,) + (ANY,) * TILES,
         scratch_shapes=[
             LISTS, QUERIES, pages_scratch(RECV), RESULT, LSE, QUERIES, LSE, LSE, RESULT, SCORES,
-            pltpu.SemaphoreType.DMA((7,)),
+            pltpu.SemaphoreType.DMA((3,)),
+            pltpu.SemaphoreType.DMA((4,)),
         ] + PROJECT_SCRATCH,
         compiler_params=PARAMS,
         name="attend_merge_project",
@@ -439,7 +473,14 @@
         idx = jnp.concatenate([fresh, idx], axis=1)
         count, tokens = count + 1, tokens + PAGE
     idx = jnp.pad(idx, ((0, 0), (0, POSITIONS - idx.shape[1])))
-    return jnp.concatenate([idx.reshape(-1), count, tokens])
+    wide = count > NARROW
+    place_of = jnp.cumsum(wide.astype(jnp.int32)) - 1
+    row = jnp.arange(ROWS, dtype=jnp.int32)
+    picked = wide[None, :] & (place_of[None, :] == row[:, None])
+    wide_rows = jnp.sum(jnp.where(picked, row[None, :], 0), axis=1)
+    wide_count = jnp.broadcast_to(jnp.sum(wide.astype(jnp.int32)), (ROWS,))
+    spare = jnp.zeros((LIST_ROWS * DH - LIST,), jnp.int32)
+    return jnp.concatenate([idx.reshape(-1), count, tokens, wide_rows, wide_count, spare]).reshape(LIST_ROWS, DH)
 
 
 def local_lists(table, lengths):
@@ -455,6 +496,10 @@
     group = (source >> 3) * 4 + (source & 3)
     here = (table >= POOL) & (((source >> 2) & 1) == half)
     return page_lists(here, 1 + group * SLOTS + rank, lengths)
+
+
+def as_rows(lists):
+    return jnp.concatenate([lists >> 8, lists & 255], axis=0).astype(jnp.bfloat16)
 
 
 def per_device(
@@ -485,17 +530,18 @@
     pages = (page(prompt_keys), page(prompt_values), page(moved_keys), page(moved_values))
     far_recv = exchange(pack((1 - half)[None], prompt_dest, moved_dest, *pages))
     q = queries.reshape(ROWS * QROWS, DH)
-    far_q = lax.ppermute(q, "izh", swap)
-    far_lists = lax.ppermute(arrived_lists(block_table, context_len, 1 - half), "izh", swap)
+    letter = jnp.concatenate([q, as_rows(arrived_lists(block_table, context_len, 1 - half))], axis=0)
     near_lists = arrived_lists(block_table, context_len, half)
-
+    near_send = pack(half[None], prompt_dest, moved_dest, *pages, near_lists)
     fresh = jnp.stack([new_keys, new_values], axis=0).reshape(2, STEPS, ROWS, DH).transpose(2, 0, 1, 3)
     fresh = jnp.pad(fresh, ((0, 0), (0, 0), (0, PAGE - STEPS), (0, 0)))
-    o1, lse1 = attend_local(local_lists(block_table, context_len), q, page(pool_keys), page(pool_values), fresh)
-    near_send = pack(half[None], prompt_dest, moved_dest, *pages, lse1)
-    near_recv = exchange(gate(near_send, far_q, far_lists, near_lists))
-
-    o2, lse2 = attend_far(far_lists, far_q, far_recv)
+    local_pages = (page(pool_keys), page(pool_values), fresh)
+    local = local_lists(block_table, context_len)
+    o1, lse1 = attend_local(local, q, *local_pages, near_send)
+    letter = lax.ppermute(gate(letter, lse1), "izh", swap)
+    near_recv = exchange(near_send)
+
+    o2, lse2 = attend_far(letter, far_recv)
     o2 = lax.ppermute(o2, "izh", swap)
     lse2 = lax.ppermute(lse2, "izh", swap)
 

time: 148 us -> 147 us (level)
  waiting for transfers between devices: 70.8 us -> 67.1 us
  other arithmetic: 4.64 us -> 7.91 us
  local copies, waits for them, and re-layouts: 4.22 us -> 7.26 us
  Pallas kernels: 35.9 us -> 32.9 us
    all_to_all x2, waiting for transfers between devices: 6.01 us -> 42.2 us  [exchange(): recv = lax.all_to_all(send, HALF, split_axis=0, concat_axis=0, tiled=True)]
    ppermute x1, waiting for transfers between devices: 29.7 us -> 0.01 us  [per_device(): lse2 = lax.ppermute(lse2, 'izh', swap)]
    ppermute x2 -> x1, waiting for transfers between devices: 19.4 us -> 8.49 us  [per_device(): letter = lax.ppermute(gate(letter, lse1), 'izh', swap)]
    broadcast_in_dim x0 -> x3, local copies, waits for them, and re-layouts: none -> 1.89 us  [page_lists(): wide_count = jnp.broadcast_to(jnp.sum(wide.astype(jnp.int32)), (ROWS,))]
    reduce_sum x0 -> x5, other arithmetic: none -> 1.72 us  [the longest x2 1.37 us: page_lists(): wide_count = jnp.broadcast_to(jnp.sum(wide.astype(jnp.int32)), (ROWS,))]
    ppermute x2 -> x1, starting transfers between devices: 3.39 us -> 3.78 us  [per_device(): letter = lax.ppermute(gate(letter, lse1), 'izh', swap)]
  transfers between devices with their start and end apart: 13 -> 12, of which waited for: 9 -> 7; matrix products, arithmetic and copies ran while one was open for 5% -> 9% of each run, Pallas kernels for 15% -> 13%
where the time goes in v5:
time: 147 us; the launch traced here: 146 us
  waiting for transfers between devices  67.1 us (46%)
  Pallas kernels  32.9 us (22%)
  starting transfers between devices  30.2 us (21%)
  other arithmetic  7.91 us (5%)
  local copies, waits for them, and re-layouts  7.26 us (5%)
    all_to_all x2, waiting for transfers between devices, exchange(): recv = lax.all_to_all(send, HALF, split_axis=0, concat_axis=0, tiled=True)  42.2 us
    all_to_all x2, starting transfers between devices, exchange(): recv = lax.all_to_all(send, HALF, split_axis=0, concat_axis=0, tiled=True)  10.3 us
    pallas_call x1, Pallas kernels, finish(): pl.pallas_call(finish_kernel, out_shape=(heads,) + TERMS, in_specs=[SMEM]...  9.41 us
    ppermute x6, starting transfers between devices, sum_over_y(): moved = lax.ppermute(term, 'ty', [(i, (i + shift) % 4) for i in range(4)])  8.51 us
    ppermute x1, waiting for transfers between devices, per_device(): letter = lax.ppermute(gate(letter, lse1), 'izh', swap)  8.49 us
    pallas_call x2, Pallas kernels, pack(): pl.pallas_call(pack_kernel, out_shape=jax.ShapeDtypeStruct((RECV, 2, PAGE...  8.47 us
    ppermute x1, waiting for transfers between devices, per_device(): other = lax.ppermute(sum_over_y(terms).astype(jnp.bfloat16), 'tz', swap)  8.34 us
    ppermute x6, waiting for transfers between devices, sum_over_y(): moved = lax.ppermute(term, 'ty', [(i, (i + shift) % 4) for i in range(4)])  7.98 us
  transfers between devices with their start and end apart: 12, of which 7 were waited for; matrix products, arithmetic and copies ran while one was open for 9% of the time, Pallas kernels for 13%

profile of v5, /device:TPU:8, one launch (start us, length us, event | category | flops | bytes accessed | tf_op | source)
XLA Modules:
  0.0 145.7 jit_solution(484799959423676467)
XLA Ops:
  0.0 4.2 %pack_pages.3 = bf16[288,2,16,128]{3,2,1,0:T(8,128)(2,1)} custom-call(s32[1]{0:T(128)} %bitcast.23.half, s32[192]{0:T(256)} %pdest.3, s32[96]{0:T(128)} %mdest.3, bf16[192,16,128]{2,1,0:T(8,128)(2,1)} %bitcast.37, bf16[192,16,128]{2,1,0:T(8,128)(2,1)} %bitcast.39, bf16[96,16,128]{2,1,0:T(8,128)(2,1)} %bitcast.44, bf16[96,16,128]{2,1,0:T(8,128)(2,1)} %bitcast.46), custom_call_target="tpu_custom_call" | custom-call | flops 1000000 | bytes 10000000 | tf_op jit(solution)/shard_map/pack_pages/pallas_call | solution.py:94
  4.3 5.8 %all-to-all-start.1 = ((bf16[16,18,2,16,128]{4,3,2,1,0:T(8,128)(2,1)}), bf16[16,18,2,16,128]{4,3,2,1,0:T(8,128)(2,1)}, u32[]{:S(2)}, u32[]{:S(2)}) async-start(bf16[16,18,2,16,128]{4,3,2,1,0:T(8,128)(2,1)} %bitcast.36), calls=%async_computation.1 | async-start | bytes 4718592 | tf_op jit(solution)/shard_map/all_to_all | solution.py:527
  13.6 1.0 select_reduce_fusion
  15.4 0.9 pad.17.fresh
  17.7 4.2 %pack_pages.2.after = bf16[288,2,16,128]{3,2,1,0:T(8,128)(2,1)} custom-call(s32[1]{0:T(128)} %bitcast.5.half, s32[192]{0:T(256)} %pdest.3, s32[96]{0:T(128)} %mdest.3, bf16[192,16,128]{2,1,0:T(8,128)(2,1)} %bitcast.38, bf16[192,16,128]{2,1,0:T(8,128)(2,1)} %bitcast.40, bf16[96,16,128]{2,1,0:T(8,128)(2,1)} %bitcast.45, bf16[96,16,128]{2,1,0:T(8,128)(2,1)} %bitcast.47, ...), custom_call_target="tpu_custom_call" | custom-call | flops 1000000 | bytes 10000000 | tf_op jit(solution)/shard_map/pack_pages/pallas_call | solution.py:94
  23.3 5.3 %attend_local.1 = (f32[2048,128]{1,0:T(8,128)}, f32[16,128]{1,0:T(8,128)}) custom-call(s32[40,128]{1,0:T(8,128)} %bitcast.50, bf16[2048,128]{1,0:T(8,128)(2,1)} %bitcast.41, bf16[192,16,128]{2,1,0:T(8,128)(2,1)} %bitcast.51, bf16[192,16,128]{2,1,0:T(8,128)(2,1)} %bitcast.52, bf16[64,2,16,128]{3,2,1,0:T(8,128)(2,1)} %pad.17.fresh, ...), custom_call_target="tpu_custom_call" | custom-call | flops 99999997952 | bytes 100000000 | tf_op jit(solution)/shard_map/attend_local/pallas_call | solution.py:286
  30.8 3.8 %collective-permute-start = (bf16[2128,128]{1,0:T(8,128)(2,1)}, bf16[2128,128]{1,0:T(8,128)(2,1)S(1)}, u32[]{:S(2)}, u32[]{:S(2)}) collective-permute-start(bf16[2128,128]{1,0:T(8,128)(2,1)} %gate.1), channel_id=1, source_target_pairs={{0,32},{32,0},{1,33},{33,1},{2,34},{34,2},{3,35},{35,3},{4,36},{36... | collective-permute-start | bytes 1634312 | tf_op jit(solution)/shard_map/ppermute | solution.py:541
  34.6 11.5 %all-to-all-done.1 = bf16[16,18,2,16,128]{4,3,2,1,0:T(8,128)(2,1)} async-done(((bf16[16,18,2,16,128]{4,3,2,1,0:T(8,128)(2,1)}), bf16[16,18,2,16,128]{4,3,2,1,0:T(8,128)(2,1)}, u32[]{:S(2)}, u32[]{:S(2)}) %all-to-all-start.1) | async-done | bytes 2359328 | tf_op jit(solution)/shard_map/all_to_all | solution.py:527
  46.0 4.4 %all-to-all-start = ((bf16[16,18,2,16,128]{4,3,2,1,0:T(8,128)(2,1)}), bf16[16,18,2,16,128]{4,3,2,1,0:T(8,128)(2,1)}, u32[]{:S(2)}, u32[]{:S(2)}) async-start(bf16[16,18,2,16,128]{4,3,2,1,0:T(8,128)(2,1)} %bitcast.10), calls=%async_computation | async-start | bytes 4718592 | tf_op jit(solution)/shard_map/all_to_all | solution.py:527
  50.5 8.5 %collective-permute-done.letter = bf16[2128,128]{1,0:T(8,128)(2,1)S(1)} collective-permute-done((bf16[2128,128]{1,0:T(8,128)(2,1)}, bf16[2128,128]{1,0:T(8,128)(2,1)S(1)}, u32[]{:S(2)}, u32[]{:S(2)}) %collective-permute-start) | collective-permute-done | bytes 544800 | tf_op jit(solution)/shard_map/ppermute | solution.py:541
  59.8 4.9 %attend_far.1 = (bf16[2048,128]{1,0:T(8,128)(2,1)}, f32[16,128]{1,0:T(8,128)}) custom-call(bf16[2128,128]{1,0:T(8,128)(2,1)} %copy-done.9, bf16[288,2,16,128]{3,2,1,0:T(8,128)(2,1)} %bitcast.25.recv), custom_call_target="tpu_custom_call" | custom-call | flops 99999997952 | bytes 100000000 | tf_op jit(solution)/shard_map/attend_far/pallas_call | solution.py:323
  64.8 2.9 %collective-permute-start.2 = (f32[16,128]{1,0:T(8,128)}, f32[16,128]{1,0:T(8,128)S(1)}, u32[]{:S(2)}, u32[]{:S(2)}) collective-permute-start(f32[16,128]{1,0:T(8,128)} %get-tuple-element.21), channel_id=1, source_target_pairs={{0,32},{32,0},{1,33},{33,1},{2,34},{34,2},{3,35},{35,3},{4,36},{36... | collective-permute-start | bytes 24584 | tf_op jit(solution)/shard_map/ppermute | solution.py:546
  68.4 30.8 %all-to-all-done = bf16[16,18,2,16,128]{4,3,2,1,0:T(8,128)(2,1)} async-done(((bf16[16,18,2,16,128]{4,3,2,1,0:T(8,128)(2,1)}), bf16[16,18,2,16,128]{4,3,2,1,0:T(8,128)(2,1)}, u32[]{:S(2)}, u32[]{:S(2)}) %all-to-all-start) | async-done | bytes 2359328 | tf_op jit(solution)/shard_map/all_to_all | solution.py:527
  99.9 9.4 %attend_merge_project.1 = (bf16[256,1024]{1,0:T(8,128)(2,1)}, bf16[256,512]{1,0:T(8,128)(2,1)}, bf16[256,512]{1,0:T(8,128)(2,1)}, bf16[256,512]{1,0:T(8,128)(2,1)}, bf16[256,512]{1,0:T(8,128)(2,1)}) custom-call(s32[2]{0:T(128)} %pad_add_fusion.1.place, s32[40,128]{1,0:T(8,128)} %bitcast.49, bf16[2048,128]{1,0:T(8,128)(2,1)} %bitcast.42, ...), custom_call_target="tpu_custom_call" | custom-call | tf_op jit(solution)/shard_map/attend_merge_project/pallas_call | solution.py:419
  109.4 2.4 %collective-permute-start.6 = (bf16[256,512]{1,0:T(8,128)(2,1)}, bf16[256,512]{1,0:T(8,128)(2,1)S(1)}, u32[]{:S(2)}, u32[]{:S(2)}) collective-permute-start(bf16[256,512]{1,0:T(8,128)(2,1)} %get-tuple-element.28), channel_id=1, source_target_pairs={{0,4},{2,6},{4,0},{6,2},{1,5},{3,7},{5,1},{7,3},{8,12},{10,14},{12... | collective-permute-start | bytes 786440 | tf_op jit(solution)/shard_map/ppermute | solution.py:457
  111.7 2.0 %collective-permute-start.8 = (bf16[256,512]{1,0:T(8,128)(2,1)}, bf16[256,512]{1,0:T(8,128)(2,1)}, u32[]{:S(2)}, u32[]{:S(2)}) collective-permute-start(bf16[256,512]{1,0:T(8,128)(2,1)} %get-tuple-element.30), channel_id=1, source_target_pairs={{0,6},{2,0},{4,2},{6,4},{1,7},{3,1},{5,3},{7,5},{8,14},{10,8},{12,... | collective-permute-start | bytes 786440 | tf_op jit(solution)/shard_map/ppermute | solution.py:457
  113.8 4.9 %project_mine.1 = (bf16[256,512]{1,0:T(8,128)(2,1)}, bf16[256,512]{1,0:T(8,128)(2,1)}, bf16[256,512]{1,0:T(8,128)(2,1)}, bf16[256,512]{1,0:T(8,128)(2,1)}) custom-call(s32[2]{0:T(128)} %pad_add_fusion.1.place, bf16[256,1024]{1,0:T(8,128)(2,1)} %get-tuple-element.22.heads, bf16[1024,4096]{1,0:T(8,128)(2,1)} %weight.3), custom_call_target="tpu_custom_call" | custom-call | flops 1000000000 | bytes 6000000 | tf_op jit(solution)/shard_map/project_mine/pallas_call | solution.py:441
  118.7 1.5 %collective-permute-start.3 = (bf16[256,512]{1,0:T(8,128)(2,1)}, bf16[256,512]{1,0:T(8,128)(2,1)S(1)}, u32[]{:S(2)}, u32[]{:S(2)}) collective-permute-start(bf16[256,512]{1,0:T(8,128)(2,1)} %get-tuple-element.24), channel_id=1, source_target_pairs={{0,4},{2,6},{4,0},{6,2},{1,5},{3,7},{5,1},{7,3},{8,12},{10,14},{12... | collective-permute-start | bytes 786440 | tf_op jit(solution)/shard_map/ppermute | solution.py:457
  120.1 2.6 %collective-permute-start.4 = (bf16[256,512]{1,0:T(8,128)(2,1)}, bf16[256,512]{1,0:T(8,128)(2,1)S(1)}, u32[]{:S(2)}, u32[]{:S(2)}) collective-permute-start(bf16[256,512]{1,0:T(8,128)(2,1)} %get-tuple-element.25), channel_id=1, source_target_pairs={{0,2},{2,4},{4,6},{6,0},{1,3},{3,5},{5,7},{7,1},{8,10},{10,12},{12... | collective-permute-start | bytes 786440 | tf_op jit(solution)/shard_map/ppermute | solution.py:457
  122.8 3.3 %collective-permute-done.7 = bf16[256,512]{1,0:T(8,128)(2,1)S(1)} collective-permute-done((bf16[256,512]{1,0:T(8,128)(2,1)}, bf16[256,512]{1,0:T(8,128)(2,1)S(1)}, u32[]{:S(2)}, u32[]{:S(2)}) %collective-permute-start.7) | collective-permute-done | bytes 262176 | tf_op jit(solution)/shard_map/ppermute | solution.py:457
  126.2 1.1 add_convert_fusion.1
  127.3 4.7 %collective-permute-start.9 = (bf16[256,512]{1,0:T(8,128)(2,1)S(1)}, bf16[256,512]{1,0:T(8,128)(2,1)S(1)}, u32[]{:S(2)}, u32[]{:S(2)}) collective-permute-start(bf16[256,512]{1,0:T(8,128)(2,1)S(1)} %add_convert_fusion.1), channel_id=1, source_target_pairs={{0,1},{1,0},{2,3},{3,2},{4,5},{5,4},{6,7},{7,6},{8,9},{9,8},{10,11... | collective-permute-start | bytes 786440 | tf_op jit(solution)/shard_map/ppermute | solution.py:550
  131.9 4.6 %collective-permute-done.4 = bf16[256,512]{1,0:T(8,128)(2,1)S(1)} collective-permute-done((bf16[256,512]{1,0:T(8,128)(2,1)}, bf16[256,512]{1,0:T(8,128)(2,1)S(1)}, u32[]{:S(2)}, u32[]{:S(2)}) %collective-permute-start.4) | collective-permute-done | bytes 262176 | tf_op jit(solution)/shard_map/ppermute | solution.py:457
  136.5 8.3 %collective-permute-done.9 = bf16[256,512]{1,0:T(8,128)(2,1)S(1)} collective-permute-done((bf16[256,512]{1,0:T(8,128)(2,1)S(1)}, bf16[256,512]{1,0:T(8,128)(2,1)S(1)}, u32[]{:S(2)}, u32[]{:S(2)}) %collective-permute-start.9) | collective-permute-done | bytes 262176 | tf_op jit(solution)/shard_map/ppermute | solution.py:550
  (88 shorter events, 12.3 us)
Async XLA Ops:
  4.3 5.9 %copy-start.4 = (s32[64,48]{0,1:T(8,128)S(1)}, s32[64,48]{0,1:T(8,128)}, u32[]{:S(2)}) copy-start(s32[64,48]{0,1:T(8,128)} %param.25) | copy-start | bytes 36868
  4.3 5.9 %copy-start.8 = (s32[64]{0:T(128)S(1)}, s32[64]{0:T(128)}, u32[]{:S(2)}) copy-start(s32[64]{0:T(128)} %param.26) | copy-start | bytes 772
  4.3 41.8 %all-to-all-start.1 = ((bf16[16,18,2,16,128]{4,3,2,1,0:T(8,128)(2,1)}), bf16[16,18,2,16,128]{4,3,2,1,0:T(8,128)(2,1)}, u32[]{:S(2)}, u32[]{:S(2)}) async-start(bf16[16,18,2,16,128]{4,3,2,1,0:T(8,128)(2,1)} %bitcast.36), calls=%async_computation.1 | async-start | bytes 4718592 | tf_op jit(solution)/shard_map/all_to_all | solution.py:527
  10.1 5.1 %copy-start.5 = (bf16[4,64,1,128]{3,1,2,0:T(8,128)(2,1)S(1)}, bf16[4,64,1,128]{3,1,2,0:T(8,128)(2,1)}, u32[]{:S(2)}) copy-start(bf16[4,64,1,128]{3,1,2,0:T(8,128)(2,1)} %param.16) | copy-start | bytes 196612
  10.1 5.1 %copy-start.6 = (bf16[4,64,1,128]{3,1,2,0:T(8,128)(2,1)S(1)}, bf16[4,64,1,128]{3,1,2,0:T(8,128)(2,1)}, u32[]{:S(2)}) copy-start(bf16[4,64,1,128]{3,1,2,0:T(8,128)(2,1)} %param.15) | copy-start | bytes 196612
  23.3 6.6 %copy-start = (bf16[4,64,8,128]{3,2,1,0:T(8,128)(2,1)S(1)}, bf16[4,64,8,128]{3,2,1,0:T(8,128)(2,1)}, u32[]{:S(2)}) copy-start(bf16[4,64,8,128]{3,2,1,0:T(8,128)(2,1)} %param.14) | copy-start | bytes 1572868
  30.8 28.2 %collective-permute-start = (bf16[2128,128]{1,0:T(8,128)(2,1)}, bf16[2128,128]{1,0:T(8,128)(2,1)S(1)}, u32[]{:S(2)}, u32[]{:S(2)}) collective-permute-start(bf16[2128,128]{1,0:T(8,128)(2,1)} %gate.1), channel_id=1, source_target_pairs={{0,32},{32,0},{1,33},{33,1},{2,34},{34,2},{3,35},{35,3},{4,36},{36... | collective-permute-start | bytes 1634312 | tf_op jit(solution)/shard_map/ppermute | solution.py:541
  46.0 53.1 %all-to-all-start = ((bf16[16,18,2,16,128]{4,3,2,1,0:T(8,128)(2,1)}), bf16[16,18,2,16,128]{4,3,2,1,0:T(8,128)(2,1)}, u32[]{:S(2)}, u32[]{:S(2)}) async-start(bf16[16,18,2,16,128]{4,3,2,1,0:T(8,128)(2,1)} %bitcast.10), calls=%async_computation | async-start | bytes 4718592 | tf_op jit(solution)/shard_map/all_to_all | solution.py:527
  59.0 0.8 copy-start.9
  64.7 34.4 %collective-permute-start.1 = (bf16[2048,128]{1,0:T(8,128)(2,1)}, bf16[2048,128]{1,0:T(8,128)(2,1)S(1)}, u32[]{:S(2)}, u32[]{:S(2)}) collective-permute-start(bf16[2048,128]{1,0:T(8,128)(2,1)} %get-tuple-element.20), channel_id=1, source_target_pairs={{0,32},{32,0},{1,33},{33,1},{2,34},{34,2},{3,35},{35,3},{4,36},{36... | collective-permute-start | bytes 1572872 | tf_op jit(solution)/shard_map/ppermute | solution.py:545
  64.8 34.3 %collective-permute-start.2 = (f32[16,128]{1,0:T(8,128)}, f32[16,128]{1,0:T(8,128)S(1)}, u32[]{:S(2)}, u32[]{:S(2)}) collective-permute-start(f32[16,128]{1,0:T(8,128)} %get-tuple-element.21), channel_id=1, source_target_pairs={{0,32},{32,0},{1,33},{33,1},{2,34},{34,2},{3,35},{35,3},{4,36},{36... | collective-permute-start | bytes 24584 | tf_op jit(solution)/shard_map/ppermute | solution.py:546
  99.1 0.6 copy-start.7
  99.1 0.8 copy-start.1
  109.4 13.4 %collective-permute-start.6 = (bf16[256,512]{1,0:T(8,128)(2,1)}, bf16[256,512]{1,0:T(8,128)(2,1)S(1)}, u32[]{:S(2)}, u32[]{:S(2)}) collective-permute-start(bf16[256,512]{1,0:T(8,128)(2,1)} %get-tuple-element.28), channel_id=1, source_target_pairs={{0,4},{2,6},{4,0},{6,2},{1,5},{3,7},{5,1},{7,3},{8,12},{10,14},{12... | collective-permute-start | bytes 786440 | tf_op jit(solution)/shard_map/ppermute | solution.py:457
  111.7 14.4 %collective-permute-start.7 = (bf16[256,512]{1,0:T(8,128)(2,1)}, bf16[256,512]{1,0:T(8,128)(2,1)S(1)}, u32[]{:S(2)}, u32[]{:S(2)}) collective-permute-start(bf16[256,512]{1,0:T(8,128)(2,1)} %get-tuple-element.29), channel_id=1, source_target_pairs={{0,2},{2,4},{4,6},{6,0},{1,3},{3,5},{5,7},{7,1},{8,10},{10,12},{12... | collective-permute-start | bytes 786440 | tf_op jit(solution)/shard_map/ppermute | solution.py:457
  111.7 14.4 %collective-permute-start.8 = (bf16[256,512]{1,0:T(8,128)(2,1)}, bf16[256,512]{1,0:T(8,128)(2,1)}, u32[]{:S(2)}, u32[]{:S(2)}) collective-permute-start(bf16[256,512]{1,0:T(8,128)(2,1)} %get-tuple-element.30), channel_id=1, source_target_pairs={{0,6},{2,0},{4,2},{6,4},{1,7},{3,1},{5,3},{7,5},{8,14},{10,8},{12,... | collective-permute-start | bytes 786440 | tf_op jit(solution)/shard_map/ppermute | solution.py:457
  113.8 12.4 %copy-start.2 = (bf16[256,512]{1,0:T(8,128)(2,1)S(1)}, bf16[256,512]{1,0:T(8,128)(2,1)}, u32[]{:S(2)}) copy-start(bf16[256,512]{1,0:T(8,128)(2,1)} %get-tuple-element.27) | copy-start | bytes 786436
  118.7 26.2 %copy-start.3 = (bf16[256,512]{1,0:T(8,128)(2,1)S(1)}, bf16[256,512]{1,0:T(8,128)(2,1)}, u32[]{:S(2)}) copy-start(bf16[256,512]{1,0:T(8,128)(2,1)} %get-tuple-element.23) | copy-start | bytes 786436
  118.7 13.2 %collective-permute-start.3 = (bf16[256,512]{1,0:T(8,128)(2,1)}, bf16[256,512]{1,0:T(8,128)(2,1)S(1)}, u32[]{:S(2)}, u32[]{:S(2)}) collective-permute-start(bf16[256,512]{1,0:T(8,128)(2,1)} %get-tuple-element.24), channel_id=1, source_target_pairs={{0,4},{2,6},{4,0},{6,2},{1,5},{3,7},{5,1},{7,3},{8,12},{10,14},{12... | collective-permute-start | bytes 786440 | tf_op jit(solution)/shard_map/ppermute | solution.py:457
  120.1 16.4 %collective-permute-start.4 = (bf16[256,512]{1,0:T(8,128)(2,1)}, bf16[256,512]{1,0:T(8,128)(2,1)S(1)}, u32[]{:S(2)}, u32[]{:S(2)}) collective-permute-start(bf16[256,512]{1,0:T(8,128)(2,1)} %get-tuple-element.25), channel_id=1, source_target_pairs={{0,2},{2,4},{4,6},{6,0},{1,3},{3,5},{5,7},{7,1},{8,10},{10,12},{12... | collective-permute-start | bytes 786440 | tf_op jit(solution)/shard_map/ppermute | solution.py:457
  122.8 13.7 %collective-permute-start.5 = (bf16[256,512]{1,0:T(8,128)(2,1)}, bf16[256,512]{1,0:T(8,128)(2,1)S(1)}, u32[]{:S(2)}, u32[]{:S(2)}) collective-permute-start(bf16[256,512]{1,0:T(8,128)(2,1)} %get-tuple-element.26), channel_id=1, source_target_pairs={{0,6},{2,0},{4,2},{6,4},{1,7},{3,1},{5,3},{7,5},{8,14},{10,8},{12,... | collective-permute-start | bytes 786440 | tf_op jit(solution)/shard_map/ppermute | solution.py:457
  127.3 17.6 %collective-permute-start.9 = (bf16[256,512]{1,0:T(8,128)(2,1)S(1)}, bf16[256,512]{1,0:T(8,128)(2,1)S(1)}, u32[]{:S(2)}, u32[]{:S(2)}) collective-permute-start(bf16[256,512]{1,0:T(8,128)(2,1)S(1)} %add_convert_fusion.1), channel_id=1, source_target_pairs={{0,1},{1,0},{2,3},{3,2},{4,5},{5,4},{6,7},{7,6},{8,9},{9,8},{10,11... | collective-permute-start | bytes 786440 | tf_op jit(solution)/shard_map/ppermute | solution.py:550

commit v6 on v5

--- a/solution.py
+++ b/solution.py
@@ -28,11 +28,12 @@
 POSITIONS = WIDE * WIDE_CHUNKS
 LIST = ROWS * (POSITIONS + 4)
 LIST_ROWS = 40
+PIECES = 6
 TEAM = 4
 TEAMS = ROWS // TEAM
 LANES = TEAM * QROWS
 SCALE = DH ** -0.5
-VMEM_LIMIT = 63 * 1024 * 1024
+VMEM_LIMIT = 62 * 1024 * 1024
 
 SMEM = pl.BlockSpec(memory_space=pltpu.SMEM)
 VMEM = pl.BlockSpec(memory_space=pltpu.VMEM)
@@ -53,7 +54,7 @@
 
 
 def pack_kernel(half, pdest, mdest, pk, pv, mk, mv, *refs):
-    out, pages, send, pdest_s, mdest_s, slots, count, sems, out_sem = refs[-9:]
+    out, pages, send, pdest_s, mdest_s, chosen, count, sems, out_sems = refs[-9:]
     loads = start_all(
         [
             (pdest, pdest_s),
@@ -69,6 +70,12 @@
     for d in range(N_INST):
         count[d] = 0
         count[N_INST + d] = PCAP
+
+    def clear(n, carry):
+        chosen[n] = 0
+        return carry
+
+    lax.fori_loop(0, RECV, clear, 0, unroll=8)
     wait_all(loads[:2])
 
     def rank(dest, kind, first, j, carry):
@@ -76,18 +83,22 @@
         k = count[kind + d]
         count[kind + d] = k + 1
         group = (d >> 3) * 4 + (d & 3)
-        slots[first + j] = jnp.where(((d >> 2) & 1) == wanted, group * SLOTS + k, RECV)
+        chosen[jnp.where(((d >> 2) & 1) == wanted, group * SLOTS + k, RECV)] = first + j
         return carry
 
-    def copy_page(j, carry):
-        send[slots[j]] = pages[j]
+    def copy_page(n, carry):
+        send[n] = pages[chosen[n]]
         return carry
 
     lax.fori_loop(0, OUT, functools.partial(rank, pdest_s, 0, 0), 0, unroll=8)
     lax.fori_loop(0, MIG, functools.partial(rank, mdest_s, N_INST, OUT), 0, unroll=8)
     wait_all(loads[2:])
-    lax.fori_loop(0, OUT + MIG, copy_page, 0, unroll=8)
-    wait_all(start_all([(send.at[pl.ds(0, RECV)], out)], out_sem))
+    stores = []
+    for n in range(PIECES):
+        piece = pl.ds(n * (RECV // PIECES), RECV // PIECES)
+        lax.fori_loop(n * (RECV // PIECES), (n + 1) * (RECV // PIECES), copy_page, 0, unroll=8)
+        stores += start_all([(send.at[piece], out.at[piece])], out_sems.at[pl.ds(n, 1)])
+    wait_all(stores)
 
 
 def pack(half, pdest, mdest, pk, pv, mk, mv, *after):
@@ -98,13 +109,13 @@
         out_specs=ANY,
         scratch_shapes=[
             pltpu.VMEM((OUT + MIG, 2, PAGE, DH), jnp.bfloat16),
-            pltpu.VMEM((RECV + 1, 2, PAGE, DH), jnp.bfloat16),
+            pltpu.VMEM((RECV, 2, PAGE, DH), jnp.bfloat16),
             pltpu.SMEM((OUT,), jnp.int32),
             pltpu.SMEM((MIG,), jnp.int32),
-            pltpu.SMEM((OUT + MIG,), jnp.int32),
+            pltpu.SMEM((RECV + 1,), jnp.int32),
             pltpu.SMEM((2 * N_INST,), jnp.int32),
             pltpu.SemaphoreType.DMA((6,)),
-            pltpu.SemaphoreType.DMA((1,)),
+            pltpu.SemaphoreType.DMA((PIECES,)),
         ],
         compiler_params=PARAMS,
         cost_estimate=pl.CostEstimate(flops=10**6, bytes_accessed=10**7, transcendentals=0),

time: 147 us -> 144 us (0.980)
  transfers between devices with their start and end apart: 12 -> 12, of which waited for: 7 -> 7; matrix products, arithmetic and copies ran while one was open for 9% -> 8% of each run, Pallas kernels for 13% -> 13%
where the time goes in v6:
time: 144 us
  waiting for transfers between devices  66.5 us (46%)
  Pallas kernels  32.2 us (22%)
  starting transfers between devices  30.2 us (21%)
  local copies, waits for them, and re-layouts  7.26 us (5%)
  other arithmetic  6.96 us (5%)
    all_to_all x2, waiting for transfers between devices, exchange(): recv = lax.all_to_all(send, HALF, split_axis=0, concat_axis=0, tiled=True)  42.7 us
    all_to_all x2, starting transfers between devices, exchange(): recv = lax.all_to_all(send, HALF, split_axis=0, concat_axis=0, tiled=True)  10.3 us
    pallas_call x1, Pallas kernels, finish(): pl.pallas_call(finish_kernel, out_shape=(heads,) + TERMS, in_specs=[SMEM]...  9.41 us
    ppermute x6, waiting for transfers between devices, sum_over_y(): moved = lax.ppermute(term, 'ty', [(i, (i + shift) % 4) for i in range(4)])  8.86 us
    ppermute x6, starting transfers between devices, sum_over_y(): moved = lax.ppermute(term, 'ty', [(i, (i + shift) % 4) for i in range(4)])  8.52 us
    ppermute x1, waiting for transfers between devices, per_device(): letter = lax.ppermute(gate(letter, lse1), 'izh', swap)  7.94 us
    pallas_call x2, Pallas kernels, pack(): pl.pallas_call(pack_kernel, out_shape=jax.ShapeDtypeStruct((RECV, 2, PAGE...  7.78 us
    ppermute x1, waiting for transfers between devices, per_device(): other = lax.ppermute(sum_over_y(terms).astype(jnp.bfloat16), 'tz', swap)  6.9 us
  transfers between devices with their start and end apart: 12, of which 7 were waited for; matrix products, arithmetic and copies ran while one was open for 8% of the time, Pallas kernels for 13%

profile of v6, /device:TPU:8, one launch (start us, length us, event | category | flops | bytes accessed | tf_op | source)
XLA Modules:
  0.0 143.5 jit_solution(16292277987921156692)
XLA Ops:
  0.0 3.9 %pack_pages.3 = bf16[288,2,16,128]{3,2,1,0:T(8,128)(2,1)} custom-call(s32[1]{0:T(128)} %bitcast.23.half, s32[192]{0:T(256)} %pdest.3, s32[96]{0:T(128)} %mdest.3, bf16[192,16,128]{2,1,0:T(8,128)(2,1)} %bitcast.37, bf16[192,16,128]{2,1,0:T(8,128)(2,1)} %bitcast.39, bf16[96,16,128]{2,1,0:T(8,128)(2,1)} %bitcast.44, bf16[96,16,128]{2,1,0:T(8,128)(2,1)} %bitcast.46), custom_call_target="tpu_custom_call" | custom-call | flops 1000000 | bytes 10000000 | tf_op jit(solution)/shard_map/pack_pages/pallas_call | solution.py:105
  3.9 5.8 %all-to-all-start.1 = ((bf16[16,18,2,16,128]{4,3,2,1,0:T(8,128)(2,1)}), bf16[16,18,2,16,128]{4,3,2,1,0:T(8,128)(2,1)}, u32[]{:S(2)}, u32[]{:S(2)}) async-start(bf16[16,18,2,16,128]{4,3,2,1,0:T(8,128)(2,1)} %bitcast.36), calls=%async_computation.1 | async-start | bytes 4718592 | tf_op jit(solution)/shard_map/all_to_all | solution.py:538
  13.2 1.0 select_reduce_fusion
  15.1 0.9 pad.17.fresh
  17.4 3.9 %pack_pages.2.after = bf16[288,2,16,128]{3,2,1,0:T(8,128)(2,1)} custom-call(s32[1]{0:T(128)} %bitcast.5.half, s32[192]{0:T(256)} %pdest.3, s32[96]{0:T(128)} %mdest.3, bf16[192,16,128]{2,1,0:T(8,128)(2,1)} %bitcast.38, bf16[192,16,128]{2,1,0:T(8,128)(2,1)} %bitcast.40, bf16[96,16,128]{2,1,0:T(8,128)(2,1)} %bitcast.45, bf16[96,16,128]{2,1,0:T(8,128)(2,1)} %bitcast.47, ...), custom_call_target="tpu_custom_call" | custom-call | flops 1000000 | bytes 10000000 | tf_op jit(solution)/shard_map/pack_pages/pallas_call | solution.py:105
  22.6 5.3 %attend_local.1 = (f32[2048,128]{1,0:T(8,128)}, f32[16,128]{1,0:T(8,128)}) custom-call(s32[40,128]{1,0:T(8,128)} %bitcast.50, bf16[2048,128]{1,0:T(8,128)(2,1)} %bitcast.41, bf16[192,16,128]{2,1,0:T(8,128)(2,1)} %bitcast.51, bf16[192,16,128]{2,1,0:T(8,128)(2,1)} %bitcast.52, bf16[64,2,16,128]{3,2,1,0:T(8,128)(2,1)} %pad.17.fresh, ...), custom_call_target="tpu_custom_call" | custom-call | flops 99999997952 | bytes 100000000 | tf_op jit(solution)/shard_map/attend_local/pallas_call | solution.py:297
  29.2 0.9 pad_maximum_fusion.x
  30.1 3.3 %collective-permute-start = (bf16[2128,128]{1,0:T(8,128)(2,1)}, bf16[2128,128]{1,0:T(8,128)(2,1)S(1)}, u32[]{:S(2)}, u32[]{:S(2)}) collective-permute-start(bf16[2128,128]{1,0:T(8,128)(2,1)} %gate.1), channel_id=1, source_target_pairs={{0,32},{32,0},{1,33},{33,1},{2,34},{34,2},{3,35},{35,3},{4,36},{36... | collective-permute-start | bytes 1634312 | tf_op jit(solution)/shard_map/ppermute | solution.py:552
  33.4 12.7 %all-to-all-done.1 = bf16[16,18,2,16,128]{4,3,2,1,0:T(8,128)(2,1)} async-done(((bf16[16,18,2,16,128]{4,3,2,1,0:T(8,128)(2,1)}), bf16[16,18,2,16,128]{4,3,2,1,0:T(8,128)(2,1)}, u32[]{:S(2)}, u32[]{:S(2)}) %all-to-all-start.1) | async-done | bytes 2359328 | tf_op jit(solution)/shard_map/all_to_all | solution.py:538
  46.0 4.4 %all-to-all-start = ((bf16[16,18,2,16,128]{4,3,2,1,0:T(8,128)(2,1)}), bf16[16,18,2,16,128]{4,3,2,1,0:T(8,128)(2,1)}, u32[]{:S(2)}, u32[]{:S(2)}) async-start(bf16[16,18,2,16,128]{4,3,2,1,0:T(8,128)(2,1)} %bitcast.10), calls=%async_computation | async-start | bytes 4718592 | tf_op jit(solution)/shard_map/all_to_all | solution.py:538
  50.5 7.9 %collective-permute-done.letter = bf16[2128,128]{1,0:T(8,128)(2,1)S(1)} collective-permute-done((bf16[2128,128]{1,0:T(8,128)(2,1)}, bf16[2128,128]{1,0:T(8,128)(2,1)S(1)}, u32[]{:S(2)}, u32[]{:S(2)}) %collective-permute-start) | collective-permute-done | bytes 544800 | tf_op jit(solution)/shard_map/ppermute | solution.py:552
  59.3 4.9 %attend_far.1 = (bf16[2048,128]{1,0:T(8,128)(2,1)}, f32[16,128]{1,0:T(8,128)}) custom-call(bf16[2128,128]{1,0:T(8,128)(2,1)} %copy-done.9, bf16[288,2,16,128]{3,2,1,0:T(8,128)(2,1)} %bitcast.25.recv), custom_call_target="tpu_custom_call" | custom-call | flops 99999997952 | bytes 100000000 | tf_op jit(solution)/shard_map/attend_far/pallas_call | solution.py:334
  64.2 2.9 %collective-permute-start.2 = (f32[16,128]{1,0:T(8,128)}, f32[16,128]{1,0:T(8,128)S(1)}, u32[]{:S(2)}, u32[]{:S(2)}) collective-permute-start(f32[16,128]{1,0:T(8,128)} %get-tuple-element.21), channel_id=1, source_target_pairs={{0,32},{32,0},{1,33},{33,1},{2,34},{34,2},{3,35},{35,3},{4,36},{36... | collective-permute-start | bytes 24584 | tf_op jit(solution)/shard_map/ppermute | solution.py:557
  67.8 30.1 %all-to-all-done = bf16[16,18,2,16,128]{4,3,2,1,0:T(8,128)(2,1)} async-done(((bf16[16,18,2,16,128]{4,3,2,1,0:T(8,128)(2,1)}), bf16[16,18,2,16,128]{4,3,2,1,0:T(8,128)(2,1)}, u32[]{:S(2)}, u32[]{:S(2)}) %all-to-all-start) | async-done | bytes 2359328 | tf_op jit(solution)/shard_map/all_to_all | solution.py:538
  98.7 9.4 %attend_merge_project.1 = (bf16[256,1024]{1,0:T(8,128)(2,1)}, bf16[256,512]{1,0:T(8,128)(2,1)}, bf16[256,512]{1,0:T(8,128)(2,1)}, bf16[256,512]{1,0:T(8,128)(2,1)}, bf16[256,512]{1,0:T(8,128)(2,1)}) custom-call(s32[2]{0:T(128)} %pad_add_fusion.1.place, s32[40,128]{1,0:T(8,128)} %bitcast.49, bf16[2048,128]{1,0:T(8,128)(2,1)} %bitcast.42, ...), custom_call_target="tpu_custom_call" | custom-call | tf_op jit(solution)/shard_map/attend_merge_project/pallas_call | solution.py:430
  108.1 2.4 %collective-permute-start.6 = (bf16[256,512]{1,0:T(8,128)(2,1)}, bf16[256,512]{1,0:T(8,128)(2,1)S(1)}, u32[]{:S(2)}, u32[]{:S(2)}) collective-permute-start(bf16[256,512]{1,0:T(8,128)(2,1)} %get-tuple-element.28), channel_id=1, source_target_pairs={{0,4},{2,6},{4,0},{6,2},{1,5},{3,7},{5,1},{7,3},{8,12},{10,14},{12... | collective-permute-start | bytes 786440 | tf_op jit(solution)/shard_map/ppermute | solution.py:468
  110.5 2.0 %collective-permute-start.8 = (bf16[256,512]{1,0:T(8,128)(2,1)}, bf16[256,512]{1,0:T(8,128)(2,1)S(1)}, u32[]{:S(2)}, u32[]{:S(2)}) collective-permute-start(bf16[256,512]{1,0:T(8,128)(2,1)} %get-tuple-element.30), channel_id=1, source_target_pairs={{0,6},{2,0},{4,2},{6,4},{1,7},{3,1},{5,3},{7,5},{8,14},{10,8},{12,... | collective-permute-start | bytes 786440 | tf_op jit(solution)/shard_map/ppermute | solution.py:468
  112.5 4.9 %project_mine.1 = (bf16[256,512]{1,0:T(8,128)(2,1)}, bf16[256,512]{1,0:T(8,128)(2,1)}, bf16[256,512]{1,0:T(8,128)(2,1)}, bf16[256,512]{1,0:T(8,128)(2,1)}) custom-call(s32[2]{0:T(128)} %pad_add_fusion.1.place, bf16[256,1024]{1,0:T(8,128)(2,1)} %get-tuple-element.22.heads, bf16[1024,4096]{1,0:T(8,128)(2,1)} %weight.3), custom_call_target="tpu_custom_call" | custom-call | flops 1000000000 | bytes 6000000 | tf_op jit(solution)/shard_map/project_mine/pallas_call | solution.py:452
  117.4 1.5 %collective-permute-start.3 = (bf16[256,512]{1,0:T(8,128)(2,1)}, bf16[256,512]{1,0:T(8,128)(2,1)S(1)}, u32[]{:S(2)}, u32[]{:S(2)}) collective-permute-start(bf16[256,512]{1,0:T(8,128)(2,1)} %get-tuple-element.24), channel_id=1, source_target_pairs={{0,4},{2,6},{4,0},{6,2},{1,5},{3,7},{5,1},{7,3},{8,12},{10,14},{12... | collective-permute-start | bytes 786440 | tf_op jit(solution)/shard_map/ppermute | solution.py:468
  118.9 2.6 %collective-permute-start.4 = (bf16[256,512]{1,0:T(8,128)(2,1)}, bf16[256,512]{1,0:T(8,128)(2,1)S(1)}, u32[]{:S(2)}, u32[]{:S(2)}) collective-permute-start(bf16[256,512]{1,0:T(8,128)(2,1)} %get-tuple-element.25), channel_id=1, source_target_pairs={{0,2},{2,4},{4,6},{6,0},{1,3},{3,5},{5,7},{7,1},{8,10},{10,12},{12... | collective-permute-start | bytes 786440 | tf_op jit(solution)/shard_map/ppermute | solution.py:468
  121.5 3.3 %collective-permute-done.7 = bf16[256,512]{1,0:T(8,128)(2,1)S(1)} collective-permute-done((bf16[256,512]{1,0:T(8,128)(2,1)}, bf16[256,512]{1,0:T(8,128)(2,1)S(1)}, u32[]{:S(2)}, u32[]{:S(2)}) %collective-permute-start.7) | collective-permute-done | bytes 262176 | tf_op jit(solution)/shard_map/ppermute | solution.py:468
  125.0 5.2 %collective-permute-start.9 = (bf16[256,512]{1,0:T(8,128)(2,1)S(1)}, bf16[256,512]{1,0:T(8,128)(2,1)S(1)}, u32[]{:S(2)}, u32[]{:S(2)}) collective-permute-start(bf16[256,512]{1,0:T(8,128)(2,1)S(1)} %add_convert_fusion.1), channel_id=1, source_target_pairs={{0,1},{1,0},{2,3},{3,2},{4,5},{5,4},{6,7},{7,6},{8,9},{9,8},{10,11... | collective-permute-start | bytes 786440 | tf_op jit(solution)/shard_map/ppermute | solution.py:561
  130.4 5.4 %collective-permute-done.4 = bf16[256,512]{1,0:T(8,128)(2,1)S(1)} collective-permute-done((bf16[256,512]{1,0:T(8,128)(2,1)}, bf16[256,512]{1,0:T(8,128)(2,1)S(1)}, u32[]{:S(2)}, u32[]{:S(2)}) %collective-permute-start.4) | collective-permute-done | bytes 262176 | tf_op jit(solution)/shard_map/ppermute | solution.py:468
  135.7 6.9 %collective-permute-done.9 = bf16[256,512]{1,0:T(8,128)(2,1)S(1)} collective-permute-done((bf16[256,512]{1,0:T(8,128)(2,1)S(1)}, bf16[256,512]{1,0:T(8,128)(2,1)S(1)}, u32[]{:S(2)}, u32[]{:S(2)}) %collective-permute-start.9) | collective-permute-done | bytes 262176 | tf_op jit(solution)/shard_map/ppermute | solution.py:561
  (88 shorter events, 11.7 us)
Async XLA Ops:
  3.9 5.9 %copy-start.4 = (s32[64,48]{0,1:T(8,128)S(1)}, s32[64,48]{0,1:T(8,128)}, u32[]{:S(2)}) copy-start(s32[64,48]{0,1:T(8,128)} %param.25) | copy-start | bytes 36868
  3.9 5.9 %copy-start.8 = (s32[64]{0:T(128)S(1)}, s32[64]{0:T(128)}, u32[]{:S(2)}) copy-start(s32[64]{0:T(128)} %param.26) | copy-start | bytes 772
  3.9 42.1 %all-to-all-start.1 = ((bf16[16,18,2,16,128]{4,3,2,1,0:T(8,128)(2,1)}), bf16[16,18,2,16,128]{4,3,2,1,0:T(8,128)(2,1)}, u32[]{:S(2)}, u32[]{:S(2)}) async-start(bf16[16,18,2,16,128]{4,3,2,1,0:T(8,128)(2,1)} %bitcast.36), calls=%async_computation.1 | async-start | bytes 4718592 | tf_op jit(solution)/shard_map/all_to_all | solution.py:538
  9.8 5.1 %copy-start.5 = (bf16[4,64,1,128]{3,1,2,0:T(8,128)(2,1)S(1)}, bf16[4,64,1,128]{3,1,2,0:T(8,128)(2,1)}, u32[]{:S(2)}) copy-start(bf16[4,64,1,128]{3,1,2,0:T(8,128)(2,1)} %param.16) | copy-start | bytes 196612
  9.8 5.1 %copy-start.6 = (bf16[4,64,1,128]{3,1,2,0:T(8,128)(2,1)S(1)}, bf16[4,64,1,128]{3,1,2,0:T(8,128)(2,1)}, u32[]{:S(2)}) copy-start(bf16[4,64,1,128]{3,1,2,0:T(8,128)(2,1)} %param.15) | copy-start | bytes 196612
  22.6 6.6 %copy-start = (bf16[4,64,8,128]{3,2,1,0:T(8,128)(2,1)S(1)}, bf16[4,64,8,128]{3,2,1,0:T(8,128)(2,1)}, u32[]{:S(2)}) copy-start(bf16[4,64,8,128]{3,2,1,0:T(8,128)(2,1)} %param.14) | copy-start | bytes 1572868
  30.1 28.3 %collective-permute-start = (bf16[2128,128]{1,0:T(8,128)(2,1)}, bf16[2128,128]{1,0:T(8,128)(2,1)S(1)}, u32[]{:S(2)}, u32[]{:S(2)}) collective-permute-start(bf16[2128,128]{1,0:T(8,128)(2,1)} %gate.1), channel_id=1, source_target_pairs={{0,32},{32,0},{1,33},{33,1},{2,34},{34,2},{3,35},{35,3},{4,36},{36... | collective-permute-start | bytes 1634312 | tf_op jit(solution)/shard_map/ppermute | solution.py:552
  46.0 51.9 %all-to-all-start = ((bf16[16,18,2,16,128]{4,3,2,1,0:T(8,128)(2,1)}), bf16[16,18,2,16,128]{4,3,2,1,0:T(8,128)(2,1)}, u32[]{:S(2)}, u32[]{:S(2)}) async-start(bf16[16,18,2,16,128]{4,3,2,1,0:T(8,128)(2,1)} %bitcast.10), calls=%async_computation | async-start | bytes 4718592 | tf_op jit(solution)/shard_map/all_to_all | solution.py:538
  58.4 0.8 copy-start.9
  64.1 33.8 %collective-permute-start.1 = (bf16[2048,128]{1,0:T(8,128)(2,1)}, bf16[2048,128]{1,0:T(8,128)(2,1)S(1)}, u32[]{:S(2)}, u32[]{:S(2)}) collective-permute-start(bf16[2048,128]{1,0:T(8,128)(2,1)} %get-tuple-element.20), channel_id=1, source_target_pairs={{0,32},{32,0},{1,33},{33,1},{2,34},{34,2},{3,35},{35,3},{4,36},{36... | collective-permute-start | bytes 1572872 | tf_op jit(solution)/shard_map/ppermute | solution.py:556
  64.2 33.6 %collective-permute-start.2 = (f32[16,128]{1,0:T(8,128)}, f32[16,128]{1,0:T(8,128)S(1)}, u32[]{:S(2)}, u32[]{:S(2)}) collective-permute-start(f32[16,128]{1,0:T(8,128)} %get-tuple-element.21), channel_id=1, source_target_pairs={{0,32},{32,0},{1,33},{33,1},{2,34},{34,2},{3,35},{35,3},{4,36},{36... | collective-permute-start | bytes 24584 | tf_op jit(solution)/shard_map/ppermute | solution.py:557
  97.9 0.6 copy-start.7
  97.9 0.8 copy-start.1
  108.1 13.4 %collective-permute-start.6 = (bf16[256,512]{1,0:T(8,128)(2,1)}, bf16[256,512]{1,0:T(8,128)(2,1)S(1)}, u32[]{:S(2)}, u32[]{:S(2)}) collective-permute-start(bf16[256,512]{1,0:T(8,128)(2,1)} %get-tuple-element.28), channel_id=1, source_target_pairs={{0,4},{2,6},{4,0},{6,2},{1,5},{3,7},{5,1},{7,3},{8,12},{10,14},{12... | collective-permute-start | bytes 786440 | tf_op jit(solution)/shard_map/ppermute | solution.py:468
  110.5 14.3 %collective-permute-start.7 = (bf16[256,512]{1,0:T(8,128)(2,1)}, bf16[256,512]{1,0:T(8,128)(2,1)S(1)}, u32[]{:S(2)}, u32[]{:S(2)}) collective-permute-start(bf16[256,512]{1,0:T(8,128)(2,1)} %get-tuple-element.29), channel_id=1, source_target_pairs={{0,2},{2,4},{4,6},{6,0},{1,3},{3,5},{5,7},{7,1},{8,10},{10,12},{12... | collective-permute-start | bytes 786440 | tf_op jit(solution)/shard_map/ppermute | solution.py:468
  110.5 14.3 %collective-permute-start.8 = (bf16[256,512]{1,0:T(8,128)(2,1)}, bf16[256,512]{1,0:T(8,128)(2,1)S(1)}, u32[]{:S(2)}, u32[]{:S(2)}) collective-permute-start(bf16[256,512]{1,0:T(8,128)(2,1)} %get-tuple-element.30), channel_id=1, source_target_pairs={{0,6},{2,0},{4,2},{6,4},{1,7},{3,1},{5,3},{7,5},{8,14},{10,8},{12,... | collective-permute-start | bytes 786440 | tf_op jit(solution)/shard_map/ppermute | solution.py:468
  112.5 12.3 %copy-start.2 = (bf16[256,512]{1,0:T(8,128)(2,1)S(1)}, bf16[256,512]{1,0:T(8,128)(2,1)}, u32[]{:S(2)}) copy-start(bf16[256,512]{1,0:T(8,128)(2,1)} %get-tuple-element.27) | copy-start | bytes 786436
  117.4 25.2 %copy-start.3 = (bf16[256,512]{1,0:T(8,128)(2,1)S(1)}, bf16[256,512]{1,0:T(8,128)(2,1)}, u32[]{:S(2)}) copy-start(bf16[256,512]{1,0:T(8,128)(2,1)} %get-tuple-element.23) | copy-start | bytes 786436
  117.4 12.9 %collective-permute-start.3 = (bf16[256,512]{1,0:T(8,128)(2,1)}, bf16[256,512]{1,0:T(8,128)(2,1)S(1)}, u32[]{:S(2)}, u32[]{:S(2)}) collective-permute-start(bf16[256,512]{1,0:T(8,128)(2,1)} %get-tuple-element.24), channel_id=1, source_target_pairs={{0,4},{2,6},{4,0},{6,2},{1,5},{3,7},{5,1},{7,3},{8,12},{10,14},{12... | collective-permute-start | bytes 786440 | tf_op jit(solution)/shard_map/ppermute | solution.py:468
  118.9 16.8 %collective-permute-start.4 = (bf16[256,512]{1,0:T(8,128)(2,1)}, bf16[256,512]{1,0:T(8,128)(2,1)S(1)}, u32[]{:S(2)}, u32[]{:S(2)}) collective-permute-start(bf16[256,512]{1,0:T(8,128)(2,1)} %get-tuple-element.25), channel_id=1, source_target_pairs={{0,2},{2,4},{4,6},{6,0},{1,3},{3,5},{5,7},{7,1},{8,10},{10,12},{12... | collective-permute-start | bytes 786440 | tf_op jit(solution)/shard_map/ppermute | solution.py:468
  121.5 14.2 %collective-permute-start.5 = (bf16[256,512]{1,0:T(8,128)(2,1)}, bf16[256,512]{1,0:T(8,128)(2,1)S(1)}, u32[]{:S(2)}, u32[]{:S(2)}) collective-permute-start(bf16[256,512]{1,0:T(8,128)(2,1)} %get-tuple-element.26), channel_id=1, source_target_pairs={{0,6},{2,0},{4,2},{6,4},{1,7},{3,1},{5,3},{7,5},{8,14},{10,8},{12,... | collective-permute-start | bytes 786440 | tf_op jit(solution)/shard_map/ppermute | solution.py:468
  125.0 17.7 %collective-permute-start.9 = (bf16[256,512]{1,0:T(8,128)(2,1)S(1)}, bf16[256,512]{1,0:T(8,128)(2,1)S(1)}, u32[]{:S(2)}, u32[]{:S(2)}) collective-permute-start(bf16[256,512]{1,0:T(8,128)(2,1)S(1)} %add_convert_fusion.1), channel_id=1, source_target_pairs={{0,1},{1,0},{2,3},{3,2},{4,5},{5,4},{6,7},{7,6},{8,9},{9,8},{10,11... | collective-permute-start | bytes 786440 | tf_op jit(solution)/shard_map/ppermute | solution.py:561

commit v7 on v6

--- a/solution.py
+++ b/solution.py
@@ -54,7 +54,7 @@
 
 
 def pack_kernel(half, pdest, mdest, pk, pv, mk, mv, *refs):
-    out, pages, send, pdest_s, mdest_s, chosen, count, sems, out_sems = refs[-9:]
+    out, pages, send, pdest_s, mdest_s, chosen, prompts, moved, sems, out_sems = refs[-10:]
     loads = start_all(
         [
             (pdest, pdest_s),
@@ -68,8 +68,8 @@
     )
     wanted = half[0]
     for d in range(N_INST):
-        count[d] = 0
-        count[N_INST + d] = PCAP
+        prompts[d] = 0
+        moved[d] = PCAP
 
     def clear(n, carry):
         chosen[n] = 0
@@ -78,20 +78,24 @@
     lax.fori_loop(0, RECV, clear, 0, unroll=8)
     wait_all(loads[:2])
 
-    def rank(dest, kind, first, j, carry):
+    def rank(dest, count, first, j):
         d = dest[j]
-        k = count[kind + d]
-        count[kind + d] = k + 1
+        k = count[d]
+        count[d] = k + 1
         group = (d >> 3) * 4 + (d & 3)
         chosen[jnp.where(((d >> 2) & 1) == wanted, group * SLOTS + k, RECV)] = first + j
-        return carry
 
     def copy_page(n, carry):
         send[n] = pages[chosen[n]]
         return carry
 
-    lax.fori_loop(0, OUT, functools.partial(rank, pdest_s, 0, 0), 0, unroll=8)
-    lax.fori_loop(0, MIG, functools.partial(rank, mdest_s, N_INST, OUT), 0, unroll=8)
+    def ranks(j, carry):
+        rank(pdest_s, prompts, 0, 2 * j)
+        rank(mdest_s, moved, OUT, j)
+        rank(pdest_s, prompts, 0, 2 * j + 1)
+        return carry
+
+    lax.fori_loop(0, MIG, ranks, 0, unroll=8)
     wait_all(loads[2:])
     stores = []
     for n in range(PIECES):
@@ -113,7 +117,8 @@
             pltpu.SMEM((OUT,), jnp.int32),
             pltpu.SMEM((MIG,), jnp.int32),
             pltpu.SMEM((RECV + 1,), jnp.int32),
-            pltpu.SMEM((2 * N_INST,), jnp.int32),
+            pltpu.SMEM((N_INST,), jnp.int32),
+            pltpu.SMEM((N_INST,), jnp.int32),
             pltpu.SemaphoreType.DMA((6,)),
             pltpu.SemaphoreType.DMA((PIECES,)),
         ],
@@ -397,9 +402,9 @@
 ]
 
 
-def finish_kernel(place, lists, q, recv, o1, lse1, o2, lse2, weight, heads, *refs):
+def finish_kernel(place, lists, q, recv, o1, lse1, o2, lse2, weight, heads_out, *refs):
     outs, refs = refs[:TILES], refs[TILES:]
-    lists_s, q_s, kv, o1_s, lse1_s, o2_s, lse2_s, lse3, result, scores, sems, part_sems, w, terms, w_sems, out_sems = refs
+    lists_s, q_s, kv, o1_s, lse1_s, o2_s, lse2_s, lse3, result, scores, heads, sems, part_sems, heads_sem, w, terms, w_sems, out_sems = refs
     copies = start_all([(lists, lists_s), (q, q_s), (recv, kv.at[pl.ds(1, RECV)])], sems)
     parts = start_all([(lse1, lse1_s), (lse2, lse2_s), (o1, o1_s), (o2, o2_s)], part_sems)
     kv[0] = blank_page()
@@ -422,7 +427,9 @@
         for h in range(GROUPS):
             column = result[pl.ds(t * ROWS * GROUPS + h, ROWS, stride=GROUPS), :]
             heads[pl.ds(t * ROWS, ROWS), pl.ds(h * DH, DH)] = column.astype(jnp.bfloat16)
+    heads_store = start_all([(heads, heads_out)], heads_sem)
     project(loads, heads, w, outs, terms, out_sems)
+    wait_all(heads_store)
 
 
 def finish(place, lists, q, recv, o1, lse1, o2, lse2, weight):
@@ -431,11 +438,13 @@
         finish_kernel,
         out_shape=(heads,) + TERMS,
         in_specs=[SMEM] + [ANY] * 8,
-        out_specs=(VMEM,) + (ANY,) * TILES,
+        out_specs=(ANY,) * (1 + TILES),
         scratch_shapes=[
             LISTS, QUERIES, pages_scratch(RECV), RESULT, LSE, QUERIES, LSE, LSE, RESULT, SCORES,
+            pltpu.VMEM((STEPS * ROWS, GROUPS * DH), jnp.bfloat16),
             pltpu.SemaphoreType.DMA((3,)),
             pltpu.SemaphoreType.DMA((4,)),
+            pltpu.SemaphoreType.DMA((1,)),
         ] + PROJECT_SCRATCH,
         compiler_params=PARAMS,
         name="attend_merge_project",

time: 144 us -> 142 us (0.986)
  waiting for transfers between devices: 66.5 us -> 64.8 us
  starting transfers between devices: 30.2 us -> 31.8 us
  Pallas kernels: 32.2 us -> 30.7 us
  transfers between devices with their start and end apart: 12 -> 12, of which waited for: 7 -> 6; matrix products, arithmetic and copies ran while one was open for 8% -> 8% of each run, Pallas kernels for 13% -> 13%
where the time goes in v7:
time: 142 us
  waiting for transfers between devices  64.8 us (46%)
  starting transfers between devices  31.8 us (22%)
  Pallas kernels  30.7 us (22%)
  local copies, waits for them, and re-layouts  7.26 us (5%)
  other arithmetic  6.96 us (5%)
    all_to_all x2, waiting for transfers between devices, exchange(): recv = lax.all_to_all(send, HALF, split_axis=0, concat_axis=0, tiled=True)  42.6 us
    all_to_all x2, starting transfers between devices, exchange(): recv = lax.all_to_all(send, HALF, split_axis=0, concat_axis=0, tiled=True)  10.3 us
    pallas_call x1, Pallas kernels, finish(): pl.pallas_call(finish_kernel, out_shape=(heads,) + TERMS, in_specs=[SMEM]...  8.63 us
    ppermute x6, starting transfers between devices, sum_over_y(): moved = lax.ppermute(term, 'ty', [(i, (i + shift) % 4) for i in range(4)])  8.52 us
    ppermute x6, waiting for transfers between devices, sum_over_y(): moved = lax.ppermute(term, 'ty', [(i, (i + shift) % 4) for i in range(4)])  7.84 us
    pallas_call x2, Pallas kernels, pack(): pl.pallas_call(pack_kernel, out_shape=jax.ShapeDtypeStruct((RECV, 2, PAGE...  7.48 us
    ppermute x1, waiting for transfers between devices, per_device(): other = lax.ppermute(sum_over_y(terms).astype(jnp.bfloat16), 'tz', swap)  7.34 us
    ppermute x1, waiting for transfers between devices, per_device(): letter = lax.ppermute(gate(letter, lse1), 'izh', swap)  6.98 us
  transfers between devices with their start and end apart: 12, of which 6 were waited for; matrix products, arithmetic and copies ran while one was open for 8% of the time, Pallas kernels for 13%

profile of v7, /device:TPU:8, one launch (start us, length us, event | category | flops | bytes accessed | tf_op | source)
XLA Modules:
  0.0 141.9 jit_solution(8300384941434478930)
XLA Ops:
  0.0 3.7 %pack_pages.3 = bf16[288,2,16,128]{3,2,1,0:T(8,128)(2,1)} custom-call(s32[1]{0:T(128)} %bitcast.23.half, s32[192]{0:T(256)} %pdest.3, s32[96]{0:T(128)} %mdest.3, bf16[192,16,128]{2,1,0:T(8,128)(2,1)} %bitcast.37, bf16[192,16,128]{2,1,0:T(8,128)(2,1)} %bitcast.39, bf16[96,16,128]{2,1,0:T(8,128)(2,1)} %bitcast.44, bf16[96,16,128]{2,1,0:T(8,128)(2,1)} %bitcast.46), custom_call_target="tpu_custom_call" | custom-call | flops 1000000 | bytes 10000000 | tf_op jit(solution)/shard_map/pack_pages/pallas_call | solution.py:109
  3.8 5.8 %all-to-all-start.1 = ((bf16[16,18,2,16,128]{4,3,2,1,0:T(8,128)(2,1)}), bf16[16,18,2,16,128]{4,3,2,1,0:T(8,128)(2,1)}, u32[]{:S(2)}, u32[]{:S(2)}) async-start(bf16[16,18,2,16,128]{4,3,2,1,0:T(8,128)(2,1)} %bitcast.36), calls=%async_computation.1 | async-start | bytes 4718592 | tf_op jit(solution)/shard_map/all_to_all | solution.py:547
  13.1 1.0 select_reduce_fusion
  14.9 0.9 pad.17.fresh
  17.2 3.7 %pack_pages.2.after = bf16[288,2,16,128]{3,2,1,0:T(8,128)(2,1)} custom-call(s32[1]{0:T(128)} %bitcast.5.half, s32[192]{0:T(256)} %pdest.3, s32[96]{0:T(128)} %mdest.3, bf16[192,16,128]{2,1,0:T(8,128)(2,1)} %bitcast.38, bf16[192,16,128]{2,1,0:T(8,128)(2,1)} %bitcast.40, bf16[96,16,128]{2,1,0:T(8,128)(2,1)} %bitcast.45, bf16[96,16,128]{2,1,0:T(8,128)(2,1)} %bitcast.47, ...), custom_call_target="tpu_custom_call" | custom-call | flops 1000000 | bytes 10000000 | tf_op jit(solution)/shard_map/pack_pages/pallas_call | solution.py:109
  22.3 4.8 %attend_local.1 = (f32[2048,128]{1,0:T(8,128)}, f32[16,128]{1,0:T(8,128)}) custom-call(s32[40,128]{1,0:T(8,128)} %bitcast.50, bf16[2048,128]{1,0:T(8,128)(2,1)} %bitcast.41, bf16[192,16,128]{2,1,0:T(8,128)(2,1)} %bitcast.51, bf16[192,16,128]{2,1,0:T(8,128)(2,1)} %bitcast.52, bf16[64,2,16,128]{3,2,1,0:T(8,128)(2,1)} %pad.17.fresh, ...), custom_call_target="tpu_custom_call" | custom-call | flops 99999997952 | bytes 100000000 | tf_op jit(solution)/shard_map/attend_local/pallas_call | solution.py:302
  28.4 0.9 pad_maximum_fusion.x
  29.3 4.3 %collective-permute-start = (bf16[2128,128]{1,0:T(8,128)(2,1)}, bf16[2128,128]{1,0:T(8,128)(2,1)S(1)}, u32[]{:S(2)}, u32[]{:S(2)}) collective-permute-start(bf16[2128,128]{1,0:T(8,128)(2,1)} %gate.1), channel_id=1, source_target_pairs={{0,32},{32,0},{1,33},{33,1},{2,34},{34,2},{3,35},{35,3},{4,36},{36... | collective-permute-start | bytes 1634312 | tf_op jit(solution)/shard_map/ppermute | solution.py:561
  33.6 13.0 %all-to-all-done.1 = bf16[16,18,2,16,128]{4,3,2,1,0:T(8,128)(2,1)} async-done(((bf16[16,18,2,16,128]{4,3,2,1,0:T(8,128)(2,1)}), bf16[16,18,2,16,128]{4,3,2,1,0:T(8,128)(2,1)}, u32[]{:S(2)}, u32[]{:S(2)}) %all-to-all-start.1) | async-done | bytes 2359328 | tf_op jit(solution)/shard_map/all_to_all | solution.py:547
  46.6 4.4 %all-to-all-start = ((bf16[16,18,2,16,128]{4,3,2,1,0:T(8,128)(2,1)}), bf16[16,18,2,16,128]{4,3,2,1,0:T(8,128)(2,1)}, u32[]{:S(2)}, u32[]{:S(2)}) async-start(bf16[16,18,2,16,128]{4,3,2,1,0:T(8,128)(2,1)} %bitcast.10), calls=%async_computation | async-start | bytes 4718592 | tf_op jit(solution)/shard_map/all_to_all | solution.py:547
  51.0 7.0 %collective-permute-done.letter = bf16[2128,128]{1,0:T(8,128)(2,1)S(1)} collective-permute-done((bf16[2128,128]{1,0:T(8,128)(2,1)}, bf16[2128,128]{1,0:T(8,128)(2,1)S(1)}, u32[]{:S(2)}, u32[]{:S(2)}) %collective-permute-start) | collective-permute-done | bytes 544800 | tf_op jit(solution)/shard_map/ppermute | solution.py:561
  58.8 4.9 %attend_far.1 = (bf16[2048,128]{1,0:T(8,128)(2,1)}, f32[16,128]{1,0:T(8,128)}) custom-call(bf16[2128,128]{1,0:T(8,128)(2,1)} %copy-done.9, bf16[288,2,16,128]{3,2,1,0:T(8,128)(2,1)} %bitcast.25.recv), custom_call_target="tpu_custom_call" | custom-call | flops 99999997952 | bytes 100000000 | tf_op jit(solution)/shard_map/attend_far/pallas_call | solution.py:339
  63.9 2.9 %collective-permute-start.2 = (f32[16,128]{1,0:T(8,128)}, f32[16,128]{1,0:T(8,128)S(1)}, u32[]{:S(2)}, u32[]{:S(2)}) collective-permute-start(f32[16,128]{1,0:T(8,128)} %get-tuple-element.21), channel_id=1, source_target_pairs={{0,32},{32,0},{1,33},{33,1},{2,34},{34,2},{3,35},{35,3},{4,36},{36... | collective-permute-start | bytes 24584 | tf_op jit(solution)/shard_map/ppermute | solution.py:566
  67.4 29.7 %all-to-all-done = bf16[16,18,2,16,128]{4,3,2,1,0:T(8,128)(2,1)} async-done(((bf16[16,18,2,16,128]{4,3,2,1,0:T(8,128)(2,1)}), bf16[16,18,2,16,128]{4,3,2,1,0:T(8,128)(2,1)}, u32[]{:S(2)}, u32[]{:S(2)}) %all-to-all-start) | async-done | bytes 2359328 | tf_op jit(solution)/shard_map/all_to_all | solution.py:547
  97.9 8.6 %attend_merge_project.1 = (bf16[256,1024]{1,0:T(8,128)(2,1)}, bf16[256,512]{1,0:T(8,128)(2,1)}, bf16[256,512]{1,0:T(8,128)(2,1)}, bf16[256,512]{1,0:T(8,128)(2,1)}, bf16[256,512]{1,0:T(8,128)(2,1)}) custom-call(s32[2]{0:T(128)} %pad_add_fusion.1.place, s32[40,128]{1,0:T(8,128)} %bitcast.49, bf16[2048,128]{1,0:T(8,128)(2,1)} %bitcast.42, ...), custom_call_target="tpu_custom_call" | custom-call | tf_op jit(solution)/shard_map/attend_merge_project/pallas_call | solution.py:437
  106.5 2.4 %collective-permute-start.6 = (bf16[256,512]{1,0:T(8,128)(2,1)}, bf16[256,512]{1,0:T(8,128)(2,1)S(1)}, u32[]{:S(2)}, u32[]{:S(2)}) collective-permute-start(bf16[256,512]{1,0:T(8,128)(2,1)} %get-tuple-element.28), channel_id=1, source_target_pairs={{0,4},{2,6},{4,0},{6,2},{1,5},{3,7},{5,1},{7,3},{8,12},{10,14},{12... | collective-permute-start | bytes 786440 | tf_op jit(solution)/shard_map/ppermute | solution.py:477
  108.9 2.0 %collective-permute-start.8 = (bf16[256,512]{1,0:T(8,128)(2,1)}, bf16[256,512]{1,0:T(8,128)(2,1)S(1)}, u32[]{:S(2)}, u32[]{:S(2)}) collective-permute-start(bf16[256,512]{1,0:T(8,128)(2,1)} %get-tuple-element.30), channel_id=1, source_target_pairs={{0,6},{2,0},{4,2},{6,4},{1,7},{3,1},{5,3},{7,5},{8,14},{10,8},{12,... | collective-permute-start | bytes 786440 | tf_op jit(solution)/shard_map/ppermute | solution.py:477
  110.9 4.9 %project_mine.1 = (bf16[256,512]{1,0:T(8,128)(2,1)}, bf16[256,512]{1,0:T(8,128)(2,1)}, bf16[256,512]{1,0:T(8,128)(2,1)}, bf16[256,512]{1,0:T(8,128)(2,1)}) custom-call(s32[2]{0:T(128)} %pad_add_fusion.1.place, bf16[256,1024]{1,0:T(8,128)(2,1)} %get-tuple-element.22.heads, bf16[1024,4096]{1,0:T(8,128)(2,1)} %weight.3), custom_call_target="tpu_custom_call" | custom-call | flops 1000000000 | bytes 6000000 | tf_op jit(solution)/shard_map/project_mine/pallas_call | solution.py:461
  115.8 1.5 %collective-permute-start.3 = (bf16[256,512]{1,0:T(8,128)(2,1)}, bf16[256,512]{1,0:T(8,128)(2,1)S(1)}, u32[]{:S(2)}, u32[]{:S(2)}) collective-permute-start(bf16[256,512]{1,0:T(8,128)(2,1)} %get-tuple-element.24), channel_id=1, source_target_pairs={{0,4},{2,6},{4,0},{6,2},{1,5},{3,7},{5,1},{7,3},{8,12},{10,14},{12... | collective-permute-start | bytes 786440 | tf_op jit(solution)/shard_map/ppermute | solution.py:477
  117.3 2.6 %collective-permute-start.4 = (bf16[256,512]{1,0:T(8,128)(2,1)}, bf16[256,512]{1,0:T(8,128)(2,1)S(1)}, u32[]{:S(2)}, u32[]{:S(2)}) collective-permute-start(bf16[256,512]{1,0:T(8,128)(2,1)} %get-tuple-element.25), channel_id=1, source_target_pairs={{0,2},{2,4},{4,6},{6,0},{1,3},{3,5},{5,7},{7,1},{8,10},{10,12},{12... | collective-permute-start | bytes 786440 | tf_op jit(solution)/shard_map/ppermute | solution.py:477
  119.9 3.3 %collective-permute-done.7 = bf16[256,512]{1,0:T(8,128)(2,1)S(1)} collective-permute-done((bf16[256,512]{1,0:T(8,128)(2,1)}, bf16[256,512]{1,0:T(8,128)(2,1)S(1)}, u32[]{:S(2)}, u32[]{:S(2)}) %collective-permute-start.7) | collective-permute-done | bytes 262176 | tf_op jit(solution)/shard_map/ppermute | solution.py:477
  123.4 5.8 %collective-permute-start.9 = (bf16[256,512]{1,0:T(8,128)(2,1)S(1)}, bf16[256,512]{1,0:T(8,128)(2,1)S(1)}, u32[]{:S(2)}, u32[]{:S(2)}) collective-permute-start(bf16[256,512]{1,0:T(8,128)(2,1)S(1)} %add_convert_fusion.1), channel_id=1, source_target_pairs={{0,1},{1,0},{2,3},{3,2},{4,5},{5,4},{6,7},{7,6},{8,9},{9,8},{10,11... | collective-permute-start | bytes 786440 | tf_op jit(solution)/shard_map/ppermute | solution.py:570
  129.1 4.5 %collective-permute-done.4 = bf16[256,512]{1,0:T(8,128)(2,1)S(1)} collective-permute-done((bf16[256,512]{1,0:T(8,128)(2,1)}, bf16[256,512]{1,0:T(8,128)(2,1)S(1)}, u32[]{:S(2)}, u32[]{:S(2)}) %collective-permute-start.4) | collective-permute-done | bytes 262176 | tf_op jit(solution)/shard_map/ppermute | solution.py:477
  133.6 7.3 %collective-permute-done.9 = bf16[256,512]{1,0:T(8,128)(2,1)S(1)} collective-permute-done((bf16[256,512]{1,0:T(8,128)(2,1)S(1)}, bf16[256,512]{1,0:T(8,128)(2,1)S(1)}, u32[]{:S(2)}, u32[]{:S(2)}) %collective-permute-start.9) | collective-permute-done | bytes 262176 | tf_op jit(solution)/shard_map/ppermute | solution.py:570
  (88 shorter events, 11.6 us)
Async XLA Ops:
  3.8 5.9 %copy-start.4 = (s32[64,48]{0,1:T(8,128)S(1)}, s32[64,48]{0,1:T(8,128)}, u32[]{:S(2)}) copy-start(s32[64,48]{0,1:T(8,128)} %param.25) | copy-start | bytes 36868
  3.8 5.9 %copy-start.8 = (s32[64]{0:T(128)S(1)}, s32[64]{0:T(128)}, u32[]{:S(2)}) copy-start(s32[64]{0:T(128)} %param.26) | copy-start | bytes 772
  3.8 42.8 %all-to-all-start.1 = ((bf16[16,18,2,16,128]{4,3,2,1,0:T(8,128)(2,1)}), bf16[16,18,2,16,128]{4,3,2,1,0:T(8,128)(2,1)}, u32[]{:S(2)}, u32[]{:S(2)}) async-start(bf16[16,18,2,16,128]{4,3,2,1,0:T(8,128)(2,1)} %bitcast.36), calls=%async_computation.1 | async-start | bytes 4718592 | tf_op jit(solution)/shard_map/all_to_all | solution.py:547
  9.6 5.1 %copy-start.5 = (bf16[4,64,1,128]{3,1,2,0:T(8,128)(2,1)S(1)}, bf16[4,64,1,128]{3,1,2,0:T(8,128)(2,1)}, u32[]{:S(2)}) copy-start(bf16[4,64,1,128]{3,1,2,0:T(8,128)(2,1)} %param.16) | copy-start | bytes 196612
  9.6 5.1 %copy-start.6 = (bf16[4,64,1,128]{3,1,2,0:T(8,128)(2,1)S(1)}, bf16[4,64,1,128]{3,1,2,0:T(8,128)(2,1)}, u32[]{:S(2)}) copy-start(bf16[4,64,1,128]{3,1,2,0:T(8,128)(2,1)} %param.15) | copy-start | bytes 196612
  22.3 6.1 %copy-start = (bf16[4,64,8,128]{3,2,1,0:T(8,128)(2,1)S(1)}, bf16[4,64,8,128]{3,2,1,0:T(8,128)(2,1)}, u32[]{:S(2)}) copy-start(bf16[4,64,8,128]{3,2,1,0:T(8,128)(2,1)} %param.14) | copy-start | bytes 1572868
  29.3 28.7 %collective-permute-start = (bf16[2128,128]{1,0:T(8,128)(2,1)}, bf16[2128,128]{1,0:T(8,128)(2,1)S(1)}, u32[]{:S(2)}, u32[]{:S(2)}) collective-permute-start(bf16[2128,128]{1,0:T(8,128)(2,1)} %gate.1), channel_id=1, source_target_pairs={{0,32},{32,0},{1,33},{33,1},{2,34},{34,2},{3,35},{35,3},{4,36},{36... | collective-permute-start | bytes 1634312 | tf_op jit(solution)/shard_map/ppermute | solution.py:561
  46.6 50.5 %all-to-all-start = ((bf16[16,18,2,16,128]{4,3,2,1,0:T(8,128)(2,1)}), bf16[16,18,2,16,128]{4,3,2,1,0:T(8,128)(2,1)}, u32[]{:S(2)}, u32[]{:S(2)}) async-start(bf16[16,18,2,16,128]{4,3,2,1,0:T(8,128)(2,1)} %bitcast.10), calls=%async_computation | async-start | bytes 4718592 | tf_op jit(solution)/shard_map/all_to_all | solution.py:547
  58.0 0.8 copy-start.9
  63.7 33.4 %collective-permute-start.1 = (bf16[2048,128]{1,0:T(8,128)(2,1)}, bf16[2048,128]{1,0:T(8,128)(2,1)S(1)}, u32[]{:S(2)}, u32[]{:S(2)}) collective-permute-start(bf16[2048,128]{1,0:T(8,128)(2,1)} %get-tuple-element.20), channel_id=1, source_target_pairs={{0,32},{32,0},{1,33},{33,1},{2,34},{34,2},{3,35},{35,3},{4,36},{36... | collective-permute-start | bytes 1572872 | tf_op jit(solution)/shard_map/ppermute | solution.py:565
  63.9 33.2 %collective-permute-start.2 = (f32[16,128]{1,0:T(8,128)}, f32[16,128]{1,0:T(8,128)S(1)}, u32[]{:S(2)}, u32[]{:S(2)}) collective-permute-start(f32[16,128]{1,0:T(8,128)} %get-tuple-element.21), channel_id=1, source_target_pairs={{0,32},{32,0},{1,33},{33,1},{2,34},{34,2},{3,35},{35,3},{4,36},{36... | collective-permute-start | bytes 24584 | tf_op jit(solution)/shard_map/ppermute | solution.py:566
  97.0 0.6 copy-start.7
  97.1 0.8 copy-start.1
  106.5 13.4 %collective-permute-start.6 = (bf16[256,512]{1,0:T(8,128)(2,1)}, bf16[256,512]{1,0:T(8,128)(2,1)S(1)}, u32[]{:S(2)}, u32[]{:S(2)}) collective-permute-start(bf16[256,512]{1,0:T(8,128)(2,1)} %get-tuple-element.28), channel_id=1, source_target_pairs={{0,4},{2,6},{4,0},{6,2},{1,5},{3,7},{5,1},{7,3},{8,12},{10,14},{12... | collective-permute-start | bytes 786440 | tf_op jit(solution)/shard_map/ppermute | solution.py:477
  108.9 14.4 %collective-permute-start.7 = (bf16[256,512]{1,0:T(8,128)(2,1)}, bf16[256,512]{1,0:T(8,128)(2,1)S(1)}, u32[]{:S(2)}, u32[]{:S(2)}) collective-permute-start(bf16[256,512]{1,0:T(8,128)(2,1)} %get-tuple-element.29), channel_id=1, source_target_pairs={{0,2},{2,4},{4,6},{6,0},{1,3},{3,5},{5,7},{7,1},{8,10},{10,12},{12... | collective-permute-start | bytes 786440 | tf_op jit(solution)/shard_map/ppermute | solution.py:477
  108.9 14.4 %collective-permute-start.8 = (bf16[256,512]{1,0:T(8,128)(2,1)}, bf16[256,512]{1,0:T(8,128)(2,1)S(1)}, u32[]{:S(2)}, u32[]{:S(2)}) collective-permute-start(bf16[256,512]{1,0:T(8,128)(2,1)} %get-tuple-element.30), channel_id=1, source_target_pairs={{0,6},{2,0},{4,2},{6,4},{1,7},{3,1},{5,3},{7,5},{8,14},{10,8},{12,... | collective-permute-start | bytes 786440 | tf_op jit(solution)/shard_map/ppermute | solution.py:477
  110.9 12.3 %copy-start.2 = (bf16[256,512]{1,0:T(8,128)(2,1)S(1)}, bf16[256,512]{1,0:T(8,128)(2,1)}, u32[]{:S(2)}) copy-start(bf16[256,512]{1,0:T(8,128)(2,1)} %get-tuple-element.27) | copy-start | bytes 786436
  115.8 25.2 %copy-start.3 = (bf16[256,512]{1,0:T(8,128)(2,1)S(1)}, bf16[256,512]{1,0:T(8,128)(2,1)}, u32[]{:S(2)}) copy-start(bf16[256,512]{1,0:T(8,128)(2,1)} %get-tuple-element.23) | copy-start | bytes 786436
  115.8 13.4 %collective-permute-start.3 = (bf16[256,512]{1,0:T(8,128)(2,1)}, bf16[256,512]{1,0:T(8,128)(2,1)S(1)}, u32[]{:S(2)}, u32[]{:S(2)}) collective-permute-start(bf16[256,512]{1,0:T(8,128)(2,1)} %get-tuple-element.24), channel_id=1, source_target_pairs={{0,4},{2,6},{4,0},{6,2},{1,5},{3,7},{5,1},{7,3},{8,12},{10,14},{12... | collective-permute-start | bytes 786440 | tf_op jit(solution)/shard_map/ppermute | solution.py:477
  117.3 16.4 %collective-permute-start.4 = (bf16[256,512]{1,0:T(8,128)(2,1)}, bf16[256,512]{1,0:T(8,128)(2,1)S(1)}, u32[]{:S(2)}, u32[]{:S(2)}) collective-permute-start(bf16[256,512]{1,0:T(8,128)(2,1)} %get-tuple-element.25), channel_id=1, source_target_pairs={{0,2},{2,4},{4,6},{6,0},{1,3},{3,5},{5,7},{7,1},{8,10},{10,12},{12... | collective-permute-start | bytes 786440 | tf_op jit(solution)/shard_map/ppermute | solution.py:477
  119.9 13.7 %collective-permute-start.5 = (bf16[256,512]{1,0:T(8,128)(2,1)}, bf16[256,512]{1,0:T(8,128)(2,1)S(1)}, u32[]{:S(2)}, u32[]{:S(2)}) collective-permute-start(bf16[256,512]{1,0:T(8,128)(2,1)} %get-tuple-element.26), channel_id=1, source_target_pairs={{0,6},{2,0},{4,2},{6,4},{1,7},{3,1},{5,3},{7,5},{8,14},{10,8},{12,... | collective-permute-start | bytes 786440 | tf_op jit(solution)/shard_map/ppermute | solution.py:477
  123.4 17.6 %collective-permute-start.9 = (bf16[256,512]{1,0:T(8,128)(2,1)S(1)}, bf16[256,512]{1,0:T(8,128)(2,1)S(1)}, u32[]{:S(2)}, u32[]{:S(2)}) collective-permute-start(bf16[256,512]{1,0:T(8,128)(2,1)S(1)} %add_convert_fusion.1), channel_id=1, source_target_pairs={{0,1},{1,0},{2,3},{3,2},{4,5},{5,4},{6,7},{7,6},{8,9},{9,8},{10,11... | collective-permute-start | bytes 786440 | tf_op jit(solution)/shard_map/ppermute | solution.py:570
